TPU v7x, 32 devices: a whole 2x2x4 slice. The times are simulated.
32 devices in a mesh: wide: 8 (over z, x), narrow: 4 (over y, core).
Axes of the slice: x: 2, y: 2, z: 4, core: 2. Of those that a mesh axis runs over, the one named last changes fastest.
Arguments:
- amps: bfloat16 [64, 128, 128], P(('wide', 'narrow')), may hold values from -4 to 4
- resp: bfloat16 [64, 128, 128], P(('wide', 'narrow')), may hold values from -4 to 4
- trans: bfloat16 [64, 512, 128], P(('wide', 'narrow')), may hold values from -0.375 to 0.375
- ints: bfloat16 [64, 128, 128], P(('wide', 'narrow')), may hold values from -6 to 6
- energies: float32 [64, 128], P(('wide', 'narrow')), may hold values from 0.5 to 4
- couple: float32 [64, 12], P(('wide', 'narrow')), may hold values from -1 to 1
- readers: int32 [64, 12], P(('wide', 'narrow')), may hold values from 0 to 15, as said below
- domains: int32 [64, 4], replicated, may hold values from 0 to 7, as said below
- integrals: bfloat16 [1024, 512], P(None, 'narrow'), may hold values from -0.01171875 to 0.01171875
Outputs:
- new_amps: float32 [64, 128, 128], P(('wide', 'narrow'))
- new_resp: float32 [64, 128, 128], P(('wide', 'narrow'))
- response: float32 [1024, 512], P('wide', 'narrow')
Inputs may be any that keep to these rules, and one draw needn't show every extreme that they name: `readers`: each row lists 12 different positions among the 16 pairs of the same narrow index. `domains`: each row lists 4 different function blocks.
All inputs are finite; a program needn't handle non-finite values.
Results may differ from a plain program's by a relative error of at most 0.015.
Values may be sent and summed in bfloat16 or wider, within the bound.
No kernel may reach another device: no remote copies, remote signals or barrier semaphores. Data moves between devices by JAX's collectives and lax.ppermute only.
A program may use at most 64 MiB of HBM per device.

v0:
```python
import jax
import jax.numpy as jnp
from jax import lax
from jax.sharding import PartitionSpec as P

NPNO = 128
BLK = 128
NFB = 8


def reader_terms(own_q, own_dom, their_q, their_dom, their_amps):
    blocks = own_q.shape[0]
    reader_count = their_q.shape[0]
    matches = (own_dom[None, :, None] == their_dom[:, None, :]).astype(jnp.bfloat16)
    split_q = their_q.reshape(reader_count, blocks, BLK, NPNO)
    shifted = jnp.einsum(
        "sab,sbfp->safp", matches, split_q, preferred_element_type=jnp.float32
    ).astype(jnp.bfloat16)
    intersection = jnp.einsum(
        "afp,safq->spq", own_q, shifted, preferred_element_type=jnp.float32
    ).astype(jnp.bfloat16)
    halfway = jnp.einsum(
        "spq,sqc->spc", intersection, their_amps, preferred_element_type=jnp.float32
    ).astype(jnp.bfloat16)
    halfway = halfway.reshape(reader_count, NPNO, 2, NPNO)
    return jnp.einsum("spkc,sqc->skpq", halfway, intersection, preferred_element_type=jnp.float32)


def per_device(amps, resp, trans, ints, energies, couple, readers, domains, integrals):
    wide_size = lax.axis_size("wide")
    narrow_size = lax.axis_size("narrow")
    wide_pos = lax.axis_index("wide")
    narrow_pos = lax.axis_index("narrow")
    pairs_here = amps.shape[0]
    dom_blk = trans.shape[1] // BLK
    grid = domains.reshape(wide_size, narrow_size, pairs_here, dom_blk)
    dom_row = lax.dynamic_index_in_dim(grid, narrow_pos, axis=1, keepdims=False).reshape(
        wide_size * pairs_here, dom_blk
    )
    own_dom = lax.dynamic_slice_in_dim(
        domains, (wide_pos * narrow_size + narrow_pos) * pairs_here, pairs_here, 0
    )
    own_q = trans.reshape(pairs_here, dom_blk, BLK, NPNO)
    pair_amps = jnp.concatenate([amps, resp], axis=2)
    gathered_q, gathered_amps = (
        lax.all_gather(trans, "wide", axis=0, tiled=True),
        lax.all_gather(pair_amps, "wide", axis=0, tiled=True),
    )
    collected = []
    for member in range(pairs_here):
        picks = readers[member]
        contrib = reader_terms(
            own_q[member], own_dom[member], gathered_q[picks], dom_row[picks], gathered_amps[picks]
        )
        collected.append(jnp.einsum("s,skpq->kpq", couple[member], contrib))
    coupled = jnp.stack(collected)
    amps_f = amps.astype(jnp.float32)
    resp_f = resp.astype(jnp.float32)
    denominator = energies[:, :, None] + energies[:, None, :]
    new_amps = (
        amps_f
        - 0.5 * (ints.astype(jnp.float32) + denominator * amps_f + coupled[:, 0]) / denominator
    )
    new_resp = resp_f - 0.5 * (amps_f + denominator * resp_f + coupled[:, 1]) / denominator
    amps_b = new_amps.astype(jnp.bfloat16)
    resp_b = new_resp.astype(jnp.bfloat16)
    weights = 0.5 * (
        jnp.einsum("gpc,gqc->gpq", amps_b, resp_b, preferred_element_type=jnp.float32)
        + jnp.einsum("gpc,gqc->gpq", resp_b, amps_b, preferred_element_type=jnp.float32)
    )
    weights = weights.astype(jnp.bfloat16)
    place = (jnp.arange(NFB, dtype=jnp.int32)[None, :, None] == own_dom[:, None, :]).astype(
        jnp.bfloat16
    )
    full_q = jnp.einsum("gnd,gdfp->gnfp", place, own_q, preferred_element_type=jnp.float32)
    full_q = full_q.astype(jnp.bfloat16).reshape(pairs_here, NFB * BLK, NPNO)
    left = jnp.einsum("gmp,gpq->gmq", full_q, weights, preferred_element_type=jnp.float32).astype(
        jnp.bfloat16
    )
    share = lax.psum_scatter(
        jnp.einsum("gmq,gnq->mn", left, full_q, preferred_element_type=jnp.float32),
        "wide",
        scatter_dimension=0,
        tiled=True,
    )
    panel = lax.psum(share, "narrow")
    response = jnp.dot(panel, integrals.astype(jnp.float32), precision=lax.Precision.HIGHEST)
    return (new_amps, new_resp, response)


def solution(mesh):
    in_specs = (
        P(("wide", "narrow"), None, None),
        P(("wide", "narrow"), None, None),
        P(("wide", "narrow"), None, None),
        P(("wide", "narrow"), None, None),
        P(("wide", "narrow"), None),
        P(("wide", "narrow"), None),
        P(("wide", "narrow"), None),
        P(),
        P(None, "narrow"),
    )
    out_specs = (
        P(("wide", "narrow"), None, None),
        P(("wide", "narrow"), None, None),
        P("wide", "narrow"),
    )
    return jax.shard_map(
        per_device, mesh=mesh, in_specs=in_specs, out_specs=out_specs, check_vma=False
    )
```

profile of v0, /device:TPU:0, one launch (start us, length us, event | category | flops | bytes accessed | tf_op | source)
XLA Modules:
  0.0 256.9 jit_solution(17380734375711505053)
XLA Ops:
  7.2 1.6 pad_maximum_fusion.1
  8.9 0.7 all-gather.3.cloned.1.call-update
  9.7 0.8 copy.23
  10.5 0.8 fusion.53
  12.3 0.8 constant_dynamic-slice_fusion.1
  13.2 1.4 convolution_convert_fusion.5
  14.9 38.7 %all-gather.5.cloned.1.call-done = bf16[16,128,256]{2,1,0:T(8,128)(2,1)} async-done(((bf16[2,128,256]{2,1,0:T(8,128)(2,1)}), bf16[16,128,256]{2,1,0:T(8,128)(2,1)}) %all-gather.5.cloned.1.call-update) | async-done | bytes 1048592 | tf_op jit(solution)/shard_map/all_gather | solution.py:47
  53.6 1.9 gather_fusion.2
  55.5 1.5 gather_fusion.5
  57.0 46.8 %all-gather.3.cloned.1.call-done = bf16[16,512,128]{2,1,0:T(8,128)(2,1)} async-done(((bf16[2,512,128]{2,1,0:T(8,128)(2,1)}), bf16[16,512,128]{2,1,0:T(8,128)(2,1)}) %all-gather.3.cloned.1.call-update) | async-done | bytes 2097168 | tf_op jit(solution)/shard_map/all_gather | solution.py:46
  103.8 2.4 gather_fusion.1
  106.3 1.4 convolution_convert_fusion.1
  107.6 0.6 fusion.17
  108.7 1.3 convolution_bitcast_fusion.2
  110.0 2.6 %copy.41 = bf16[12,2,128,128]{3,0,2,1:T(8,128)(2,1)} copy(bf16[12,2,128,128]{2,3,1,0:T(8,128)(2,1)} %convolution_bitcast_fusion.2) | data formatting | bytes 1572864 | tf_op jit(solution)/shard_map/spkc,sqc->skpq/transpose | solution.py:26
  112.6 2.0 gather_fusion.4
  114.6 2.8 %convolution_convert_fusion = bf16[12,4,128,128]{3,1,2,0:T(4,128)(2,1)S(1)} fusion(bf16[12,4,128,128]{3,2,1,0:T(8,128)(2,1)} %bitcast.122, s32[12,4]{1,0:T(8,128)S(1)} %gather_fusion.3, s32[4]{0:T(128)S(1)} %get-tuple-element.4), kind=kOutput, calls=%fused_computation.7 | convolution fusion | flops 7078080 | bytes 3145936 | tf_op jit(solution)/shard_map/sab,sbfp->safp/dot_general | solution.py:16
  117.4 0.6 fusion.14
  118.9 1.3 convolution_bitcast_fusion.1
  120.2 1.9 copy.48
  123.6 2.8 %convolution_bitcast_fusion = f32[1024,1024]{1,0:T(8,128)} fusion(bf16[2,1024,128]{2,1,0:T(8,128)(2,1)S(1)} %bitcast.118, bf16[2,128,128]{2,1,0:T(8,128)(2,1)S(1)} %fusion.21), kind=kOutput, calls=%fused_computation.6 | convolution fusion | flops 604241920 | bytes 4784128 | tf_op jit(solution)/shard_map/gmq,gnq->mn/dot_general | solution.py:81
  126.5 86.5 %reduce-scatter.2.cloned.1.call-done = f32[128,1024]{1,0:T(8,128)} async-done(((f32[1024,1024]{1,0:T(8,128)}), f32[128,1024]{1,0:T(8,128)}) %reduce-scatter.2.cloned.1.call-update) | async-done | bytes 524304 | tf_op jit(solution)/shard_map/reduce_scatter | solution.py:80
  213.0 35.3 %all-reduce.2.cloned.1.call-done = f32[128,1024]{1,0:T(8,128)} async-done(((f32[128,1024]{1,0:T(8,128)}), f32[128,1024]{1,0:T(8,128)}) %all-reduce.2.cloned.1.call-update) | async-done | bytes 524304 | tf_op jit(solution)/shard_map/psum | solution.py:86
  248.3 2.0 fusion.62
  (48 shorter events, 4.5 us)
Async XLA Ops:
  7.2 241.1 %copy-start = (bf16[1024,128]{1,0:T(8,128)(2,1)S(1)}, bf16[1024,128]{1,0:T(8,128)(2,1)}, u32[]{:S(2)}) copy-start(bf16[1024,128]{1,0:T(8,128)(2,1)} %param.17) | copy-start | bytes 786436
  7.2 7.7 %copy-start.5 = (bf16[2,512,128]{2,1,0:T(8,128)(2,1)S(1)}, bf16[2,512,128]{2,1,0:T(8,128)(2,1)}, u32[]{:S(2)}) copy-start(bf16[2,512,128]{2,1,0:T(8,128)(2,1)} %param.11) | copy-start | bytes 786436
  7.2 46.4 %all-gather.5.cloned.1.call-start = ((), (), s32[]{:S(2)}) async-start(), calls=%async_computation.2 | async-start | bytes 1179648 | tf_op jit(solution)/shard_map/all_gather | solution.py:47
  8.9 94.9 %all-gather.3.cloned.1.call-start = ((), (), s32[]{:S(2)}) async-start(), calls=%async_computation.1 | async-start | bytes 2359296 | tf_op jit(solution)/shard_map/all_gather | solution.py:46
  9.6 203.3 %reduce-scatter.2.cloned.1.call-start = ((), (), s32[]{:S(2)}) async-start(), calls=%async_computation.3 | async-start | bytes 4718592 | tf_op jit(solution)/shard_map/reduce_scatter | solution.py:80
  53.6 1.9 copy-start.4
  108.7 3.9 %copy-start.1 = (bf16[16,512,128]{2,1,0:T(8,128)(2,1)S(1)}, bf16[16,512,128]{2,1,0:T(8,128)(2,1)}, u32[]{:S(2)}) copy-start(bf16[16,512,128]{2,1,0:T(8,128)(2,1)} %all-gather.3.cloned.1.call-done) | copy-start | bytes 6291460
  117.4 1.1 copy-start.3
  118.9 3.2 %copy-start.2 = (bf16[12,2,128,128]{3,0,2,1:T(8,128)(2,1)S(1)}, bf16[12,2,128,128]{3,0,2,1:T(8,128)(2,1)}, u32[]{:S(2)}) copy-start(bf16[12,2,128,128]{3,0,2,1:T(8,128)(2,1)} %copy.41) | copy-start | bytes 2359300
  118.9 3.2 %copy-start.12 = (f32[2,12]{1,0:T(2,128)S(1)}, f32[2,12]{1,0:T(2,128)}, u32[]{:S(2)}) copy-start(f32[2,12]{1,0:T(2,128)} %param.14) | copy-start | bytes 292
  122.2 0.8 copy-start.8
  122.2 0.9 copy-start.9
  122.2 0.9 copy-start.10
  122.2 0.9 copy-start.11
  123.2 3.2 %copy-start.6 = (f32[2,128,128]{2,1,0:T(8,128)}, f32[2,128,128]{2,1,0:T(8,128)S(1)}, u32[]{:S(2)}) copy-start(f32[2,128,128]{2,1,0:T(8,128)S(1)} %get-tuple-element.5) | copy-start | bytes 393220
  123.2 3.2 %copy-start.7 = (f32[2,128,128]{2,1,0:T(8,128)}, f32[2,128,128]{2,1,0:T(8,128)S(1)}, u32[]{:S(2)}) copy-start(f32[2,128,128]{2,1,0:T(8,128)S(1)} %get-tuple-element.6) | copy-start | bytes 393220
  126.4 121.9 %all-reduce.2.cloned.1.call-start = ((), (), s32[]{:S(2)}) async-start(), calls=%async_computation.4 | async-start | bytes 1048576 | tf_op jit(solution)/shard_map/psum | solution.py:86
Sparse Core Ops, SparseCore 0:
  10.7 42.8 all-gather.4
  55.7 48.0 all-gather.2
  126.5 86.3 reduce-scatter.1
  215.3 32.9 all-reduce.1
where the time goes:
time: 257 us
  waiting for transfers between devices  208 us (81%)
  local copies, waits for them, and re-layouts  16.2 us (6%)
  matrix products  16 us (6%)
  between operations  14 us (5%)
    reduce_scatter x1, waiting for transfers between devices, per_device(): lax.psum_scatter(jnp.einsum('gmq,gnq->mn', left, full_q, preferred_elemen...  86.5 us
    all_gather x1, waiting for transfers between devices, per_device(): lax.all_gather(trans, 'wide', axis=0, tiled=True)  46.8 us
    all_gather x1, waiting for transfers between devices, per_device(): lax.all_gather(pair_amps, 'wide', axis=0, tiled=True)  38.7 us
    psum x1, waiting for transfers between devices, per_device(): panel = lax.psum(share, 'narrow')  35.3 us
  transfers between devices with their start and end apart: 4, of which 4 were waited for; matrix products, arithmetic and copies ran while one was open for 3% of the time, Pallas kernels for 0%

commit v1 on v0

v1 whole, which is shorter than its diff:
```python
import functools

import jax
import jax.numpy as jnp
from jax import lax
from jax.experimental import pallas as pl
from jax.experimental.pallas import tpu as pltpu
from jax.sharding import PartitionSpec as P

BF16 = jnp.bfloat16
F32 = jnp.float32
SMEM = pl.BlockSpec(memory_space=pltpu.SMEM)
VMEM = pl.BlockSpec(memory_space=pltpu.VMEM)


def swap(value, axis, mask):
    size = lax.axis_size(axis)
    return lax.ppermute(value, axis, [(i, i ^ mask) for i in range(size)])


def call(kernel, out_shape, specs, *args):
    return pl.pallas_call(
        kernel,
        out_shape=out_shape,
        in_specs=specs,
        out_specs=jax.tree.map(lambda _: VMEM, out_shape),
        compiler_params=pltpu.CompilerParams(vmem_limit_bytes=32 * 1024 * 1024),
    )(*args)


def amps_kernel(amps_ref, resp_ref, out_ref):
    npno = amps_ref.shape[1]
    for p in range(amps_ref.shape[0]):
        out_ref[p, :, :npno] = amps_ref[p]
        out_ref[p, :, npno:] = resp_ref[p]


def spread_kernel(blk, narrow, mask, where_ref, dom_ref, own_ref, far_ref, out_ref):
    pairs, _, npno = own_ref.shape
    dom_blk = own_ref.shape[1] // blk
    out_ref[...] = jnp.zeros_like(out_ref)
    for side, q_ref in enumerate((own_ref, far_ref)):
        dev = where_ref[0] ^ (mask * side)
        for p in range(pairs):
            pair = (dev * narrow + where_ref[1]) * pairs + p
            for a in range(dom_blk):
                rows = pl.ds((side * pairs + p) * npno, npno)
                out_ref[dom_ref[pair * dom_blk + a], rows, :] = q_ref[p, a * blk : (a + 1) * blk, :].T


def couple_kernel(masks, blk, narrow, last, *refs):
    count = len(masks)
    where_ref, dom_ref, own_c_ref, far_c_ref, spread_ref = refs[:5]
    q_refs, tz_refs = refs[5 : 5 + count], refs[5 + count : 5 + 2 * count]
    rest = refs[5 + 2 * count :]
    pairs, _, npno = q_refs[0].shape
    dom_blk = q_refs[0].shape[1] // blk
    sums = [None] * (2 * pairs)
    if last:
        sums = [rest[0][g] for g in range(2 * pairs)]
    for k, mask in enumerate(masks):
        dev = where_ref[0] ^ mask
        overlap, half = [], []
        for p in range(pairs):
            pair = (dev * narrow + where_ref[1]) * pairs + p
            left = jnp.concatenate([spread_ref[dom_ref[pair * dom_blk + b]] for b in range(dom_blk)], axis=1)
            s = jnp.dot(left, q_refs[k][p], preferred_element_type=F32).astype(BF16)
            h = jnp.dot(s, tz_refs[k][p], preferred_element_type=F32)
            scaled = []
            for g in range(2 * pairs):
                c_ref = own_c_ref if g < pairs else far_c_ref
                c = c_ref[g % pairs, dev * pairs + p]
                scaled.append((h[g * npno : (g + 1) * npno] * c).astype(BF16))
            overlap.append(s)
            half.append(scaled)
        for g in range(2 * pairs):
            rows = slice(g * npno, (g + 1) * npno)
            right = jnp.concatenate([s[rows] for s in overlap], axis=1)
            left = jnp.concatenate(
                [jnp.concatenate([h[g][:, i * npno : (i + 1) * npno] for h in half], axis=1) for i in range(2)], axis=0
            )
            term = lax.dot_general(left, right, (((1,), (1,)), ((), ())), preferred_element_type=F32)
            sums[g] = term if sums[g] is None else sums[g] + term
    if last:
        own_ref, far_ref = rest[1:]
        for g in range(pairs):
            own_ref[g] = sums[g]
            far_ref[g] = sums[pairs + g].astype(BF16)
    else:
        for g in range(2 * pairs):
            rest[0][g] = sums[g]


def update_kernel(own_ref, back_ref, amps_ref, resp_ref, ints_ref, energy_ref, new_amps_ref, new_resp_ref, w_ref):
    npno = amps_ref.shape[1]
    for p in range(amps_ref.shape[0]):
        across = jnp.broadcast_to(energy_ref[pl.ds(p, 1), :], (npno, npno))
        denom = across + across.T
        amps = amps_ref[p].astype(F32)
        resp = resp_ref[p].astype(F32)
        coupled_t = own_ref[p, :npno] + back_ref[p, :npno].astype(F32)
        coupled_z = own_ref[p, npno:] + back_ref[p, npno:].astype(F32)
        new_amps = amps - 0.5 * (ints_ref[p].astype(F32) + denom * amps + coupled_t) / denom
        new_resp = resp - 0.5 * (amps + denom * resp + coupled_z) / denom
        new_amps_ref[p] = new_amps
        new_resp_ref[p] = new_resp
        prod = lax.dot_general(
            new_amps.astype(BF16), new_resp.astype(BF16), (((1,), (1,)), ((), ())), preferred_element_type=F32
        )
        w_ref[p] = (0.5 * (prod + prod.T)).astype(BF16)


def place_kernel(blk, narrow, *refs):
    where_ref, dom_ref, ints_ref = refs[:3]
    q_refs, (full_ref, moved_ref) = refs[3 : 3 + narrow], refs[3 + narrow :]
    pairs, _, npno = q_refs[0].shape
    dom_blk = q_refs[0].shape[1] // blk
    full_ref[...] = jnp.zeros_like(full_ref)
    for k in range(narrow):
        for p in range(pairs):
            pair = (where_ref[0] * narrow + (where_ref[1] ^ k)) * pairs + p
            slot = k * pairs + p
            blocks = []
            for a in range(dom_blk):
                f = dom_ref[pair * dom_blk + a]
                full_ref[f, :, slot * npno : (slot + 1) * npno] = q_refs[k][p, a * blk : (a + 1) * blk, :]
                blocks.append(ints_ref[f])
            moved_ref[slot] = lax.dot_general(
                q_refs[k][p], jnp.concatenate(blocks, axis=0), (((0,), (0,)), ((), ())), preferred_element_type=F32
            ).astype(BF16)


def response_kernel(*refs):
    full_ref, moved_ref = refs[:2]
    w_refs, out_ref = refs[2:-1], refs[-1]
    pairs = w_refs[0].shape[0]
    parts = []
    for k, w_ref in enumerate(w_refs):
        for p in range(pairs):
            parts.append(jnp.dot(w_ref[p], moved_ref[k * pairs + p], preferred_element_type=F32).astype(BF16))
    right = jnp.concatenate(parts, axis=0)
    blocks, blk, depth = full_ref.shape
    rows = jnp.dot(full_ref[...].reshape(blocks * blk, depth), right, preferred_element_type=F32).astype(BF16)
    out_ref[...] = rows.reshape(out_ref.shape)


def per_device(amps, resp, trans, ints, energies, couple, readers, domains, integrals):
    wide, narrow = lax.axis_size("wide"), lax.axis_size("narrow")
    pairs, nfun, npno = trans.shape
    blk = nfun // domains.shape[1]
    nbas, cols = integrals.shape
    near = wide // 2
    partner = wide - 2
    sds = jax.ShapeDtypeStruct

    where = jnp.stack([lax.axis_index("wide"), lax.axis_index("narrow")]).astype(jnp.int32)
    dom = domains.reshape(-1)
    position = jnp.arange(wide * pairs, dtype=jnp.int32)
    own_c = jnp.sum(jnp.where(readers[:, :, None] == position, couple[:, :, None], 0.0), axis=1)

    amps_resp = call(amps_kernel, sds((pairs, npno, 2 * npno), BF16), [VMEM, VMEM], amps, resp)
    near_q, near_tz = {0: trans}, {0: amps_resp}
    near_q[1] = swap(trans, "wide", 1)
    for mask in range(2, near, 2):
        near_q[mask] = swap(trans, "wide", mask)
    near_tz[1] = swap(amps_resp, "wide", 1)
    for mask in range(2, near, 2):
        near_tz[mask] = swap(amps_resp, "wide", mask)
    far_q = swap(trans, "wide", partner)
    far_c = swap(own_c, "wide", partner)
    for mask in range(2, near, 2):
        near_q[mask + 1] = swap(near_q[mask], "wide", 1)
        near_tz[mask + 1] = swap(near_tz[mask], "wide", 1)
    narrow_q = {0: trans}
    for mask in range(1, narrow):
        narrow_q[mask] = swap(narrow_q[mask - 1], "narrow", 1) if mask % 2 else swap(trans, "narrow", mask)

    spread = call(
        functools.partial(spread_kernel, blk, narrow, partner),
        sds((nbas // blk, 2 * pairs * npno, blk), BF16),
        [SMEM, SMEM, VMEM, VMEM],
        where, dom, trans, far_q,
    )
    full, moved = call(
        functools.partial(place_kernel, blk, narrow),
        (sds((nbas // blk, blk, narrow * pairs * npno), BF16), sds((narrow * pairs, npno, cols), BF16)),
        [SMEM, SMEM] + [VMEM] * (1 + narrow),
        where, dom, integrals.reshape(nbas // blk, blk, cols), *[narrow_q[k] for k in range(narrow)],
    )
    early = [0, 1] + list(range(2, near, 2))
    late = list(range(3, near, 2))
    sums = call(
        functools.partial(couple_kernel, early, blk, narrow, False),
        sds((2 * pairs, 2 * npno, npno), F32),
        [SMEM] * 4 + [VMEM] * (1 + 2 * len(early)),
        where, dom, own_c, far_c, spread, *[near_q[m] for m in early], *[near_tz[m] for m in early],
    )
    own, far = call(
        functools.partial(couple_kernel, late, blk, narrow, True),
        (sds((pairs, 2 * npno, npno), F32), sds((pairs, 2 * npno, npno), BF16)),
        [SMEM] * 4 + [VMEM] * (2 + 2 * len(late)),
        where, dom, own_c, far_c, spread, *[near_q[m] for m in late], *[near_tz[m] for m in late], sums,
    )
    back = swap(far, "wide", partner)
    mats = sds((pairs, npno, npno), F32)
    new_amps, new_resp, weights = call(
        update_kernel,
        (mats, mats, sds((pairs, npno, npno), BF16)),
        [VMEM] * 6,
        own, back, amps, resp, ints, energies,
    )
    narrow_w = {0: weights}
    for mask in range(1, narrow):
        narrow_w[mask] = swap(narrow_w[mask - 1], "narrow", 1) if mask % 2 else swap(weights, "narrow", mask)
    partial = call(
        response_kernel,
        sds((wide, nbas // wide, cols), BF16),
        [VMEM] * (2 + narrow),
        full, moved, *[narrow_w[k] for k in range(narrow)],
    )
    shares = lax.all_to_all(partial, "wide", 0, 0, tiled=True)
    response = jnp.sum(shares.astype(F32), axis=0)
    return (new_amps, new_resp, response)


def solution(mesh):
    in_specs = (
        P(("wide", "narrow"), None, None),
        P(("wide", "narrow"), None, None),
        P(("wide", "narrow"), None, None),
        P(("wide", "narrow"), None, None),
        P(("wide", "narrow"), None),
        P(("wide", "narrow"), None),
        P(("wide", "narrow"), None),
        P(),
        P(None, "narrow"),
    )
    out_specs = (
        P(("wide", "narrow"), None, None),
        P(("wide", "narrow"), None, None),
        P("wide", "narrow"),
    )
    return jax.shard_map(
        per_device, mesh=mesh, in_specs=in_specs, out_specs=out_specs, check_vma=False
    )
```

time: 257 us -> 66.9 us (0.26)
  waiting for transfers between devices: 208 us -> 9.96 us
  starting transfers between devices: 0.16 us -> 26.4 us
  matrix products: 16 us -> 0 us
  blocking collectives: 0 us -> 14.2 us
  between operations: 14 us -> 0.79 us
  local copies, waits for them, and re-layouts: 16.2 us -> 4.12 us
  Pallas kernels: 0 us -> 10.2 us
    reduce_scatter x1 -> x0, waiting for transfers between devices: 86.5 us -> none  [per_device(): lax.psum_scatter(jnp.einsum('gmq,gnq->mn', left, full_q, preferred_elemen...]
    all_gather x2 -> x0, waiting for transfers between devices: 85.4 us -> none  [the longest x1 46.8 us: per_device(): lax.all_gather(trans, 'wide', axis=0, tiled=True)]
    psum x1 -> x0, waiting for transfers between devices: 35.3 us -> none  [per_device(): panel = lax.psum(share, 'narrow')]
    ppermute x0 -> x15, starting transfers between devices: none -> 26.4 us  [swap(): return lax.ppermute(value, axis, [(i, i ^ mask) for i in range(size)])]
    dot_general x15 -> x0, matrix products: 16 us -> none  [the longest x2 4.14 us: reader_terms(): jnp.einsum('sab,sbfp->safp', matches, split_q, preferred_element_type=jnp...]
    all_to_all x0 -> x1, blocking collectives: none -> 14.2 us  [per_device(): shares = lax.all_to_all(partial, 'wide', 0, 0, tiled=True)]
    pallas_call x0 -> x7, Pallas kernels: none -> 10.2 us  [call(): pl.pallas_call(kernel, out_shape=out_shape, in_specs=specs, out_specs=jax...]
    ppermute x0 -> x15, waiting for transfers between devices: none -> 9.96 us  [swap(): return lax.ppermute(value, axis, [(i, i ^ mask) for i in range(size)])]
  transfers between devices with their start and end apart: 4 -> 15, of which waited for: 4 -> 4; matrix products, arithmetic and copies ran while one was open for 3% -> 4% of each run, Pallas kernels for 0% -> 14%
where the time goes in v1:
time: 66.9 us; the launch traced here: 66.5 us
  starting transfers between devices  26.4 us (39%)
  blocking collectives  14.2 us (21%)
  Pallas kernels  10.2 us (15%)
  waiting for transfers between devices  9.96 us (15%)
  local copies, waits for them, and re-layouts  4.12 us (6%)
  other arithmetic  0.84 us (1%)
  between operations  0.79 us (1%)
    ppermute x15, starting transfers between devices, swap(): return lax.ppermute(value, axis, [(i, i ^ mask) for i in range(size)])  26.4 us
    all_to_all x1, blocking collectives, per_device(): shares = lax.all_to_all(partial, 'wide', 0, 0, tiled=True)  14.2 us
    pallas_call x7, Pallas kernels, call(): pl.pallas_call(kernel, out_shape=out_shape, in_specs=specs, out_specs=jax...  10.2 us
    ppermute x15, waiting for transfers between devices, swap(): return lax.ppermute(value, axis, [(i, i ^ mask) for i in range(size)])  9.96 us
    unnamed x17, local copies, waits for them, and re-layouts  4.01 us
  transfers between devices with their start and end apart: 15, of which 4 were waited for; matrix products, arithmetic and copies ran while one was open for 4% of the time, Pallas kernels for 14%

profile of v1, /device:TPU:0, one launch (start us, length us, event | category | flops | bytes accessed | tf_op | source)
XLA Modules:
  0.0 66.5 jit_solution(13948931225972261898)
XLA Ops:
  0.6 3.1 %collective-permute-start.2 = (bf16[2,512,128]{2,1,0:T(8,128)(2,1)}, bf16[2,512,128]{2,1,0:T(8,128)(2,1)S(1)}, u32[]{:S(2)}, u32[]{:S(2)}) collective-permute-start(bf16[2,512,128]{2,1,0:T(8,128)(2,1)} %refs_3_.1), channel_id=1, source_target_pairs={{0,8},{4,12},{8,0},{12,4},{16,24},{20,28},{24,16},{28,20},{1,9},{5... | collective-permute-start | bytes 786440 | tf_op jit(solution)/shard_map/ppermute | solution.py:18
  3.7 2.5 %collective-permute-start.1 = (bf16[2,512,128]{2,1,0:T(8,128)(2,1)}, bf16[2,512,128]{2,1,0:T(8,128)(2,1)S(1)}, u32[]{:S(2)}, u32[]{:S(2)}) collective-permute-start(bf16[2,512,128]{2,1,0:T(8,128)(2,1)} %refs_3_.1), channel_id=1, source_target_pairs={{0,24},{4,28},{8,16},{12,20},{16,8},{20,12},{24,0},{28,4},{1,25},{... | collective-permute-start | bytes 786440 | tf_op jit(solution)/shard_map/ppermute | solution.py:18
  6.2 1.5 %collective-permute-start.6 = (bf16[2,512,128]{2,1,0:T(8,128)(2,1)}, bf16[2,512,128]{2,1,0:T(8,128)(2,1)S(1)}, u32[]{:S(2)}, u32[]{:S(2)}) collective-permute-start(bf16[2,512,128]{2,1,0:T(8,128)(2,1)} %refs_3_.1), channel_id=1, source_target_pairs={{0,4},{4,0},{8,12},{12,8},{16,20},{20,16},{24,28},{28,24},{1,5},{5... | collective-permute-start | bytes 786440 | tf_op jit(solution)/shard_map/ppermute | solution.py:18
  7.7 0.8 %copy-done = bf16[2,128,128]{2,1,0:T(8,128)(2,1)S(1)} copy-done((bf16[2,128,128]{2,1,0:T(8,128)(2,1)S(1)}, bf16[2,128,128]{2,1,0:T(8,128)(2,1)}, u32[]{:S(2)}) %copy-start) | copy-done | bytes 65560
  8.5 0.8 %copy-done.2 = bf16[2,128,128]{2,1,0:T(8,128)(2,1)S(1)} copy-done((bf16[2,128,128]{2,1,0:T(8,128)(2,1)S(1)}, bf16[2,128,128]{2,1,0:T(8,128)(2,1)}, u32[]{:S(2)}) %copy-start.2) | copy-done | bytes 65560
  9.4 0.7 %collective-permute-start.4 = (bf16[2,128,256]{2,1,0:T(8,128)(2,1)S(1)}, bf16[2,128,256]{2,1,0:T(8,128)(2,1)S(1)}, u32[]{:S(2)}, u32[]{:S(2)}) collective-permute-start(bf16[2,128,256]{2,1,0:T(8,128)(2,1)S(1)} %shard_map.113.refs_8_), channel_id=1, source_target_pairs={{0,8},{4,12},{8,0},{12,4},{16,24},{20,28},{24,16},{28,20},{1,9},{5... | collective-permute-start | bytes 393224 | tf_op jit(solution)/shard_map/ppermute | solution.py:18
  10.1 0.8 %copy.15 = f32[2,12]{0,1:T(8,128)S(1)} copy(f32[2,12]{1,0:T(2,128)} %param.14) | data formatting | bytes 192 | tf_op args[5]
  10.9 0.8 %copy.14 = s32[2,12]{0,1:T(8,128)S(1)} copy(s32[2,12]{1,0:T(2,128)} %param.15) | data formatting | bytes 192 | tf_op args[6]
  12.4 9.9 %collective-permute-start = (f32[2,16]{1,0:T(2,128)S(1)}, f32[2,16]{1,0:T(2,128)S(1)}, u32[]{:S(2)}, u32[]{:S(2)}) collective-permute-start(f32[2,16]{1,0:T(2,128)S(1)} %fusion.refs_2_), channel_id=1, source_target_pairs={{0,24},{4,28},{8,16},{12,20},{16,8},{20,12},{24,0},{28,4},{1,25},{... | collective-permute-start | bytes 392 | tf_op jit(solution)/shard_map/ppermute | solution.py:18
  22.3 1.5 %collective-permute-done.refs_3_ = f32[2,16]{1,0:T(2,128)S(1)} collective-permute-done((f32[2,16]{1,0:T(2,128)S(1)}, f32[2,16]{1,0:T(2,128)S(1)}, u32[]{:S(2)}, u32[]{:S(2)}) %collective-permute-start) | collective-permute-done | bytes 160 | tf_op jit(solution)/shard_map/ppermute | solution.py:18
  23.8 1.5 %collective-permute-start.10 = (bf16[2,512,128]{2,1,0:T(8,128)(2,1)}, bf16[2,512,128]{2,1,0:T(8,128)(2,1)S(1)}, u32[]{:S(2)}, u32[]{:S(2)}) collective-permute-start(bf16[2,512,128]{2,1,0:T(8,128)(2,1)} %refs_3_.1), channel_id=1, source_target_pairs={{0,2},{1,3},{2,0},{3,1},{4,6},{5,7},{6,4},{7,5},{8,10},{9,11},{10,... | collective-permute-start | bytes 786440 | tf_op jit(solution)/shard_map/ppermute | solution.py:18
  25.9 1.5 %collective-permute-start.5 = (bf16[2,128,256]{2,1,0:T(8,128)(2,1)S(1)}, bf16[2,128,256]{2,1,0:T(8,128)(2,1)S(1)}, u32[]{:S(2)}, u32[]{:S(2)}) collective-permute-start(bf16[2,128,256]{2,1,0:T(8,128)(2,1)S(1)} %collective-permute-done.4.refs_10_), channel_id=1, source_target_pairs={{0,4},{4,0},{8,12},{12,8},{16,20},{20,16},{24,28},{28,24},{1,5},{5... | collective-permute-start | bytes 393224 | tf_op jit(solution)/shard_map/ppermute | solution.py:18
  27.4 0.8 %copy.13 = s32[64,4]{1,0:T(8,128)S(1)} copy(s32[64,4]{0,1:T(4,128)} %param.16) | data formatting | bytes 2048 | tf_op args[7]
  28.3 1.2 %shard_map.112.refs_4_ = bf16[8,512,128]{2,1,0:T(8,128)(2,1)S(1)} custom-call(s32[2]{0:T(128)S(1)} %pad_add_fusion.where_ref.refs_0_, s32[256]{0:T(256)S(1)} %reshape.14.dom_ref.refs_1_, bf16[2,512,128]{2,1,0:T(8,128)(2,1)} %refs_3_.1, bf16[2,512,128]{2,1,0:T(8,128)(2,1)S(1)} %collective-permute-done.1.far_ref), custom_call_target="tpu_custom_call" | custom-call | tf_op jit(solution)/shard_map/pallas_call | solution.py:22
  29.6 0.7 %collective-permute-done.7.refs_9_ = bf16[2,128,256]{2,1,0:T(8,128)(2,1)S(1)} collective-permute-done((bf16[2,128,256]{2,1,0:T(8,128)(2,1)S(1)}, bf16[2,128,256]{2,1,0:T(8,128)(2,1)S(1)}, u32[]{:S(2)}, u32[]{:S(2)}) %collective-permute-start.7) | collective-permute-done | bytes 131104 | tf_op jit(solution)/shard_map/ppermute | solution.py:18
  30.3 3.8 %shard_map.114.refs_7_ = f32[4,256,128]{2,1,0:T(8,128)S(1)} custom-call(s32[2]{0:T(128)S(1)} %pad_add_fusion.where_ref.refs_0_, s32[256]{0:T(256)S(1)} %reshape.14.dom_ref.refs_1_, f32[2,16]{1,0:T(2,128)S(1)} %fusion.refs_2_, f32[2,16]{1,0:T(2,128)S(1)} %collective-permute-done.refs_3_, bf16[8,512,128]{2,1,0:T(8,128)(2,1)S(1)} %shard_map.112.refs_4_, ...), custom_call_target="tpu_custom_call" | custom-call | tf_op jit(solution)/shard_map/pallas_call | solution.py:22
  34.1 1.7 %shard_map.115 = (f32[2,256,128]{2,1,0:T(8,128)S(1)}, bf16[2,256,128]{2,1,0:T(8,128)(2,1)S(1)}) custom-call(s32[2]{0:T(128)S(1)} %pad_add_fusion.where_ref.refs_0_, s32[256]{0:T(256)S(1)} %reshape.14.dom_ref.refs_1_, f32[2,16]{1,0:T(2,128)S(1)} %fusion.refs_2_, f32[2,16]{1,0:T(2,128)S(1)} %collective-permute-done.refs_3_, ...), custom_call_target="tpu_custom_call" | custom-call | tf_op jit(solution)/shard_map/pallas_call | solution.py:22
  35.8 3.9 %collective-permute-start.8 = (bf16[2,256,128]{2,1,0:T(8,128)(2,1)S(1)}, bf16[2,256,128]{2,1,0:T(8,128)(2,1)S(1)}, u32[]{:S(2)}, u32[]{:S(2)}) collective-permute-start(bf16[2,256,128]{2,1,0:T(8,128)(2,1)S(1)} %get-tuple-element.11), channel_id=1, source_target_pairs={{0,24},{4,28},{8,16},{12,20},{16,8},{20,12},{24,0},{28,4},{1,25},{... | collective-permute-start | bytes 393224 | tf_op jit(solution)/shard_map/ppermute | solution.py:18
  39.9 3.9 %collective-permute-done.8.back_ref = bf16[2,256,128]{2,1,0:T(8,128)(2,1)S(1)} collective-permute-done((bf16[2,256,128]{2,1,0:T(8,128)(2,1)S(1)}, bf16[2,256,128]{2,1,0:T(8,128)(2,1)S(1)}, u32[]{:S(2)}, u32[]{:S(2)}) %collective-permute-start.8) | collective-permute-done | bytes 131104 | tf_op jit(solution)/shard_map/ppermute | solution.py:18
  43.9 0.9 %shard_map.116 = (f32[2,128,128]{2,1,0:T(8,128)}, f32[2,128,128]{2,1,0:T(8,128)}, bf16[2,128,128]{2,1,0:T(8,128)(2,1)S(1)}) custom-call(f32[2,256,128]{2,1,0:T(8,128)S(1)} %get-tuple-element.10.own_ref, bf16[2,256,128]{2,1,0:T(8,128)(2,1)S(1)} %collective-permute-done.8.back_ref, bf16[2,128,128]{2,1,0:T(8,128)(2,1)S(1)} %copy-done.1, ...), custom_call_target="tpu_custom_call" | custom-call | tf_op jit(solution)/shard_map/pallas_call | solution.py:22
  45.2 3.8 %collective-permute-done.13.refs_4_ = bf16[2,128,128]{2,1,0:T(8,128)(2,1)S(1)} collective-permute-done((bf16[2,128,128]{2,1,0:T(8,128)(2,1)S(1)}, bf16[2,128,128]{2,1,0:T(8,128)(2,1)S(1)}, u32[]{:S(2)}, u32[]{:S(2)}) %collective-permute-start.13) | collective-permute-done | bytes 65568 | tf_op jit(solution)/shard_map/ppermute | solution.py:18
  49.0 1.7 %shard_map.117 = (bf16[8,128,1024]{2,1,0:T(8,128)(2,1)S(1)}, bf16[8,128,128]{2,1,0:T(8,128)(2,1)S(1)}) custom-call(s32[2]{0:T(128)S(1)} %pad_add_fusion.where_ref.refs_0_, s32[256]{0:T(256)S(1)} %reshape.14.dom_ref.refs_1_, bf16[8,128,128]{2,1,0:T(8,128)(2,1)S(1)} %bitcast.3, bf16[2,512,128]{2,1,0:T(8,128)(2,1)} %refs_3_.1, ...), custom_call_target="tpu_custom_call" | custom-call | tf_op jit(solution)/shard_map/pallas_call | solution.py:22
  50.7 0.9 %shard_map.118 = bf16[8,128,128]{2,1,0:T(8,128)(2,1)S(1)} custom-call(bf16[8,128,1024]{2,1,0:T(8,128)(2,1)S(1)} %get-tuple-element.14.refs_0_, bf16[8,128,128]{2,1,0:T(8,128)(2,1)S(1)} %get-tuple-element.15.refs_1_, bf16[2,128,128]{2,1,0:T(8,128)(2,1)S(1)} %get-tuple-element.16.refs_2_, bf16[2,128,128]{2,1,0:T(8,128)(2,1)S(1)} %collective-permute-done.12.refs_3_, ...), custom_call_target="tpu_custom_call" | custom-call | tf_op jit(solution)/shard_map/pallas_call | solution.py:22
  51.6 14.2 %all_to_all.5 = bf16[8,128,128]{2,1,0:T(8,128)(2,1)S(1)} all-to-all(bf16[8,128,128]{2,1,0:T(8,128)(2,1)S(1)} %shard_map.118), channel_id=1, replica_groups=mesh['wide'=8,'narrow'=4] {'wide'}, dimensions={0} | all-to-all | bytes 524288 | tf_op jit(solution)/shard_map/all_to_all | solution.py:221
  (35 shorter events, 2.9 us)
Async XLA Ops:
  0.6 11.1 %collective-permute-start.2 = (bf16[2,512,128]{2,1,0:T(8,128)(2,1)}, bf16[2,512,128]{2,1,0:T(8,128)(2,1)S(1)}, u32[]{:S(2)}, u32[]{:S(2)}) collective-permute-start(bf16[2,512,128]{2,1,0:T(8,128)(2,1)} %refs_3_.1), channel_id=1, source_target_pairs={{0,8},{4,12},{8,0},{12,4},{16,24},{20,28},{24,16},{28,20},{1,9},{5... | collective-permute-start | bytes 786440 | tf_op jit(solution)/shard_map/ppermute | solution.py:18
  3.7 22.1 %collective-permute-start.1 = (bf16[2,512,128]{2,1,0:T(8,128)(2,1)}, bf16[2,512,128]{2,1,0:T(8,128)(2,1)S(1)}, u32[]{:S(2)}, u32[]{:S(2)}) collective-permute-start(bf16[2,512,128]{2,1,0:T(8,128)(2,1)} %refs_3_.1), channel_id=1, source_target_pairs={{0,24},{4,28},{8,16},{12,20},{16,8},{20,12},{24,0},{28,4},{1,25},{... | collective-permute-start | bytes 786440 | tf_op jit(solution)/shard_map/ppermute | solution.py:18
  6.2 24.1 %collective-permute-start.6 = (bf16[2,512,128]{2,1,0:T(8,128)(2,1)}, bf16[2,512,128]{2,1,0:T(8,128)(2,1)S(1)}, u32[]{:S(2)}, u32[]{:S(2)}) collective-permute-start(bf16[2,512,128]{2,1,0:T(8,128)(2,1)} %refs_3_.1), channel_id=1, source_target_pairs={{0,4},{4,0},{8,12},{12,8},{16,20},{20,16},{24,28},{28,24},{1,5},{5... | collective-permute-start | bytes 786440 | tf_op jit(solution)/shard_map/ppermute | solution.py:18
  7.7 0.8 %copy-start = (bf16[2,128,128]{2,1,0:T(8,128)(2,1)S(1)}, bf16[2,128,128]{2,1,0:T(8,128)(2,1)}, u32[]{:S(2)}) copy-start(bf16[2,128,128]{2,1,0:T(8,128)(2,1)} %amps_ref.3) | copy-start | bytes 196612
  8.5 0.8 %copy-start.2 = (bf16[2,128,128]{2,1,0:T(8,128)(2,1)S(1)}, bf16[2,128,128]{2,1,0:T(8,128)(2,1)}, u32[]{:S(2)}) copy-start(bf16[2,128,128]{2,1,0:T(8,128)(2,1)} %resp_ref.3) | copy-start | bytes 196612
  9.4 15.9 %collective-permute-start.4 = (bf16[2,128,256]{2,1,0:T(8,128)(2,1)S(1)}, bf16[2,128,256]{2,1,0:T(8,128)(2,1)S(1)}, u32[]{:S(2)}, u32[]{:S(2)}) collective-permute-start(bf16[2,128,256]{2,1,0:T(8,128)(2,1)S(1)} %shard_map.113.refs_8_), channel_id=1, source_target_pairs={{0,8},{4,12},{8,0},{12,4},{16,24},{20,28},{24,16},{28,20},{1,9},{5... | collective-permute-start | bytes 393224 | tf_op jit(solution)/shard_map/ppermute | solution.py:18
  11.8 22.3 %collective-permute-start.3 = (bf16[2,512,128]{2,1,0:T(8,128)(2,1)S(1)}, bf16[2,512,128]{2,1,0:T(8,128)(2,1)S(1)}, u32[]{:S(2)}, u32[]{:S(2)}) collective-permute-start(bf16[2,512,128]{2,1,0:T(8,128)(2,1)S(1)} %collective-permute-done.2.refs_7_), channel_id=1, source_target_pairs={{0,4},{4,0},{8,12},{12,8},{16,20},{20,16},{24,28},{28,24},{1,5},{5... | collective-permute-start | bytes 786440 | tf_op jit(solution)/shard_map/ppermute | solution.py:18
  12.4 11.4 %collective-permute-start = (f32[2,16]{1,0:T(2,128)S(1)}, f32[2,16]{1,0:T(2,128)S(1)}, u32[]{:S(2)}, u32[]{:S(2)}) collective-permute-start(f32[2,16]{1,0:T(2,128)S(1)} %fusion.refs_2_), channel_id=1, source_target_pairs={{0,24},{4,28},{8,16},{12,20},{16,8},{20,12},{24,0},{28,4},{1,25},{... | collective-permute-start | bytes 392 | tf_op jit(solution)/shard_map/ppermute | solution.py:18
  23.8 15.9 %collective-permute-start.10 = (bf16[2,512,128]{2,1,0:T(8,128)(2,1)}, bf16[2,512,128]{2,1,0:T(8,128)(2,1)S(1)}, u32[]{:S(2)}, u32[]{:S(2)}) collective-permute-start(bf16[2,512,128]{2,1,0:T(8,128)(2,1)} %refs_3_.1), channel_id=1, source_target_pairs={{0,2},{1,3},{2,0},{3,1},{4,6},{5,7},{6,4},{7,5},{8,10},{9,11},{10,... | collective-permute-start | bytes 786440 | tf_op jit(solution)/shard_map/ppermute | solution.py:18
  25.3 5.0 %collective-permute-start.7 = (bf16[2,128,256]{2,1,0:T(8,128)(2,1)S(1)}, bf16[2,128,256]{2,1,0:T(8,128)(2,1)S(1)}, u32[]{:S(2)}, u32[]{:S(2)}) collective-permute-start(bf16[2,128,256]{2,1,0:T(8,128)(2,1)S(1)} %shard_map.113.refs_8_), channel_id=1, source_target_pairs={{0,4},{4,0},{8,12},{12,8},{16,20},{20,16},{24,28},{28,24},{1,5},{5... | collective-permute-start | bytes 393224 | tf_op jit(solution)/shard_map/ppermute | solution.py:18
  25.9 8.2 %collective-permute-start.5 = (bf16[2,128,256]{2,1,0:T(8,128)(2,1)S(1)}, bf16[2,128,256]{2,1,0:T(8,128)(2,1)S(1)}, u32[]{:S(2)}, u32[]{:S(2)}) collective-permute-start(bf16[2,128,256]{2,1,0:T(8,128)(2,1)S(1)} %collective-permute-done.4.refs_10_), channel_id=1, source_target_pairs={{0,4},{4,0},{8,12},{12,8},{16,20},{20,16},{24,28},{28,24},{1,5},{5... | collective-permute-start | bytes 393224 | tf_op jit(solution)/shard_map/ppermute | solution.py:18
  29.5 14.3 %copy-start.1 = (bf16[2,128,128]{2,1,0:T(8,128)(2,1)S(1)}, bf16[2,128,128]{2,1,0:T(8,128)(2,1)}, u32[]{:S(2)}) copy-start(bf16[2,128,128]{2,1,0:T(8,128)(2,1)} %amps_ref.3) | copy-start | bytes 196612
  29.6 14.3 %copy-start.3 = (bf16[2,128,128]{2,1,0:T(8,128)(2,1)S(1)}, bf16[2,128,128]{2,1,0:T(8,128)(2,1)}, u32[]{:S(2)}) copy-start(bf16[2,128,128]{2,1,0:T(8,128)(2,1)} %resp_ref.3) | copy-start | bytes 196612
  29.6 14.3 %copy-start.5 = (bf16[2,128,128]{2,1,0:T(8,128)(2,1)S(1)}, bf16[2,128,128]{2,1,0:T(8,128)(2,1)}, u32[]{:S(2)}) copy-start(bf16[2,128,128]{2,1,0:T(8,128)(2,1)} %ints_ref.1) | copy-start | bytes 196612
  29.6 14.3 %copy-start.6 = (f32[2,128]{1,0:T(2,128)S(1)}, f32[2,128]{1,0:T(2,128)}, u32[]{:S(2)}) copy-start(f32[2,128]{1,0:T(2,128)} %energy_ref.1) | copy-start | bytes 3076
  29.6 19.4 %copy-start.4 = (bf16[1024,128]{1,0:T(8,128)(2,1)S(1)}, bf16[1024,128]{1,0:T(8,128)(2,1)}, u32[]{:S(2)}) copy-start(bf16[1024,128]{1,0:T(8,128)(2,1)} %param.17) | copy-start | bytes 786436
  30.3 18.7 %collective-permute-start.9 = (bf16[2,512,128]{2,1,0:T(8,128)(2,1)}, bf16[2,512,128]{2,1,0:T(8,128)(2,1)S(1)}, u32[]{:S(2)}, u32[]{:S(2)}) collective-permute-start(bf16[2,512,128]{2,1,0:T(8,128)(2,1)} %refs_3_.1), channel_id=1, source_target_pairs={{0,1},{1,0},{2,3},{3,2},{4,5},{5,4},{6,7},{7,6},{8,9},{9,8},{10,11... | collective-permute-start | bytes 786440 | tf_op jit(solution)/shard_map/ppermute | solution.py:18
  35.8 8.1 %collective-permute-start.8 = (bf16[2,256,128]{2,1,0:T(8,128)(2,1)S(1)}, bf16[2,256,128]{2,1,0:T(8,128)(2,1)S(1)}, u32[]{:S(2)}, u32[]{:S(2)}) collective-permute-start(bf16[2,256,128]{2,1,0:T(8,128)(2,1)S(1)} %get-tuple-element.11), channel_id=1, source_target_pairs={{0,24},{4,28},{8,16},{12,20},{16,8},{20,12},{24,0},{28,4},{1,25},{... | collective-permute-start | bytes 393224 | tf_op jit(solution)/shard_map/ppermute | solution.py:18
  39.7 9.3 %collective-permute-start.11 = (bf16[2,512,128]{2,1,0:T(8,128)(2,1)S(1)}, bf16[2,512,128]{2,1,0:T(8,128)(2,1)S(1)}, u32[]{:S(2)}, u32[]{:S(2)}) collective-permute-start(bf16[2,512,128]{2,1,0:T(8,128)(2,1)S(1)} %collective-permute-done.10.refs_5_), channel_id=1, source_target_pairs={{0,1},{1,0},{2,3},{3,2},{4,5},{5,4},{6,7},{7,6},{8,9},{9,8},{10,11... | collective-permute-start | bytes 786440 | tf_op jit(solution)/shard_map/ppermute | solution.py:18
  44.7 4.3 %collective-permute-start.13 = (bf16[2,128,128]{2,1,0:T(8,128)(2,1)S(1)}, bf16[2,128,128]{2,1,0:T(8,128)(2,1)S(1)}, u32[]{:S(2)}, u32[]{:S(2)}) collective-permute-start(bf16[2,128,128]{2,1,0:T(8,128)(2,1)S(1)} %get-tuple-element.16.refs_2_), channel_id=1, source_target_pairs={{0,2},{1,3},{2,0},{3,1},{4,6},{5,7},{6,4},{7,5},{8,10},{9,11},{10,... | collective-permute-start | bytes 196616 | tf_op jit(solution)/shard_map/ppermute | solution.py:18
  45.2 5.5 %collective-permute-start.12 = (bf16[2,128,128]{2,1,0:T(8,128)(2,1)S(1)}, bf16[2,128,128]{2,1,0:T(8,128)(2,1)S(1)}, u32[]{:S(2)}, u32[]{:S(2)}) collective-permute-start(bf16[2,128,128]{2,1,0:T(8,128)(2,1)S(1)} %get-tuple-element.16.refs_2_), channel_id=1, source_target_pairs={{0,1},{1,0},{2,3},{3,2},{4,5},{5,4},{6,7},{7,6},{8,9},{9,8},{10,11... | collective-permute-start | bytes 196616 | tf_op jit(solution)/shard_map/ppermute | solution.py:18
  49.0 1.8 %collective-permute-start.14 = (bf16[2,128,128]{2,1,0:T(8,128)(2,1)S(1)}, bf16[2,128,128]{2,1,0:T(8,128)(2,1)S(1)}, u32[]{:S(2)}, u32[]{:S(2)}) collective-permute-start(bf16[2,128,128]{2,1,0:T(8,128)(2,1)S(1)} %collective-permute-done.13.refs_4_), channel_id=1, source_target_pairs={{0,1},{1,0},{2,3},{3,2},{4,5},{5,4},{6,7},{7,6},{8,9},{9,8},{10,11... | collective-permute-start | bytes 196616 | tf_op jit(solution)/shard_map/ppermute | solution.py:18

commit v2 on v1

v2 whole, which is shorter than its diff:
```python
import functools

import jax
import jax.numpy as jnp
from jax import lax
from jax.experimental import pallas as pl
from jax.experimental.pallas import tpu as pltpu
from jax.sharding import PartitionSpec as P

BF16 = jnp.bfloat16
F32 = jnp.float32
SMEM = pl.BlockSpec(memory_space=pltpu.SMEM)
VMEM = pl.BlockSpec(memory_space=pltpu.VMEM)
ANY = pl.BlockSpec(memory_space=pl.ANY)


def swap(value, axis, mask):
    size = lax.axis_size(axis)
    return lax.ppermute(value, axis, [(i, i ^ mask) for i in range(size)])


def call(kernel, out_shape, specs, micros, *args, scratch=()):
    return pl.pallas_call(
        kernel,
        out_shape=out_shape,
        in_specs=specs,
        out_specs=jax.tree.map(lambda _: VMEM, out_shape),
        scratch_shapes=scratch,
        cost_estimate=pl.CostEstimate(flops=int(micros * 1e9), bytes_accessed=0, transcendentals=0),
        compiler_params=pltpu.CompilerParams(vmem_limit_bytes=32 * 1024 * 1024),
    )(*args)


def join_kernel(amps_ref, resp_ref, out_ref, sems):
    npno = amps_ref.shape[1]
    copies = []
    for i, ref in enumerate((amps_ref, resp_ref)):
        copy = pltpu.make_async_copy(ref, out_ref.at[:, :, pl.ds(i * npno, npno)], sems.at[i])
        copy.start()
        copies.append(copy)
    for copy in copies:
        copy.wait()


def pack_kernel(blk, readers_ref, couple_ref, q_ref, after_ref, out_ref):
    del after_ref
    pairs, nfun, npno = q_ref.shape
    count = (out_ref.shape[1] - nfun) // 2
    row = lax.broadcasted_iota(jnp.int32, (count, npno), 0)
    for p in range(pairs):
        for a in range(nfun // blk):
            rows = slice(a * blk, (a + 1) * blk)
            out_ref[p, rows, :] = q_ref[p, rows, :].T
        c = jnp.zeros((count, npno), F32)
        for r in range(readers_ref.shape[1]):
            c = c + jnp.where(row == readers_ref[p, r], couple_ref[p, r], 0.0)
        high = c.astype(BF16)
        out_ref[p, nfun : nfun + count, :] = high
        out_ref[p, nfun + count :, :] = (c - high.astype(F32)).astype(BF16)


def load_coefficients(pack_ref, c_ref):
    count = c_ref.shape[1]
    nfun = pack_ref.shape[1] - 2 * count
    for p in range(pack_ref.shape[0]):
        c_ref[p] = pack_ref[p, nfun : nfun + count, :].astype(F32) + pack_ref[p, nfun + count :, :].astype(F32)


def add_terms(sums, overlaps, tz_ref, c_ref, dev):
    pairs, npno, _ = tz_ref.shape
    half = []
    for p, s in enumerate(overlaps):
        h = jnp.dot(s, tz_ref[p], preferred_element_type=F32)
        scaled = []
        for g in range(pairs):
            c = c_ref[g, pl.ds(dev * pairs + p, 1), :]
            c = jnp.concatenate([c, c], axis=1)
            scaled.append((h[g * npno : (g + 1) * npno] * c).astype(BF16))
        half.append(scaled)
    for g in range(pairs):
        rows = slice(g * npno, (g + 1) * npno)
        right = jnp.concatenate([s[rows] for s in overlaps], axis=1)
        left = jnp.concatenate(
            [jnp.concatenate([h[g][:, i * npno : (i + 1) * npno] for h in half], axis=1) for i in range(2)], axis=0
        )
        term = lax.dot_general(left, right, (((1,), (1,)), ((), ())), preferred_element_type=F32)
        sums[g] = term if sums[g] is None else sums[g] + term


def couple_kernel(masks, ahead, blk, narrow, flip, prior, *refs):
    where_ref, dom_ref, pack_ref = refs[:3]
    refs = refs[3:]
    q_refs, refs = refs[: len(masks) + len(ahead)], refs[len(masks) + len(ahead) :]
    tz_refs, refs = refs[: len(masks)], refs[len(masks) :]
    prior_ref, refs = (refs[0], refs[1:]) if prior else (None, refs)
    out_ref, spread_ref, c_ref = refs[0], refs[-2], refs[-1]
    pairs, _, npno = q_refs[0].shape
    dom_blk = q_refs[0].shape[1] // blk
    load_coefficients(pack_ref, c_ref)
    spread_ref[...] = jnp.zeros_like(spread_ref)
    for p in range(pairs):
        pair = ((where_ref[0] ^ flip) * narrow + where_ref[1]) * pairs + p
        for a in range(dom_blk):
            spread_ref[dom_ref[pair * dom_blk + a], p * npno : (p + 1) * npno, :] = pack_ref[
                p, a * blk : (a + 1) * blk, :
            ]
    sums = [prior_ref[g] if prior else None for g in range(pairs)]
    for k, mask in enumerate(masks + ahead):
        dev = where_ref[0] ^ mask
        overlaps = []
        for p in range(pairs):
            pair = (dev * narrow + where_ref[1]) * pairs + p
            left = jnp.concatenate([spread_ref[dom_ref[pair * dom_blk + b]] for b in range(dom_blk)], axis=1)
            overlaps.append(jnp.dot(left, q_refs[k][p], preferred_element_type=F32).astype(BF16))
        if k < len(masks):
            add_terms(sums, overlaps, tz_refs[k], c_ref, dev)
        else:
            for p in range(pairs):
                refs[1][(k - len(masks)) * pairs + p] = overlaps[p]
    for g in range(pairs):
        out_ref[g] = sums[g].astype(out_ref.dtype)


def finish_kernel(masks, *refs):
    where_ref, pack_ref, overlap_ref, prior_ref = refs[:4]
    tz_refs, (out_ref, c_ref) = refs[4 : 4 + len(masks)], refs[4 + len(masks) :]
    pairs = pack_ref.shape[0]
    load_coefficients(pack_ref, c_ref)
    sums = [prior_ref[g] for g in range(pairs)]
    for k, mask in enumerate(masks):
        overlaps = [overlap_ref[k * pairs + p] for p in range(pairs)]
        add_terms(sums, overlaps, tz_refs[k], c_ref, where_ref[0] ^ mask)
    for g in range(pairs):
        out_ref[g] = sums[g].astype(out_ref.dtype)


def update_kernel(own_ref, back_ref, amps_ref, resp_ref, ints_ref, energy_ref, new_amps_ref, new_resp_ref, w_ref):
    npno = amps_ref.shape[1]
    for p in range(amps_ref.shape[0]):
        across = jnp.broadcast_to(energy_ref[pl.ds(p, 1), :], (npno, npno))
        denom = across + across.T
        amps = amps_ref[p].astype(F32)
        resp = resp_ref[p].astype(F32)
        coupled_t = own_ref[p, :npno] + back_ref[p, :npno].astype(F32)
        coupled_z = own_ref[p, npno:] + back_ref[p, npno:].astype(F32)
        new_amps = amps - 0.5 * (ints_ref[p].astype(F32) + denom * amps + coupled_t) / denom
        new_resp = resp - 0.5 * (amps + denom * resp + coupled_z) / denom
        new_amps_ref[p] = new_amps
        new_resp_ref[p] = new_resp
        prod = lax.dot_general(
            new_amps.astype(BF16), new_resp.astype(BF16), (((1,), (1,)), ((), ())), preferred_element_type=F32
        )
        w_ref[p] = (0.5 * (prod + prod.T)).astype(BF16)


def place_kernel(blk, narrow, *refs):
    where_ref, dom_ref, ints_ref = refs[:3]
    q_refs, (full_ref, moved_ref) = refs[3 : 3 + narrow], refs[3 + narrow :]
    pairs, _, npno = q_refs[0].shape
    dom_blk = q_refs[0].shape[1] // blk
    full_ref[...] = jnp.zeros_like(full_ref)
    for k in range(narrow):
        for p in range(pairs):
            pair = (where_ref[0] * narrow + (where_ref[1] ^ k)) * pairs + p
            slot = k * pairs + p
            blocks = []
            for a in range(dom_blk):
                f = dom_ref[pair * dom_blk + a]
                full_ref[f, :, slot * npno : (slot + 1) * npno] = q_refs[k][p, a * blk : (a + 1) * blk, :]
                blocks.append(ints_ref[f])
            moved_ref[slot] = lax.dot_general(
                q_refs[k][p], jnp.concatenate(blocks, axis=0), (((0,), (0,)), ((), ())), preferred_element_type=F32
            ).astype(BF16)


def response_kernel(*refs):
    full_ref, moved_ref = refs[:2]
    w_refs, out_ref = refs[2:-1], refs[-1]
    pairs = w_refs[0].shape[0]
    parts = []
    for k, w_ref in enumerate(w_refs):
        for p in range(pairs):
            parts.append(jnp.dot(w_ref[p], moved_ref[k * pairs + p], preferred_element_type=F32).astype(BF16))
    right = jnp.concatenate(parts, axis=0)
    blocks, blk, depth = full_ref.shape
    rows = jnp.dot(full_ref[...].reshape(blocks * blk, depth), right, preferred_element_type=F32).astype(BF16)
    out_ref[...] = rows.reshape(out_ref.shape)


def per_device(amps, resp, trans, ints, energies, couple, readers, domains, integrals):
    wide, narrow = lax.axis_size("wide"), lax.axis_size("narrow")
    pairs, nfun, npno = trans.shape
    blk = nfun // domains.shape[1]
    nbas, cols = integrals.shape
    near = wide // 2
    partner = wide - 2
    sds = jax.ShapeDtypeStruct

    count = wide * pairs
    where = jnp.stack([lax.axis_index("wide"), lax.axis_index("narrow")]).astype(jnp.int32)
    dom = domains.reshape(-1)

    near_q, near_tz = {0: trans}, {}
    near_q[1] = swap(trans, "wide", 1)
    for mask in range(2, near, 2):
        near_q[mask] = swap(trans, "wide", mask)
    near_tz[0] = call(
        join_kernel, sds((pairs, npno, 2 * npno), BF16), [ANY, ANY], 1, amps, resp, scratch=[pltpu.SemaphoreType.DMA((2,))]
    )
    near_tz[1] = swap(near_tz[0], "wide", 1)
    for mask in range(2, near, 2):
        near_tz[mask] = swap(near_tz[0], "wide", mask)
    pack = call(
        functools.partial(pack_kernel, blk),
        sds((pairs, nfun + 2 * count, npno), BF16),
        [SMEM, SMEM, VMEM, ANY], 1,
        readers, couple, trans, near_q[near - 2],
    )
    far_pack = swap(pack, "wide", partner)
    for mask in range(2, near, 2):
        near_q[mask + 1] = swap(near_q[mask], "wide", 1)
        near_tz[mask + 1] = swap(near_tz[mask], "wide", 1)
    narrow_q = {0: trans}
    for mask in range(1, narrow):
        narrow_q[mask] = swap(narrow_q[mask - 1], "narrow", 1) if mask % 2 else swap(trans, "narrow", mask)

    full, moved = call(
        functools.partial(place_kernel, blk, narrow),
        (sds((nbas // blk, blk, narrow * pairs * npno), BF16), sds((narrow * pairs, npno, cols), BF16)),
        [SMEM, SMEM] + [VMEM] * (1 + narrow), 2,
        where, dom, integrals.reshape(nbas // blk, blk, cols), *[narrow_q[k] for k in range(narrow)],
    )
    early = [0, 1] + list(range(2, near, 2))
    late = list(range(3, near, 2))
    scratch = [
        pltpu.VMEM((nbas // blk, pairs * npno, blk), BF16),
        pltpu.VMEM((pairs, count, npno), F32),
    ]
    sums = sds((pairs, 2 * npno, npno), F32)
    own = call(
        functools.partial(couple_kernel, early, [], blk, narrow, 0, False),
        sums,
        [SMEM] * 2 + [VMEM] * (1 + 2 * len(early)), 2,
        where, dom, pack, *[near_q[m] for m in early], *[near_tz[m] for m in early],
        scratch=scratch,
    )
    far, overlap = call(
        functools.partial(couple_kernel, early, late, blk, narrow, partner, False),
        (sums, sds((len(late) * pairs, pairs * npno, npno), BF16)),
        [SMEM] * 2 + [VMEM] * (1 + 2 * len(early) + len(late)), 3,
        where, dom, far_pack, *[near_q[m] for m in early + late], *[near_tz[m] for m in early],
        scratch=scratch,
    )
    far = call(
        functools.partial(finish_kernel, late),
        sds(sums.shape, BF16),
        [SMEM] + [VMEM] * (3 + len(late)), 1,
        where, far_pack, overlap, far, *[near_tz[m] for m in late],
        scratch=scratch[1:],
    )
    back = swap(far, "wide", partner)
    own = call(
        functools.partial(couple_kernel, late, [], blk, narrow, 0, True),
        sums,
        [SMEM] * 2 + [VMEM] * (2 + 2 * len(late)), 2,
        where, dom, pack, *[near_q[m] for m in late], *[near_tz[m] for m in late], own,
        scratch=scratch,
    )
    mats = sds((pairs, npno, npno), F32)
    new_amps, new_resp, weights = call(
        update_kernel,
        (mats, mats, sds((pairs, npno, npno), BF16)),
        [VMEM] * 6, 1,
        own, back, amps, resp, ints, energies,
    )
    narrow_w = {0: weights}
    for mask in range(1, narrow):
        narrow_w[mask] = swap(narrow_w[mask - 1], "narrow", 1) if mask % 2 else swap(weights, "narrow", mask)
    partial = call(
        response_kernel,
        sds((wide, nbas // wide, cols), BF16),
        [VMEM] * (2 + narrow), 1,
        full, moved, *[narrow_w[k] for k in range(narrow)],
    )
    shares = lax.all_to_all(partial, "wide", 0, 0, tiled=True)
    response = jnp.sum(shares.astype(F32), axis=0)
    return (new_amps, new_resp, response)


def solution(mesh):
    in_specs = (
        P(("wide", "narrow"), None, None),
        P(("wide", "narrow"), None, None),
        P(("wide", "narrow"), None, None),
        P(("wide", "narrow"), None, None),
        P(("wide", "narrow"), None),
        P(("wide", "narrow"), None),
        P(("wide", "narrow"), None),
        P(),
        P(None, "narrow"),
    )
    out_specs = (
        P(("wide", "narrow"), None, None),
        P(("wide", "narrow"), None, None),
        P("wide", "narrow"),
    )
    return jax.shard_map(
        per_device, mesh=mesh, in_specs=in_specs, out_specs=out_specs, check_vma=False
    )
```

time: 66.9 us -> 55.7 us (0.83)
  starting transfers between devices: 26.4 us -> 17.2 us
  local copies, waits for them, and re-layouts: 4.12 us -> 1.92 us
  waiting for transfers between devices: 9.96 us -> 11.2 us
    ppermute x15 -> x14, starting transfers between devices: 26.4 us -> 17.2 us  [swap(): return lax.ppermute(value, axis, [(i, i ^ mask) for i in range(size)])]
    unnamed x17 -> x23, local copies, waits for them, and re-layouts: 4.01 us -> 1.82 us
    ppermute x15 -> x14, waiting for transfers between devices: 9.96 us -> 11.2 us  [swap(): return lax.ppermute(value, axis, [(i, i ^ mask) for i in range(size)])]
    pallas_call x7 -> x9, Pallas kernels: 10.2 us -> 9.89 us  [call(): pl.pallas_call(kernel, out_shape=out_shape, in_specs=specs, out_specs=jax...]
  transfers between devices with their start and end apart: 15 -> 14, of which waited for: 4 -> 4; matrix products, arithmetic and copies ran while one was open for 4% -> 0% of each run, Pallas kernels for 14% -> 16%
where the time goes in v2:
time: 55.7 us; the launch traced here: 55.5 us
  starting transfers between devices  17.2 us (31%)
  blocking collectives  13.7 us (25%)
  waiting for transfers between devices  11.2 us (20%)
  Pallas kernels  9.89 us (18%)
  local copies, waits for them, and re-layouts  1.92 us (3%)
  between operations  0.82 us (1%)
  other arithmetic  0.74 us (1%)
    ppermute x14, starting transfers between devices, swap(): return lax.ppermute(value, axis, [(i, i ^ mask) for i in range(size)])  17.2 us
    all_to_all x1, blocking collectives, per_device(): shares = lax.all_to_all(partial, 'wide', 0, 0, tiled=True)  13.7 us
    ppermute x14, waiting for transfers between devices, swap(): return lax.ppermute(value, axis, [(i, i ^ mask) for i in range(size)])  11.2 us
    pallas_call x9, Pallas kernels, call(): pl.pallas_call(kernel, out_shape=out_shape, in_specs=specs, out_specs=jax...  9.89 us
    unnamed x23, local copies, waits for them, and re-layouts  1.82 us
  transfers between devices with their start and end apart: 14, of which 4 were waited for; matrix products, arithmetic and copies ran while one was open for 0% of the time, Pallas kernels for 16%

profile of v2, /device:TPU:0, one launch (start us, length us, event | category | flops | bytes accessed | tf_op | source)
XLA Modules:
  0.0 55.5 jit_solution(4975049330960090212)
XLA Ops:
  0.6 3.1 %collective-permute-start = (bf16[2,512,128]{2,1,0:T(8,128)(2,1)}, bf16[2,512,128]{2,1,0:T(8,128)(2,1)S(1)}, u32[]{:S(2)}, u32[]{:S(2)}) collective-permute-start(bf16[2,512,128]{2,1,0:T(8,128)(2,1)} %refs_3_.5), channel_id=1, source_target_pairs={{0,8},{4,12},{8,0},{12,4},{16,24},{20,28},{24,16},{28,20},{1,9},{5... | collective-permute-start | bytes 786440 | tf_op jit(solution)/shard_map/ppermute | solution.py:19
  3.7 1.5 %collective-permute-start.4 = (bf16[2,512,128]{2,1,0:T(8,128)(2,1)}, bf16[2,512,128]{2,1,0:T(8,128)(2,1)S(1)}, u32[]{:S(2)}, u32[]{:S(2)}) collective-permute-start(bf16[2,512,128]{2,1,0:T(8,128)(2,1)} %refs_3_.5), channel_id=1, source_target_pairs={{0,4},{4,0},{8,12},{12,8},{16,20},{20,16},{24,28},{28,24},{1,5},{5... | collective-permute-start | bytes 786440 | tf_op jit(solution)/shard_map/ppermute | solution.py:19
  5.2 1.5 %collective-permute-start.9 = (bf16[2,512,128]{2,1,0:T(8,128)(2,1)}, bf16[2,512,128]{2,1,0:T(8,128)(2,1)S(1)}, u32[]{:S(2)}, u32[]{:S(2)}) collective-permute-start(bf16[2,512,128]{2,1,0:T(8,128)(2,1)} %refs_3_.5), channel_id=1, source_target_pairs={{0,2},{1,3},{2,0},{3,1},{4,6},{5,7},{6,4},{7,5},{8,10},{9,11},{10,... | collective-permute-start | bytes 786440 | tf_op jit(solution)/shard_map/ppermute | solution.py:19
  6.7 0.8 %copy-done.2 = bf16[2,128,128]{2,1,0:T(8,128)(2,1)S(1)} copy-done((bf16[2,128,128]{2,1,0:T(8,128)(2,1)S(1)}, bf16[2,128,128]{2,1,0:T(8,128)(2,1)}, u32[]{:S(2)}) %copy-start.2) | copy-done | bytes 65560
  7.6 0.8 %copy-done.4 = bf16[2,128,128]{2,1,0:T(8,128)(2,1)S(1)} copy-done((bf16[2,128,128]{2,1,0:T(8,128)(2,1)S(1)}, bf16[2,128,128]{2,1,0:T(8,128)(2,1)}, u32[]{:S(2)}) %copy-start.4) | copy-done | bytes 65560
  9.7 1.0 %collective-permute-done.after_ref.refs_5_ = bf16[2,512,128]{2,1,0:T(8,128)(2,1)S(1)} collective-permute-done((bf16[2,512,128]{2,1,0:T(8,128)(2,1)}, bf16[2,512,128]{2,1,0:T(8,128)(2,1)S(1)}, u32[]{:S(2)}, u32[]{:S(2)}) %collective-permute-start) | collective-permute-done | bytes 262176 | tf_op jit(solution)/shard_map/ppermute | solution.py:19
  10.8 0.7 %shard_map.112.refs_2_ = bf16[2,544,128]{2,1,0:T(8,128)(2,1)S(1)} custom-call(s32[2,12]{1,0:T(2,128)S(1)} %copy-done.7, f32[2,12]{1,0:T(2,128)S(1)} %copy-done.8, bf16[2,512,128]{2,1,0:T(8,128)(2,1)S(1)} %copy-done, bf16[2,512,128]{2,1,0:T(8,128)(2,1)S(1)} %collective-permute-done.after_ref.refs_5_), custom_call_target="tpu_custom_call" | custom-call | flops 1000000000 | tf_op jit(solution)/shard_map/pallas_call | solution.py:23
  11.5 4.5 %collective-permute-start.6 = (bf16[2,544,128]{2,1,0:T(8,128)(2,1)S(1)}, bf16[2,544,128]{2,1,0:T(8,128)(2,1)S(1)}, u32[]{:S(2)}, u32[]{:S(2)}) collective-permute-start(bf16[2,544,128]{2,1,0:T(8,128)(2,1)S(1)} %shard_map.112.refs_2_), channel_id=1, source_target_pairs={{0,24},{4,28},{8,16},{12,20},{16,8},{20,12},{24,0},{28,4},{1,25},{... | collective-permute-start | bytes 835592 | tf_op jit(solution)/shard_map/ppermute | solution.py:19
  15.9 1.5 %collective-permute-start.1 = (bf16[2,512,128]{2,1,0:T(8,128)(2,1)S(1)}, bf16[2,512,128]{2,1,0:T(8,128)(2,1)S(1)}, u32[]{:S(2)}, u32[]{:S(2)}) collective-permute-start(bf16[2,512,128]{2,1,0:T(8,128)(2,1)S(1)} %collective-permute-done.after_ref.refs_5_), channel_id=1, source_target_pairs={{0,4},{4,0},{8,12},{12,8},{16,20},{20,16},{24,28},{28,24},{1,5},{5... | collective-permute-start | bytes 786440 | tf_op jit(solution)/shard_map/ppermute | solution.py:19
  17.5 0.6 %collective-permute-start.3 = (bf16[2,128,256]{2,1,0:T(8,128)(2,1)S(1)}, bf16[2,128,256]{2,1,0:T(8,128)(2,1)S(1)}, u32[]{:S(2)}, u32[]{:S(2)}) collective-permute-start(bf16[2,128,256]{2,1,0:T(8,128)(2,1)S(1)} %collective-permute-done.2.refs_8_.refs_9_), channel_id=1, source_target_pairs={{0,4},{4,0},{8,12},{12,8},{16,20},{20,16},{24,28},{28,24},{1,5},{5... | collective-permute-start | bytes 393224 | tf_op jit(solution)/shard_map/ppermute | solution.py:19
  18.3 1.9 %shard_map.114.refs_5_ = f32[2,256,128]{2,1,0:T(8,128)S(1)} custom-call(s32[2]{0:T(128)S(1)} %pad_add_fusion.refs_0_, s32[256]{0:T(256)S(1)} %reshape.12.refs_1_, bf16[2,544,128]{2,1,0:T(8,128)(2,1)S(1)} %shard_map.112.refs_2_, bf16[2,512,128]{2,1,0:T(8,128)(2,1)S(1)} %copy-done, bf16[2,512,128]{2,1,0:T(8,128)(2,1)S(1)} %collective-permute-done.4.refs_4_, ...), custom_call_target="tpu_custom_call" | custom-call | flops 2000000000 | tf_op jit(solution)/shard_map/pallas_call | solution.py:23
  20.2 3.5 %collective-permute-done.1.refs_3_.refs_6_ = bf16[2,512,128]{2,1,0:T(8,128)(2,1)S(1)} collective-permute-done((bf16[2,512,128]{2,1,0:T(8,128)(2,1)S(1)}, bf16[2,512,128]{2,1,0:T(8,128)(2,1)S(1)}, u32[]{:S(2)}, u32[]{:S(2)}) %collective-permute-start.1) | collective-permute-done | bytes 262176 | tf_op jit(solution)/shard_map/ppermute | solution.py:19
  23.7 2.1 %shard_map.116 = (f32[2,256,128]{2,1,0:T(8,128)S(1)}, bf16[2,256,128]{2,1,0:T(8,128)(2,1)S(1)}) custom-call(s32[2]{0:T(128)S(1)} %pad_add_fusion.refs_0_, s32[256]{0:T(256)S(1)} %reshape.12.refs_1_, bf16[2,544,128]{2,1,0:T(8,128)(2,1)S(1)} %collective-permute-done.6.refs_2_.refs_1_, bf16[2,512,128]{2,1,0:T(8,128)(2,1)S(1)} %copy-done, ...), custom_call_target="tpu_custom_call" | custom-call | flops 3000000000 | tf_op jit(solution)/shard_map/pallas_call | solution.py:23
  25.8 0.9 %shard_map.117 = bf16[2,256,128]{2,1,0:T(8,128)(2,1)S(1)} custom-call(s32[2]{0:T(128)S(1)} %pad_add_fusion.refs_0_, bf16[2,544,128]{2,1,0:T(8,128)(2,1)S(1)} %collective-permute-done.6.refs_2_.refs_1_, bf16[2,256,128]{2,1,0:T(8,128)(2,1)S(1)} %get-tuple-element.10.refs_2_, f32[2,256,128]{2,1,0:T(8,128)S(1)} %get-tuple-element.11.refs_3_, ...), custom_call_target="tpu_custom_call" | custom-call | flops 1000000000 | tf_op jit(solution)/shard_map/pallas_call | solution.py:23
  26.8 1.8 %collective-permute-start.7 = (bf16[2,256,128]{2,1,0:T(8,128)(2,1)S(1)}, bf16[2,256,128]{2,1,0:T(8,128)(2,1)S(1)}, u32[]{:S(2)}, u32[]{:S(2)}) collective-permute-start(bf16[2,256,128]{2,1,0:T(8,128)(2,1)S(1)} %shard_map.117), channel_id=1, source_target_pairs={{0,24},{4,28},{8,16},{12,20},{16,8},{20,12},{24,0},{28,4},{1,25},{... | collective-permute-start | bytes 393224 | tf_op jit(solution)/shard_map/ppermute | solution.py:19
  28.5 1.2 %shard_map.115.own_ref = f32[2,256,128]{2,1,0:T(8,128)S(1)} custom-call(s32[2]{0:T(128)S(1)} %pad_add_fusion.refs_0_, s32[256]{0:T(256)S(1)} %reshape.12.refs_1_, bf16[2,544,128]{2,1,0:T(8,128)(2,1)S(1)} %shard_map.112.refs_2_, bf16[2,512,128]{2,1,0:T(8,128)(2,1)S(1)} %collective-permute-done.1.refs_3_.refs_6_, ...), custom_call_target="tpu_custom_call" | custom-call | flops 2000000000 | tf_op jit(solution)/shard_map/pallas_call | solution.py:23
  29.7 4.0 %collective-permute-done.7.back_ref = bf16[2,256,128]{2,1,0:T(8,128)(2,1)S(1)} collective-permute-done((bf16[2,256,128]{2,1,0:T(8,128)(2,1)S(1)}, bf16[2,256,128]{2,1,0:T(8,128)(2,1)S(1)}, u32[]{:S(2)}, u32[]{:S(2)}) %collective-permute-start.7) | collective-permute-done | bytes 131104 | tf_op jit(solution)/shard_map/ppermute | solution.py:19
  33.7 0.8 %shard_map.118 = (f32[2,128,128]{2,1,0:T(8,128)}, f32[2,128,128]{2,1,0:T(8,128)}, bf16[2,128,128]{2,1,0:T(8,128)(2,1)S(1)}) custom-call(f32[2,256,128]{2,1,0:T(8,128)S(1)} %shard_map.115.own_ref, bf16[2,256,128]{2,1,0:T(8,128)(2,1)S(1)} %collective-permute-done.7.back_ref, bf16[2,128,128]{2,1,0:T(8,128)(2,1)S(1)} %copy-done.3, ...), custom_call_target="tpu_custom_call" | custom-call | flops 1000000000 | tf_op jit(solution)/shard_map/pallas_call | solution.py:23
  34.6 1.5 %collective-permute-start.12 = (bf16[2,128,128]{2,1,0:T(8,128)(2,1)S(1)}, bf16[2,128,128]{2,1,0:T(8,128)(2,1)S(1)}, u32[]{:S(2)}, u32[]{:S(2)}) collective-permute-start(bf16[2,128,128]{2,1,0:T(8,128)(2,1)S(1)} %get-tuple-element.16.refs_2_), channel_id=1, source_target_pairs={{0,2},{1,3},{2,0},{3,1},{4,6},{5,7},{6,4},{7,5},{8,10},{9,11},{10,... | collective-permute-start | bytes 196616 | tf_op jit(solution)/shard_map/ppermute | solution.py:19
  36.1 2.7 %collective-permute-done.12.refs_4_ = bf16[2,128,128]{2,1,0:T(8,128)(2,1)S(1)} collective-permute-done((bf16[2,128,128]{2,1,0:T(8,128)(2,1)S(1)}, bf16[2,128,128]{2,1,0:T(8,128)(2,1)S(1)}, u32[]{:S(2)}, u32[]{:S(2)}) %collective-permute-start.12) | collective-permute-done | bytes 65568 | tf_op jit(solution)/shard_map/ppermute | solution.py:19
  38.9 1.3 %shard_map.119 = (bf16[8,128,1024]{2,1,0:T(8,128)(2,1)S(1)}, bf16[8,128,128]{2,1,0:T(8,128)(2,1)S(1)}) custom-call(s32[2]{0:T(128)S(1)} %pad_add_fusion.refs_0_, s32[256]{0:T(256)S(1)} %reshape.12.refs_1_, bf16[8,128,128]{2,1,0:T(8,128)(2,1)S(1)} %bitcast.3, bf16[2,512,128]{2,1,0:T(8,128)(2,1)S(1)} %copy-done, ...), custom_call_target="tpu_custom_call" | custom-call | flops 2000000000 | tf_op jit(solution)/shard_map/pallas_call | solution.py:23
  40.2 0.9 %shard_map.120 = bf16[8,128,128]{2,1,0:T(8,128)(2,1)S(1)} custom-call(bf16[8,128,1024]{2,1,0:T(8,128)(2,1)S(1)} %get-tuple-element.14.refs_0_, bf16[8,128,128]{2,1,0:T(8,128)(2,1)S(1)} %get-tuple-element.15.refs_1_, bf16[2,128,128]{2,1,0:T(8,128)(2,1)S(1)} %get-tuple-element.16.refs_2_, bf16[2,128,128]{2,1,0:T(8,128)(2,1)S(1)} %collective-permute-done.11.refs_3_, ...), custom_call_target="tpu_custom_call" | custom-call | flops 1000000000 | tf_op jit(solution)/shard_map/pallas_call | solution.py:23
  41.1 13.7 %all_to_all.5 = bf16[8,128,128]{2,1,0:T(8,128)(2,1)S(1)} all-to-all(bf16[8,128,128]{2,1,0:T(8,128)(2,1)S(1)} %shard_map.120), channel_id=1, replica_groups=mesh['wide'=8,'narrow'=4] {'wide'}, dimensions={0} | all-to-all | bytes 524288 | tf_op jit(solution)/shard_map/all_to_all | solution.py:285
  54.8 0.7 %convert_reduce_fusion = f32[128,128]{1,0:T(8,128)} fusion(bf16[8,128,128]{2,1,0:T(8,128)(2,1)S(1)} %all_to_all.5), kind=kLoop, calls=%fused_computation | loop fusion | flops 245760 | bytes 327680 | tf_op jit(solution)/shard_map/reduce_sum | solution.py:286
  (40 shorter events, 1.6 us)
Async XLA Ops:
  0.6 10.1 %copy-start = (bf16[2,512,128]{2,1,0:T(8,128)(2,1)S(1)}, bf16[2,512,128]{2,1,0:T(8,128)(2,1)}, u32[]{:S(2)}) copy-start(bf16[2,512,128]{2,1,0:T(8,128)(2,1)} %refs_3_.5) | copy-start | bytes 786436
  0.6 10.1 %collective-permute-start = (bf16[2,512,128]{2,1,0:T(8,128)(2,1)}, bf16[2,512,128]{2,1,0:T(8,128)(2,1)S(1)}, u32[]{:S(2)}, u32[]{:S(2)}) collective-permute-start(bf16[2,512,128]{2,1,0:T(8,128)(2,1)} %refs_3_.5), channel_id=1, source_target_pairs={{0,8},{4,12},{8,0},{12,4},{16,24},{20,28},{24,16},{28,20},{1,9},{5... | collective-permute-start | bytes 786440 | tf_op jit(solution)/shard_map/ppermute | solution.py:19
  3.7 13.8 %collective-permute-start.4 = (bf16[2,512,128]{2,1,0:T(8,128)(2,1)}, bf16[2,512,128]{2,1,0:T(8,128)(2,1)S(1)}, u32[]{:S(2)}, u32[]{:S(2)}) collective-permute-start(bf16[2,512,128]{2,1,0:T(8,128)(2,1)} %refs_3_.5), channel_id=1, source_target_pairs={{0,4},{4,0},{8,12},{12,8},{16,20},{20,16},{24,28},{28,24},{1,5},{5... | collective-permute-start | bytes 786440 | tf_op jit(solution)/shard_map/ppermute | solution.py:19
  5.2 12.9 %collective-permute-start.9 = (bf16[2,512,128]{2,1,0:T(8,128)(2,1)}, bf16[2,512,128]{2,1,0:T(8,128)(2,1)S(1)}, u32[]{:S(2)}, u32[]{:S(2)}) collective-permute-start(bf16[2,512,128]{2,1,0:T(8,128)(2,1)} %refs_3_.5), channel_id=1, source_target_pairs={{0,2},{1,3},{2,0},{3,1},{4,6},{5,7},{6,4},{7,5},{8,10},{9,11},{10,... | collective-permute-start | bytes 786440 | tf_op jit(solution)/shard_map/ppermute | solution.py:19
  6.7 0.8 %copy-start.2 = (bf16[2,128,128]{2,1,0:T(8,128)(2,1)S(1)}, bf16[2,128,128]{2,1,0:T(8,128)(2,1)}, u32[]{:S(2)}) copy-start(bf16[2,128,128]{2,1,0:T(8,128)(2,1)} %amps_ref.3) | copy-start | bytes 196612
  8.4 1.1 %copy-start.10 = (s32[64,4]{0,1:T(4,128)S(1)}, s32[64,4]{0,1:T(4,128)}, u32[]{:S(2)}) copy-start(s32[64,4]{0,1:T(4,128)} %param.16) | copy-start | bytes 3076
  8.4 2.3 %copy-start.7 = (s32[2,12]{1,0:T(2,128)S(1)}, s32[2,12]{1,0:T(2,128)}, u32[]{:S(2)}) copy-start(s32[2,12]{1,0:T(2,128)} %readers_ref.1) | copy-start | bytes 292
  8.4 2.3 %copy-start.8 = (f32[2,12]{1,0:T(2,128)S(1)}, f32[2,12]{1,0:T(2,128)}, u32[]{:S(2)}) copy-start(f32[2,12]{1,0:T(2,128)} %couple_ref.1) | copy-start | bytes 292
  8.5 7.4 %collective-permute-start.2 = (bf16[2,128,256]{2,1,0:T(8,128)(2,1)S(1)}, bf16[2,128,256]{2,1,0:T(8,128)(2,1)S(1)}, u32[]{:S(2)}, u32[]{:S(2)}) collective-permute-start(bf16[2,128,256]{2,1,0:T(8,128)(2,1)S(1)} %shard_map.113.refs_6_.refs_7_), channel_id=1, source_target_pairs={{0,8},{4,12},{8,0},{12,4},{16,24},{20,28},{24,16},{28,20},{1,9},{5... | collective-permute-start | bytes 393224 | tf_op jit(solution)/shard_map/ppermute | solution.py:19
  9.0 8.5 %collective-permute-start.5 = (bf16[2,128,256]{2,1,0:T(8,128)(2,1)S(1)}, bf16[2,128,256]{2,1,0:T(8,128)(2,1)S(1)}, u32[]{:S(2)}, u32[]{:S(2)}) collective-permute-start(bf16[2,128,256]{2,1,0:T(8,128)(2,1)S(1)} %shard_map.113.refs_6_.refs_7_), channel_id=1, source_target_pairs={{0,4},{4,0},{8,12},{12,8},{16,20},{20,16},{24,28},{28,24},{1,5},{5... | collective-permute-start | bytes 393224 | tf_op jit(solution)/shard_map/ppermute | solution.py:19
  11.5 12.3 %collective-permute-start.6 = (bf16[2,544,128]{2,1,0:T(8,128)(2,1)S(1)}, bf16[2,544,128]{2,1,0:T(8,128)(2,1)S(1)}, u32[]{:S(2)}, u32[]{:S(2)}) collective-permute-start(bf16[2,544,128]{2,1,0:T(8,128)(2,1)S(1)} %shard_map.112.refs_2_), channel_id=1, source_target_pairs={{0,24},{4,28},{8,16},{12,20},{16,8},{20,12},{24,0},{28,4},{1,25},{... | collective-permute-start | bytes 835592 | tf_op jit(solution)/shard_map/ppermute | solution.py:19
  15.9 7.8 %collective-permute-start.1 = (bf16[2,512,128]{2,1,0:T(8,128)(2,1)S(1)}, bf16[2,512,128]{2,1,0:T(8,128)(2,1)S(1)}, u32[]{:S(2)}, u32[]{:S(2)}) collective-permute-start(bf16[2,512,128]{2,1,0:T(8,128)(2,1)S(1)} %collective-permute-done.after_ref.refs_5_), channel_id=1, source_target_pairs={{0,4},{4,0},{8,12},{12,8},{16,20},{20,16},{24,28},{28,24},{1,5},{5... | collective-permute-start | bytes 786440 | tf_op jit(solution)/shard_map/ppermute | solution.py:19
  17.5 21.3 %collective-permute-start.8 = (bf16[2,512,128]{2,1,0:T(8,128)(2,1)S(1)}, bf16[2,512,128]{2,1,0:T(8,128)(2,1)S(1)}, u32[]{:S(2)}, u32[]{:S(2)}) collective-permute-start(bf16[2,512,128]{2,1,0:T(8,128)(2,1)S(1)} %copy-done), channel_id=1, source_target_pairs={{0,1},{1,0},{2,3},{3,2},{4,5},{5,4},{6,7},{7,6},{8,9},{9,8},{10,11... | collective-permute-start | bytes 786440 | tf_op jit(solution)/shard_map/ppermute | solution.py:19
  17.5 8.3 %collective-permute-start.3 = (bf16[2,128,256]{2,1,0:T(8,128)(2,1)S(1)}, bf16[2,128,256]{2,1,0:T(8,128)(2,1)S(1)}, u32[]{:S(2)}, u32[]{:S(2)}) collective-permute-start(bf16[2,128,256]{2,1,0:T(8,128)(2,1)S(1)} %collective-permute-done.2.refs_8_.refs_9_), channel_id=1, source_target_pairs={{0,4},{4,0},{8,12},{12,8},{16,20},{20,16},{24,28},{28,24},{1,5},{5... | collective-permute-start | bytes 393224 | tf_op jit(solution)/shard_map/ppermute | solution.py:19
  18.1 20.7 %collective-permute-start.10 = (bf16[2,512,128]{2,1,0:T(8,128)(2,1)S(1)}, bf16[2,512,128]{2,1,0:T(8,128)(2,1)S(1)}, u32[]{:S(2)}, u32[]{:S(2)}) collective-permute-start(bf16[2,512,128]{2,1,0:T(8,128)(2,1)S(1)} %collective-permute-done.9.refs_5_), channel_id=1, source_target_pairs={{0,1},{1,0},{2,3},{3,2},{4,5},{5,4},{6,7},{7,6},{8,9},{9,8},{10,11... | collective-permute-start | bytes 786440 | tf_op jit(solution)/shard_map/ppermute | solution.py:19
  26.7 7.0 %copy-start.3 = (bf16[2,128,128]{2,1,0:T(8,128)(2,1)S(1)}, bf16[2,128,128]{2,1,0:T(8,128)(2,1)}, u32[]{:S(2)}) copy-start(bf16[2,128,128]{2,1,0:T(8,128)(2,1)} %amps_ref.3) | copy-start | bytes 196612
  26.7 7.0 %copy-start.5 = (bf16[2,128,128]{2,1,0:T(8,128)(2,1)S(1)}, bf16[2,128,128]{2,1,0:T(8,128)(2,1)}, u32[]{:S(2)}) copy-start(bf16[2,128,128]{2,1,0:T(8,128)(2,1)} %resp_ref.3) | copy-start | bytes 196612
  26.7 7.0 %copy-start.6 = (bf16[2,128,128]{2,1,0:T(8,128)(2,1)S(1)}, bf16[2,128,128]{2,1,0:T(8,128)(2,1)}, u32[]{:S(2)}) copy-start(bf16[2,128,128]{2,1,0:T(8,128)(2,1)} %ints_ref.1) | copy-start | bytes 196612
  26.8 7.0 %copy-start.9 = (f32[2,128]{1,0:T(2,128)S(1)}, f32[2,128]{1,0:T(2,128)}, u32[]{:S(2)}) copy-start(f32[2,128]{1,0:T(2,128)} %energy_ref.1) | copy-start | bytes 3076
  26.8 6.9 %collective-permute-start.7 = (bf16[2,256,128]{2,1,0:T(8,128)(2,1)S(1)}, bf16[2,256,128]{2,1,0:T(8,128)(2,1)S(1)}, u32[]{:S(2)}, u32[]{:S(2)}) collective-permute-start(bf16[2,256,128]{2,1,0:T(8,128)(2,1)S(1)} %shard_map.117), channel_id=1, source_target_pairs={{0,24},{4,28},{8,16},{12,20},{16,8},{20,12},{24,0},{28,4},{1,25},{... | collective-permute-start | bytes 393224 | tf_op jit(solution)/shard_map/ppermute | solution.py:19
  29.7 9.1 %copy-start.1 = (bf16[1024,128]{1,0:T(8,128)(2,1)S(1)}, bf16[1024,128]{1,0:T(8,128)(2,1)}, u32[]{:S(2)}) copy-start(bf16[1024,128]{1,0:T(8,128)(2,1)} %param.17) | copy-start | bytes 786436
  34.6 4.3 %collective-permute-start.12 = (bf16[2,128,128]{2,1,0:T(8,128)(2,1)S(1)}, bf16[2,128,128]{2,1,0:T(8,128)(2,1)S(1)}, u32[]{:S(2)}, u32[]{:S(2)}) collective-permute-start(bf16[2,128,128]{2,1,0:T(8,128)(2,1)S(1)} %get-tuple-element.16.refs_2_), channel_id=1, source_target_pairs={{0,2},{1,3},{2,0},{3,1},{4,6},{5,7},{6,4},{7,5},{8,10},{9,11},{10,... | collective-permute-start | bytes 196616 | tf_op jit(solution)/shard_map/ppermute | solution.py:19
  36.1 4.1 %collective-permute-start.11 = (bf16[2,128,128]{2,1,0:T(8,128)(2,1)S(1)}, bf16[2,128,128]{2,1,0:T(8,128)(2,1)S(1)}, u32[]{:S(2)}, u32[]{:S(2)}) collective-permute-start(bf16[2,128,128]{2,1,0:T(8,128)(2,1)S(1)} %get-tuple-element.16.refs_2_), channel_id=1, source_target_pairs={{0,1},{1,0},{2,3},{3,2},{4,5},{5,4},{6,7},{7,6},{8,9},{9,8},{10,11... | collective-permute-start | bytes 196616 | tf_op jit(solution)/shard_map/ppermute | solution.py:19
  38.8 1.4 %collective-permute-start.13 = (bf16[2,128,128]{2,1,0:T(8,128)(2,1)S(1)}, bf16[2,128,128]{2,1,0:T(8,128)(2,1)S(1)}, u32[]{:S(2)}, u32[]{:S(2)}) collective-permute-start(bf16[2,128,128]{2,1,0:T(8,128)(2,1)S(1)} %collective-permute-done.12.refs_4_), channel_id=1, source_target_pairs={{0,1},{1,0},{2,3},{3,2},{4,5},{5,4},{6,7},{7,6},{8,9},{9,8},{10,11... | collective-permute-start | bytes 196616 | tf_op jit(solution)/shard_map/ppermute | solution.py:19
  (1 other events, 0.8 us)

commit v3 on v2

--- a/solution.py
+++ b/solution.py
@@ -12,22 +12,28 @@
 SMEM = pl.BlockSpec(memory_space=pltpu.SMEM)
 VMEM = pl.BlockSpec(memory_space=pltpu.VMEM)
 ANY = pl.BlockSpec(memory_space=pl.ANY)
-
-
-def swap(value, axis, mask):
-    size = lax.axis_size(axis)
-    return lax.ppermute(value, axis, [(i, i ^ mask) for i in range(size)])
-
-
-def call(kernel, out_shape, specs, micros, *args, scratch=()):
+HBM = pl.BlockSpec(memory_space=pltpu.HBM)
+
+
+def swap(value, wide_mask, narrow_mask, among=None):
+    wide, narrow = lax.axis_size("wide"), lax.axis_size("narrow")
+    pairs = [
+        (i * narrow + j, (i ^ wide_mask) * narrow + (j ^ narrow_mask))
+        for i in (among or range(wide))
+        for j in range(narrow)
+    ]
+    return lax.ppermute(value, ("wide", "narrow"), pairs)
+
+
+def call(kernel, out_shape, specs, micros, *args, scratch=(), out_specs=None, limit=32):
     return pl.pallas_call(
         kernel,
         out_shape=out_shape,
         in_specs=specs,
-        out_specs=jax.tree.map(lambda _: VMEM, out_shape),
+        out_specs=out_specs or jax.tree.map(lambda _: VMEM, out_shape),
         scratch_shapes=scratch,
         cost_estimate=pl.CostEstimate(flops=int(micros * 1e9), bytes_accessed=0, transcendentals=0),
-        compiler_params=pltpu.CompilerParams(vmem_limit_bytes=32 * 1024 * 1024),
+        compiler_params=pltpu.CompilerParams(vmem_limit_bytes=limit * 1024 * 1024),
     )(*args)
 
 
@@ -57,6 +63,23 @@
         high = c.astype(BF16)
         out_ref[p, nfun : nfun + count, :] = high
         out_ref[p, nfun + count :, :] = (c - high.astype(F32)).astype(BF16)
+
+
+def beside_kernel(*refs):
+    *in_refs, _, out_ref = refs
+    count = in_refs[0].shape[0]
+    for i, ref in enumerate(in_refs):
+        out_ref[i * count : (i + 1) * count] = ref[...]
+
+
+def mark_kernel(after_ref, out_ref):
+    del after_ref
+    out_ref[...] = jnp.zeros_like(out_ref)
+
+
+def again_kernel(value_ref, after_ref, out_ref):
+    del after_ref
+    out_ref[...] = value_ref[...]
 
 
 def load_coefficients(pack_ref, c_ref):
@@ -134,7 +157,10 @@
         out_ref[g] = sums[g].astype(out_ref.dtype)
 
 
-def update_kernel(own_ref, back_ref, amps_ref, resp_ref, ints_ref, energy_ref, new_amps_ref, new_resp_ref, w_ref):
+def update_kernel(
+    own_ref, back_ref, amps_ref, resp_ref, ints_ref, energy_ref, after_ref, new_amps_ref, new_resp_ref, w_ref
+):
+    del after_ref
     npno = amps_ref.shape[1]
     for p in range(amps_ref.shape[0]):
         across = jnp.broadcast_to(energy_ref[pl.ds(p, 1), :], (npno, npno))
@@ -153,38 +179,52 @@
         w_ref[p] = (0.5 * (prod + prod.T)).astype(BF16)
 
 
-def place_kernel(blk, narrow, *refs):
+def place_kernel(blk, narrow, pairs, *refs):
     where_ref, dom_ref, ints_ref = refs[:3]
-    q_refs, (full_ref, moved_ref) = refs[3 : 3 + narrow], refs[3 + narrow :]
-    pairs, _, npno = q_refs[0].shape
-    dom_blk = q_refs[0].shape[1] // blk
+    q_refs, (full_ref, moved_ref) = refs[3 : 3 + narrow], refs[4 + narrow :]
+    both, nfun, npno = q_refs[0].shape
+    dom_blk = nfun // blk
+    trash, rows = full_ref.shape[0] - 1, full_ref.shape[1]
     full_ref[...] = jnp.zeros_like(full_ref)
     for k in range(narrow):
-        for p in range(pairs):
-            pair = (where_ref[0] * narrow + (where_ref[1] ^ k)) * pairs + p
-            slot = k * pairs + p
+        for i in range(both):
+            pair = ((where_ref[0] ^ (i // pairs)) * narrow + (where_ref[1] ^ k)) * pairs + i % pairs
+            slot = k * both + i
             blocks = []
             for a in range(dom_blk):
                 f = dom_ref[pair * dom_blk + a]
-                full_ref[f, :, slot * npno : (slot + 1) * npno] = q_refs[k][p, a * blk : (a + 1) * blk, :]
+                for j in range(blk // rows):
+                    dev = f * (blk // rows) + j
+                    at = jnp.where((dev ^ where_ref[0]) & 1, trash, dev // 2)
+                    start = a * blk + j * rows
+                    full_ref[at, :, slot * npno : (slot + 1) * npno] = q_refs[k][i, start : start + rows, :]
                 blocks.append(ints_ref[f])
             moved_ref[slot] = lax.dot_general(
-                q_refs[k][p], jnp.concatenate(blocks, axis=0), (((0,), (0,)), ((), ())), preferred_element_type=F32
+                q_refs[k][i], jnp.concatenate(blocks, axis=0), (((0,), (0,)), ((), ())), preferred_element_type=F32
             ).astype(BF16)
 
 
-def response_kernel(*refs):
-    full_ref, moved_ref = refs[:2]
-    w_refs, out_ref = refs[2:-1], refs[-1]
-    pairs = w_refs[0].shape[0]
+def response_kernel(others, narrow, *refs):
+    where_ref, full_ref, moved_ref, near_w_ref, core_w_ref = refs[:5]
+    out_refs, sum_ref = refs[5:-1], refs[-1]
+    slots = moved_ref.shape[0]
+    both = slots // narrow
     parts = []
-    for k, w_ref in enumerate(w_refs):
-        for p in range(pairs):
-            parts.append(jnp.dot(w_ref[p], moved_ref[k * pairs + p], preferred_element_type=F32).astype(BF16))
+    for slot in range(slots):
+        k, i = slot // both, slot % both
+        w = (core_w_ref if k % 2 else near_w_ref)[k // 2 * both + i]
+        parts.append(jnp.dot(w, moved_ref[slot], preferred_element_type=F32).astype(BF16))
     right = jnp.concatenate(parts, axis=0)
-    blocks, blk, depth = full_ref.shape
-    rows = jnp.dot(full_ref[...].reshape(blocks * blk, depth), right, preferred_element_type=F32).astype(BF16)
-    out_ref[...] = rows.reshape(out_ref.shape)
+    devs, rows, depth = sum_ref.shape[0], full_ref.shape[1], full_ref.shape[2]
+    total = jnp.dot(full_ref[:devs].reshape(devs * rows, depth), right, preferred_element_type=F32)
+    sum_ref[...] = total.reshape(sum_ref.shape)
+    for mask, out_ref in zip([0] + others, out_refs):
+        out_ref[...] = sum_ref[(where_ref[0] ^ mask) // 2].astype(out_ref.dtype)
+
+
+def sum_kernel(*refs):
+    *in_refs, _, out_ref = refs
+    out_ref[...] = sum(ref[...].astype(F32) for ref in in_refs)
 
 
 def per_device(amps, resp, trans, ints, energies, couple, readers, domains, integrals):
@@ -201,35 +241,25 @@
     dom = domains.reshape(-1)
 
     near_q, near_tz = {0: trans}, {}
-    near_q[1] = swap(trans, "wide", 1)
+    near_q[1] = swap(trans, 1, 0)
     for mask in range(2, near, 2):
-        near_q[mask] = swap(trans, "wide", mask)
+        near_q[mask] = swap(trans, mask, 0)
     near_tz[0] = call(
         join_kernel, sds((pairs, npno, 2 * npno), BF16), [ANY, ANY], 1, amps, resp, scratch=[pltpu.SemaphoreType.DMA((2,))]
     )
-    near_tz[1] = swap(near_tz[0], "wide", 1)
+    near_tz[1] = swap(near_tz[0], 1, 0)
     for mask in range(2, near, 2):
-        near_tz[mask] = swap(near_tz[0], "wide", mask)
+        near_tz[mask] = swap(near_tz[0], mask, 0)
     pack = call(
         functools.partial(pack_kernel, blk),
         sds((pairs, nfun + 2 * count, npno), BF16),
         [SMEM, SMEM, VMEM, ANY], 1,
         readers, couple, trans, near_q[near - 2],
     )
-    far_pack = swap(pack, "wide", partner)
+    far_pack = swap(pack, partner, 0)
     for mask in range(2, near, 2):
-        near_q[mask + 1] = swap(near_q[mask], "wide", 1)
-        near_tz[mask + 1] = swap(near_tz[mask], "wide", 1)
-    narrow_q = {0: trans}
-    for mask in range(1, narrow):
-        narrow_q[mask] = swap(narrow_q[mask - 1], "narrow", 1) if mask % 2 else swap(trans, "narrow", mask)
-
-    full, moved = call(
-        functools.partial(place_kernel, blk, narrow),
-        (sds((nbas // blk, blk, narrow * pairs * npno), BF16), sds((narrow * pairs, npno, cols), BF16)),
-        [SMEM, SMEM] + [VMEM] * (1 + narrow), 2,
-        where, dom, integrals.reshape(nbas // blk, blk, cols), *[narrow_q[k] for k in range(narrow)],
-    )
+        near_q[mask + 1] = swap(near_q[mask], 1, 0)
+        near_tz[mask + 1] = swap(near_tz[mask], 1, 0)
     early = [0, 1] + list(range(2, near, 2))
     late = list(range(3, near, 2))
     scratch = [
@@ -258,32 +288,58 @@
         where, far_pack, overlap, far, *[near_tz[m] for m in late],
         scratch=scratch[1:],
     )
-    back = swap(far, "wide", partner)
-    own = call(
+    back = swap(far, partner, 0)
+    own_late = call(
         functools.partial(couple_kernel, late, [], blk, narrow, 0, True),
         sums,
         [SMEM] * 2 + [VMEM] * (2 + 2 * len(late)), 2,
         where, dom, pack, *[near_q[m] for m in late], *[near_tz[m] for m in late], own,
         scratch=scratch,
     )
+    both_q = call(
+        beside_kernel, sds((2 * pairs, nfun, npno), BF16), [VMEM] * 2 + [ANY], 0.3, trans, near_q[1], near_tz[1]
+    )
+    core_q = swap(both_q, 0, 1)
     mats = sds((pairs, npno, npno), F32)
     new_amps, new_resp, weights = call(
         update_kernel,
         (mats, mats, sds((pairs, npno, npno), BF16)),
-        [VMEM] * 6, 1,
-        own, back, amps, resp, ints, energies,
-    )
-    narrow_w = {0: weights}
-    for mask in range(1, narrow):
-        narrow_w[mask] = swap(narrow_w[mask - 1], "narrow", 1) if mask % 2 else swap(weights, "narrow", mask)
-    partial = call(
-        response_kernel,
-        sds((wide, nbas // wide, cols), BF16),
-        [VMEM] * (2 + narrow), 1,
-        full, moved, *[narrow_w[k] for k in range(narrow)],
-    )
-    shares = lax.all_to_all(partial, "wide", 0, 0, tiled=True)
-    response = jnp.sum(shares.astype(F32), axis=0)
+        [VMEM] * 6 + [ANY], 1,
+        own_late, back, amps, resp, ints, energies, core_q,
+    )
+    narrow_q = {0: both_q, 1: core_q}
+    for mask in range(2, narrow, 2):
+        arrived = swap(both_q, 0, mask)
+        narrow_q[mask] = call(again_kernel, sds(both_q.shape, BF16), [VMEM, ANY], 0.3, arrived, weights)
+        narrow_q[mask + 1] = swap(narrow_q[mask], 0, 1)
+    slots = 2 * narrow * pairs
+    full, moved = call(
+        functools.partial(place_kernel, blk, narrow, pairs),
+        (sds((near + 1, nbas // wide, slots * npno), BF16), sds((slots, npno, cols), BF16)),
+        [SMEM, SMEM] + [VMEM] * (1 + narrow) + [ANY], 1,
+        where, dom, integrals.reshape(nbas // blk, blk, cols), *[narrow_q[k] for k in range(narrow)], weights,
+    )
+    group = [(bit, mask) for mask in range(0, narrow, 2) for bit in range(2)]
+    arrived = {key: swap(weights, *key) if any(key) else weights for key in sorted(group, reverse=True)}
+    near_w = call(
+        beside_kernel, sds((len(group) * pairs, npno, npno), BF16), [VMEM] * len(group) + [ANY], 0.3,
+        *[arrived[key] for key in group], moved,
+    )
+    core_w = swap(near_w, 0, 1)
+    others = list(range(wide - 2, 0, -2))
+    block = (nbas // wide, cols)
+    shares = call(
+        functools.partial(response_kernel, others, narrow),
+        (sds(block, F32),) + (sds(block, BF16),) * len(others),
+        [SMEM] + [VMEM] * 4, 1,
+        where, full, moved, near_w, core_w,
+        scratch=[pltpu.VMEM((near,) + block, F32)],
+    )
+    received = [swap(share, mask, 0) for mask, share in zip(others, shares[1:])]
+    mark = call(mark_kernel, sds((8, 128), F32), [ANY], 0.1, received[0])
+    response = call(
+        sum_kernel, sds(block, F32), [VMEM] * (1 + len(others)) + [ANY], 0.1, shares[0], *received, mark
+    )
     return (new_amps, new_resp, response)
 
 

time: 55.7 us -> 53.6 us (0.962)
  blocking collectives: 13.7 us -> 0 us
  starting transfers between devices: 17.2 us -> 22.6 us
  waiting for transfers between devices: 11.2 us -> 16.1 us
  Pallas kernels: 9.89 us -> 11.8 us
  other arithmetic: 0.74 us -> 0.07 us
    all_to_all x1 -> x0, blocking collectives: 13.7 us -> none  [per_device(): shares = lax.all_to_all(partial, 'wide', 0, 0, tiled=True)]
    ppermute x14 -> x18, starting transfers between devices: 17.2 us -> 22.6 us  [swap(): return lax.ppermute(value, ('wide', 'narrow'), pairs)]
    ppermute x14 -> x18, waiting for transfers between devices: 11.2 us -> 16.1 us  [swap(): return lax.ppermute(value, ('wide', 'narrow'), pairs)]
    pallas_call x9 -> x14, Pallas kernels: 9.89 us -> 11.8 us  [call(): pl.pallas_call(kernel, out_shape=out_shape, in_specs=specs, out_specs=out...]
    reduce_sum x1 -> x0, other arithmetic: 0.67 us -> none  [per_device(): response = jnp.sum(shares.astype(F32), axis=0)]
  transfers between devices with their start and end apart: 14 -> 18, of which waited for: 4 -> 9; matrix products, arithmetic and copies ran while one was open for 0% -> 1% of each run, Pallas kernels for 16% -> 18%
where the time goes in v3:
time: 53.6 us; the launch traced here: 53.4 us
  starting transfers between devices  22.6 us (42%)
  waiting for transfers between devices  16.1 us (30%)
  Pallas kernels  11.8 us (22%)
  local copies, waits for them, and re-layouts  1.93 us (4%)
  between operations  0.85 us (2%)
    ppermute x18, starting transfers between devices, swap(): return lax.ppermute(value, ('wide', 'narrow'), pairs)  22.6 us
    ppermute x18, waiting for transfers between devices, swap(): return lax.ppermute(value, ('wide', 'narrow'), pairs)  16.1 us
    pallas_call x14, Pallas kernels, call(): pl.pallas_call(kernel, out_shape=out_shape, in_specs=specs, out_specs=out...  11.8 us
    unnamed x23, local copies, waits for them, and re-layouts  1.82 us
  transfers between devices with their start and end apart: 18, of which 9 were waited for; matrix products, arithmetic and copies ran while one was open for 1% of the time, Pallas kernels for 18%

profile of v3, /device:TPU:0, one launch (start us, length us, event | category | flops | bytes accessed | tf_op | source)
XLA Modules:
  0.0 53.4 jit_solution(6298111873630034314)
XLA Ops:
  0.6 3.1 %collective-permute-start = (bf16[2,512,128]{2,1,0:T(8,128)(2,1)}, bf16[2,512,128]{2,1,0:T(8,128)(2,1)S(1)}, u32[]{:S(2)}, u32[]{:S(2)}) collective-permute-start(bf16[2,512,128]{2,1,0:T(8,128)(2,1)} %refs_0_.1), channel_id=1, source_target_pairs={{0,8},{1,9},{2,10},{3,11},{4,12},{5,13},{6,14},{7,15},{8,0},{9,1},... | collective-permute-start | bytes 786440 | tf_op jit(solution)/shard_map/ppermute | solution.py:25
  3.7 1.5 %collective-permute-start.4 = (bf16[2,512,128]{2,1,0:T(8,128)(2,1)}, bf16[2,512,128]{2,1,0:T(8,128)(2,1)S(1)}, u32[]{:S(2)}, u32[]{:S(2)}) collective-permute-start(bf16[2,512,128]{2,1,0:T(8,128)(2,1)} %refs_0_.1), channel_id=1, source_target_pairs={{0,4},{1,5},{2,6},{3,7},{4,0},{5,1},{6,2},{7,3},{8,12},{9,13},{10,... | collective-permute-start | bytes 786440 | tf_op jit(solution)/shard_map/ppermute | solution.py:25
  7.7 3.4 %collective-permute-done.after_ref.refs_5_ = bf16[2,512,128]{2,1,0:T(8,128)(2,1)S(1)} collective-permute-done((bf16[2,512,128]{2,1,0:T(8,128)(2,1)}, bf16[2,512,128]{2,1,0:T(8,128)(2,1)S(1)}, u32[]{:S(2)}, u32[]{:S(2)}) %collective-permute-start) | collective-permute-done | bytes 262176 | tf_op jit(solution)/shard_map/ppermute | solution.py:25
  11.8 4.1 %collective-permute-start.6 = (bf16[2,544,128]{2,1,0:T(8,128)(2,1)S(1)}, bf16[2,544,128]{2,1,0:T(8,128)(2,1)S(1)}, u32[]{:S(2)}, u32[]{:S(2)}) collective-permute-start(bf16[2,544,128]{2,1,0:T(8,128)(2,1)S(1)} %shard_map.112.refs_2_), channel_id=1, source_target_pairs={{0,24},{1,25},{2,26},{3,27},{4,28},{5,29},{6,30},{7,31},{8,16},{9,... | collective-permute-start | bytes 835592 | tf_op jit(solution)/shard_map/ppermute | solution.py:25
  15.9 1.5 %collective-permute-start.1 = (bf16[2,512,128]{2,1,0:T(8,128)(2,1)S(1)}, bf16[2,512,128]{2,1,0:T(8,128)(2,1)S(1)}, u32[]{:S(2)}, u32[]{:S(2)}) collective-permute-start(bf16[2,512,128]{2,1,0:T(8,128)(2,1)S(1)} %collective-permute-done.after_ref.refs_5_), channel_id=1, source_target_pairs={{0,4},{1,5},{2,6},{3,7},{4,0},{5,1},{6,2},{7,3},{8,12},{9,13},{10,... | collective-permute-start | bytes 786440 | tf_op jit(solution)/shard_map/ppermute | solution.py:25
  18.4 1.6 %collective-permute-start.9 = (bf16[4,512,128]{2,1,0:T(8,128)(2,1)S(1)}, bf16[4,512,128]{2,1,0:T(8,128)(2,1)S(1)}, u32[]{:S(2)}, u32[]{:S(2)}) collective-permute-start(bf16[4,512,128]{2,1,0:T(8,128)(2,1)S(1)} %shard_map.118.refs_3_), channel_id=1, source_target_pairs={{0,2},{1,3},{2,0},{3,1},{4,6},{5,7},{6,4},{7,5},{8,10},{9,11},{10,... | collective-permute-start | bytes 1572872 | tf_op jit(solution)/shard_map/ppermute | solution.py:25
  20.0 1.9 %shard_map.114.refs_5_ = f32[2,256,128]{2,1,0:T(8,128)S(1)} custom-call(s32[2]{0:T(128)S(1)} %pad_add_fusion.refs_0_, s32[256]{0:T(256)S(1)} %reshape.12.refs_1_, bf16[2,544,128]{2,1,0:T(8,128)(2,1)S(1)} %shard_map.112.refs_2_, bf16[2,512,128]{2,1,0:T(8,128)(2,1)S(1)} %copy-done, bf16[2,512,128]{2,1,0:T(8,128)(2,1)S(1)} %collective-permute-done.4.refs_4_.refs_1_, ...), custom_call_target="tpu_custom_call" | custom-call | flops 2000000000 | tf_op jit(solution)/shard_map/pallas_call | solution.py:29
  21.9 1.1 %collective-permute-done.1.refs_3_.refs_6_ = bf16[2,512,128]{2,1,0:T(8,128)(2,1)S(1)} collective-permute-done((bf16[2,512,128]{2,1,0:T(8,128)(2,1)S(1)}, bf16[2,512,128]{2,1,0:T(8,128)(2,1)S(1)}, u32[]{:S(2)}, u32[]{:S(2)}) %collective-permute-start.1) | collective-permute-done | bytes 262176 | tf_op jit(solution)/shard_map/ppermute | solution.py:25
  23.1 2.1 %shard_map.116 = (f32[2,256,128]{2,1,0:T(8,128)S(1)}, bf16[2,256,128]{2,1,0:T(8,128)(2,1)S(1)}) custom-call(s32[2]{0:T(128)S(1)} %pad_add_fusion.refs_0_, s32[256]{0:T(256)S(1)} %reshape.12.refs_1_, bf16[2,544,128]{2,1,0:T(8,128)(2,1)S(1)} %collective-permute-done.6.refs_2_.refs_1_, bf16[2,512,128]{2,1,0:T(8,128)(2,1)S(1)} %copy-done, ...), custom_call_target="tpu_custom_call" | custom-call | flops 3000000000 | tf_op jit(solution)/shard_map/pallas_call | solution.py:29
  25.2 0.9 %shard_map.117 = bf16[2,256,128]{2,1,0:T(8,128)(2,1)S(1)} custom-call(s32[2]{0:T(128)S(1)} %pad_add_fusion.refs_0_, bf16[2,544,128]{2,1,0:T(8,128)(2,1)S(1)} %collective-permute-done.6.refs_2_.refs_1_, bf16[2,256,128]{2,1,0:T(8,128)(2,1)S(1)} %get-tuple-element.14.refs_2_, f32[2,256,128]{2,1,0:T(8,128)S(1)} %get-tuple-element.15.refs_3_, ...), custom_call_target="tpu_custom_call" | custom-call | flops 1000000000 | tf_op jit(solution)/shard_map/pallas_call | solution.py:29
  26.1 1.3 %collective-permute-start.7 = (bf16[2,256,128]{2,1,0:T(8,128)(2,1)S(1)}, bf16[2,256,128]{2,1,0:T(8,128)(2,1)S(1)}, u32[]{:S(2)}, u32[]{:S(2)}) collective-permute-start(bf16[2,256,128]{2,1,0:T(8,128)(2,1)S(1)} %shard_map.117), channel_id=1, source_target_pairs={{0,24},{1,25},{2,26},{3,27},{4,28},{5,29},{6,30},{7,31},{8,16},{9,... | collective-permute-start | bytes 393224 | tf_op jit(solution)/shard_map/ppermute | solution.py:25
  27.5 1.2 %shard_map.115.own_ref = f32[2,256,128]{2,1,0:T(8,128)S(1)} custom-call(s32[2]{0:T(128)S(1)} %pad_add_fusion.refs_0_, s32[256]{0:T(256)S(1)} %reshape.12.refs_1_, bf16[2,544,128]{2,1,0:T(8,128)(2,1)S(1)} %shard_map.112.refs_2_, bf16[2,512,128]{2,1,0:T(8,128)(2,1)S(1)} %collective-permute-done.1.refs_3_.refs_6_, ...), custom_call_target="tpu_custom_call" | custom-call | flops 2000000000 | tf_op jit(solution)/shard_map/pallas_call | solution.py:29
  28.7 4.4 %collective-permute-done.7.back_ref = bf16[2,256,128]{2,1,0:T(8,128)(2,1)S(1)} collective-permute-done((bf16[2,256,128]{2,1,0:T(8,128)(2,1)S(1)}, bf16[2,256,128]{2,1,0:T(8,128)(2,1)S(1)}, u32[]{:S(2)}, u32[]{:S(2)}) %collective-permute-start.7) | collective-permute-done | bytes 131104 | tf_op jit(solution)/shard_map/ppermute | solution.py:25
  33.1 0.8 %shard_map.119 = (f32[2,128,128]{2,1,0:T(8,128)}, f32[2,128,128]{2,1,0:T(8,128)}, bf16[2,128,128]{2,1,0:T(8,128)(2,1)S(1)}) custom-call(f32[2,256,128]{2,1,0:T(8,128)S(1)} %shard_map.115.own_ref, bf16[2,256,128]{2,1,0:T(8,128)(2,1)S(1)} %collective-permute-done.7.back_ref, bf16[2,128,128]{2,1,0:T(8,128)(2,1)S(1)} %copy-done.3, ...), custom_call_target="tpu_custom_call" | custom-call | flops 1000000000 | tf_op jit(solution)/shard_map/pallas_call | solution.py:29
  34.0 1.6 %collective-permute-start.11 = (bf16[2,128,128]{2,1,0:T(8,128)(2,1)S(1)}, bf16[2,128,128]{2,1,0:T(8,128)(2,1)S(1)}, u32[]{:S(2)}, u32[]{:S(2)}) collective-permute-start(bf16[2,128,128]{2,1,0:T(8,128)(2,1)S(1)} %get-tuple-element.18.after_ref.refs_7_.refs_0_), channel_id=1, source_target_pairs={{0,4},{1,5},{2,6},{3,7},{4,0},{5,1},{6,2},{7,3},{8,12},{9,13},{10,... | collective-permute-start | bytes 196616 | tf_op jit(solution)/shard_map/ppermute | solution.py:25
  35.6 1.5 %collective-permute-start.12 = (bf16[2,128,128]{2,1,0:T(8,128)(2,1)S(1)}, bf16[2,128,128]{2,1,0:T(8,128)(2,1)S(1)}, u32[]{:S(2)}, u32[]{:S(2)}) collective-permute-start(bf16[2,128,128]{2,1,0:T(8,128)(2,1)S(1)} %get-tuple-element.18.after_ref.refs_7_.refs_0_), channel_id=1, source_target_pairs={{0,2},{1,3},{2,0},{3,1},{4,6},{5,7},{6,4},{7,5},{8,10},{9,11},{10,... | collective-permute-start | bytes 196616 | tf_op jit(solution)/shard_map/ppermute | solution.py:25
  37.6 2.0 %shard_map.121 = (bf16[5,128,2048]{2,1,0:T(8,128)(2,1)S(1)}, bf16[16,128,128]{2,1,0:T(8,128)(2,1)S(1)}) custom-call(s32[2]{0:T(128)S(1)} %pad_add_fusion.refs_0_, s32[256]{0:T(256)S(1)} %reshape.12.refs_1_, bf16[8,128,128]{2,1,0:T(8,128)(2,1)S(1)} %bitcast.3, bf16[4,512,128]{2,1,0:T(8,128)(2,1)S(1)} %shard_map.118.refs_3_, ...), custom_call_target="tpu_custom_call" | custom-call | flops 1000000000 | tf_op jit(solution)/shard_map/pallas_call | solution.py:29
  39.8 2.4 %collective-permute-done.13.refs_3_ = bf16[2,128,128]{2,1,0:T(8,128)(2,1)S(1)} collective-permute-done((bf16[2,128,128]{2,1,0:T(8,128)(2,1)S(1)}, bf16[2,128,128]{2,1,0:T(8,128)(2,1)S(1)}, u32[]{:S(2)}, u32[]{:S(2)}) %collective-permute-start.13) | collective-permute-done | bytes 65568 | tf_op jit(solution)/shard_map/ppermute | solution.py:25
  42.4 1.5 %collective-permute-done.14.refs_4_ = bf16[8,128,128]{2,1,0:T(8,128)(2,1)S(1)} collective-permute-done((bf16[8,128,128]{2,1,0:T(8,128)(2,1)S(1)}, bf16[8,128,128]{2,1,0:T(8,128)(2,1)S(1)}, u32[]{:S(2)}, u32[]{:S(2)}) %collective-permute-start.14) | collective-permute-done | bytes 262176 | tf_op jit(solution)/shard_map/ppermute | solution.py:25
  43.9 1.5 %shard_map.123 = (f32[128,128]{1,0:T(8,128)S(1)}, bf16[128,128]{1,0:T(8,128)(2,1)S(1)}, bf16[128,128]{1,0:T(8,128)(2,1)S(1)}, bf16[128,128]{1,0:T(8,128)(2,1)S(1)}) custom-call(s32[2]{0:T(128)S(1)} %pad_add_fusion.refs_0_, bf16[5,128,2048]{2,1,0:T(8,128)(2,1)S(1)} %get-tuple-element.19.refs_1_, bf16[16,128,128]{2,1,0:T(8,128)(2,1)S(1)} %get-tuple-element.20.refs_4_.refs_2_, ...), custom_call_target="tpu_custom_call" | custom-call | flops 1000000000 | tf_op jit(solution)/shard_map/pallas_call | solution.py:29
  45.4 1.4 %collective-permute-start.15 = (bf16[128,128]{1,0:T(8,128)(2,1)S(1)}, bf16[128,128]{1,0:T(8,128)(2,1)S(1)}, u32[]{:S(2)}, u32[]{:S(2)}) collective-permute-start(bf16[128,128]{1,0:T(8,128)(2,1)S(1)} %get-tuple-element.22), channel_id=1, source_target_pairs={{0,24},{1,25},{2,26},{3,27},{4,28},{5,29},{6,30},{7,31},{8,16},{9,... | collective-permute-start | bytes 98312 | tf_op jit(solution)/shard_map/ppermute | solution.py:25
  46.7 2.1 %collective-permute-start.16 = (bf16[128,128]{1,0:T(8,128)(2,1)S(1)}, bf16[128,128]{1,0:T(8,128)(2,1)S(1)}, u32[]{:S(2)}, u32[]{:S(2)}) collective-permute-start(bf16[128,128]{1,0:T(8,128)(2,1)S(1)} %get-tuple-element.23), channel_id=1, source_target_pairs={{0,16},{1,17},{2,18},{3,19},{4,20},{5,21},{6,22},{7,23},{8,24},{9,... | collective-permute-start | bytes 98312 | tf_op jit(solution)/shard_map/ppermute | solution.py:25
  48.8 1.0 %collective-permute-start.17 = (bf16[128,128]{1,0:T(8,128)(2,1)S(1)}, bf16[128,128]{1,0:T(8,128)(2,1)S(1)}, u32[]{:S(2)}, u32[]{:S(2)}) collective-permute-start(bf16[128,128]{1,0:T(8,128)(2,1)S(1)} %get-tuple-element.24), channel_id=1, source_target_pairs={{0,8},{1,9},{2,10},{3,11},{4,12},{5,13},{6,14},{7,15},{8,0},{9,1},... | collective-permute-start | bytes 98312 | tf_op jit(solution)/shard_map/ppermute | solution.py:25
  49.8 1.5 %collective-permute-done.15.after_ref.refs_1_ = bf16[128,128]{1,0:T(8,128)(2,1)S(1)} collective-permute-done((bf16[128,128]{1,0:T(8,128)(2,1)S(1)}, bf16[128,128]{1,0:T(8,128)(2,1)S(1)}, u32[]{:S(2)}, u32[]{:S(2)}) %collective-permute-start.15) | collective-permute-done | bytes 32800 | tf_op jit(solution)/shard_map/ppermute | solution.py:25
  (51 shorter events, 7.1 us)
Async XLA Ops:
  0.6 10.4 %copy-start = (bf16[2,512,128]{2,1,0:T(8,128)(2,1)S(1)}, bf16[2,512,128]{2,1,0:T(8,128)(2,1)}, u32[]{:S(2)}) copy-start(bf16[2,512,128]{2,1,0:T(8,128)(2,1)} %refs_0_.1) | copy-start | bytes 786436
  0.6 10.4 %collective-permute-start = (bf16[2,512,128]{2,1,0:T(8,128)(2,1)}, bf16[2,512,128]{2,1,0:T(8,128)(2,1)S(1)}, u32[]{:S(2)}, u32[]{:S(2)}) collective-permute-start(bf16[2,512,128]{2,1,0:T(8,128)(2,1)} %refs_0_.1), channel_id=1, source_target_pairs={{0,8},{1,9},{2,10},{3,11},{4,12},{5,13},{6,14},{7,15},{8,0},{9,1},... | collective-permute-start | bytes 786440 | tf_op jit(solution)/shard_map/ppermute | solution.py:25
  3.7 14.6 %collective-permute-start.4 = (bf16[2,512,128]{2,1,0:T(8,128)(2,1)}, bf16[2,512,128]{2,1,0:T(8,128)(2,1)S(1)}, u32[]{:S(2)}, u32[]{:S(2)}) collective-permute-start(bf16[2,512,128]{2,1,0:T(8,128)(2,1)} %refs_0_.1), channel_id=1, source_target_pairs={{0,4},{1,5},{2,6},{3,7},{4,0},{5,1},{6,2},{7,3},{8,12},{9,13},{10,... | collective-permute-start | bytes 786440 | tf_op jit(solution)/shard_map/ppermute | solution.py:25
  7.0 10.5 %copy-start.10 = (s32[64,4]{0,1:T(4,128)S(1)}, s32[64,4]{0,1:T(4,128)}, u32[]{:S(2)}) copy-start(s32[64,4]{0,1:T(4,128)} %param.16) | copy-start | bytes 3076
  7.0 10.7 %collective-permute-start.2 = (bf16[2,128,256]{2,1,0:T(8,128)(2,1)S(1)}, bf16[2,128,256]{2,1,0:T(8,128)(2,1)S(1)}, u32[]{:S(2)}, u32[]{:S(2)}) collective-permute-start(bf16[2,128,256]{2,1,0:T(8,128)(2,1)S(1)} %shard_map.113.refs_6_.refs_7_), channel_id=1, source_target_pairs={{0,8},{1,9},{2,10},{3,11},{4,12},{5,13},{6,14},{7,15},{8,0},{9,1},... | collective-permute-start | bytes 393224 | tf_op jit(solution)/shard_map/ppermute | solution.py:25
  7.5 10.8 %collective-permute-start.5 = (bf16[2,128,256]{2,1,0:T(8,128)(2,1)S(1)}, bf16[2,128,256]{2,1,0:T(8,128)(2,1)S(1)}, u32[]{:S(2)}, u32[]{:S(2)}) collective-permute-start(bf16[2,128,256]{2,1,0:T(8,128)(2,1)S(1)} %shard_map.113.refs_6_.refs_7_), channel_id=1, source_target_pairs={{0,4},{1,5},{2,6},{3,7},{4,0},{5,1},{6,2},{7,3},{8,12},{9,13},{10,... | collective-permute-start | bytes 393224 | tf_op jit(solution)/shard_map/ppermute | solution.py:25
  11.8 11.3 %collective-permute-start.6 = (bf16[2,544,128]{2,1,0:T(8,128)(2,1)S(1)}, bf16[2,544,128]{2,1,0:T(8,128)(2,1)S(1)}, u32[]{:S(2)}, u32[]{:S(2)}) collective-permute-start(bf16[2,544,128]{2,1,0:T(8,128)(2,1)S(1)} %shard_map.112.refs_2_), channel_id=1, source_target_pairs={{0,24},{1,25},{2,26},{3,27},{4,28},{5,29},{6,30},{7,31},{8,16},{9,... | collective-permute-start | bytes 835592 | tf_op jit(solution)/shard_map/ppermute | solution.py:25
  15.9 7.2 %collective-permute-start.1 = (bf16[2,512,128]{2,1,0:T(8,128)(2,1)S(1)}, bf16[2,512,128]{2,1,0:T(8,128)(2,1)S(1)}, u32[]{:S(2)}, u32[]{:S(2)}) collective-permute-start(bf16[2,512,128]{2,1,0:T(8,128)(2,1)S(1)} %collective-permute-done.after_ref.refs_5_), channel_id=1, source_target_pairs={{0,4},{1,5},{2,6},{3,7},{4,0},{5,1},{6,2},{7,3},{8,12},{9,13},{10,... | collective-permute-start | bytes 786440 | tf_op jit(solution)/shard_map/ppermute | solution.py:25
  17.7 7.5 %collective-permute-start.3 = (bf16[2,128,256]{2,1,0:T(8,128)(2,1)S(1)}, bf16[2,128,256]{2,1,0:T(8,128)(2,1)S(1)}, u32[]{:S(2)}, u32[]{:S(2)}) collective-permute-start(bf16[2,128,256]{2,1,0:T(8,128)(2,1)S(1)} %collective-permute-done.2.refs_8_.refs_9_), channel_id=1, source_target_pairs={{0,4},{1,5},{2,6},{3,7},{4,0},{5,1},{6,2},{7,3},{8,12},{9,13},{10,... | collective-permute-start | bytes 393224 | tf_op jit(solution)/shard_map/ppermute | solution.py:25
  18.4 14.7 %collective-permute-start.8 = (bf16[4,512,128]{2,1,0:T(8,128)(2,1)S(1)}, bf16[4,512,128]{2,1,0:T(8,128)(2,1)S(1)}, u32[]{:S(2)}, u32[]{:S(2)}) collective-permute-start(bf16[4,512,128]{2,1,0:T(8,128)(2,1)S(1)} %shard_map.118.refs_3_), channel_id=1, source_target_pairs={{0,1},{1,0},{2,3},{3,2},{4,5},{5,4},{6,7},{7,6},{8,9},{9,8},{10,11... | collective-permute-start | bytes 1572872 | tf_op jit(solution)/shard_map/ppermute | solution.py:25
  18.4 15.5 %collective-permute-start.9 = (bf16[4,512,128]{2,1,0:T(8,128)(2,1)S(1)}, bf16[4,512,128]{2,1,0:T(8,128)(2,1)S(1)}, u32[]{:S(2)}, u32[]{:S(2)}) collective-permute-start(bf16[4,512,128]{2,1,0:T(8,128)(2,1)S(1)} %shard_map.118.refs_3_), channel_id=1, source_target_pairs={{0,2},{1,3},{2,0},{3,1},{4,6},{5,7},{6,4},{7,5},{8,10},{9,11},{10,... | collective-permute-start | bytes 1572872 | tf_op jit(solution)/shard_map/ppermute | solution.py:25
  26.1 6.9 %copy-start.3 = (bf16[2,128,128]{2,1,0:T(8,128)(2,1)S(1)}, bf16[2,128,128]{2,1,0:T(8,128)(2,1)}, u32[]{:S(2)}) copy-start(bf16[2,128,128]{2,1,0:T(8,128)(2,1)} %amps_ref.3) | copy-start | bytes 196612
  26.1 6.9 %copy-start.5 = (bf16[2,128,128]{2,1,0:T(8,128)(2,1)S(1)}, bf16[2,128,128]{2,1,0:T(8,128)(2,1)}, u32[]{:S(2)}) copy-start(bf16[2,128,128]{2,1,0:T(8,128)(2,1)} %resp_ref.3) | copy-start | bytes 196612
  26.1 6.9 %copy-start.6 = (bf16[2,128,128]{2,1,0:T(8,128)(2,1)S(1)}, bf16[2,128,128]{2,1,0:T(8,128)(2,1)}, u32[]{:S(2)}) copy-start(bf16[2,128,128]{2,1,0:T(8,128)(2,1)} %ints_ref.1) | copy-start | bytes 196612
  26.1 6.9 %collective-permute-start.7 = (bf16[2,256,128]{2,1,0:T(8,128)(2,1)S(1)}, bf16[2,256,128]{2,1,0:T(8,128)(2,1)S(1)}, u32[]{:S(2)}, u32[]{:S(2)}) collective-permute-start(bf16[2,256,128]{2,1,0:T(8,128)(2,1)S(1)} %shard_map.117), channel_id=1, source_target_pairs={{0,24},{1,25},{2,26},{3,27},{4,28},{5,29},{6,30},{7,31},{8,16},{9,... | collective-permute-start | bytes 393224 | tf_op jit(solution)/shard_map/ppermute | solution.py:25
  28.6 8.9 %copy-start.1 = (bf16[1024,128]{1,0:T(8,128)(2,1)S(1)}, bf16[1024,128]{1,0:T(8,128)(2,1)}, u32[]{:S(2)}) copy-start(bf16[1024,128]{1,0:T(8,128)(2,1)} %param.17) | copy-start | bytes 786436
  33.9 3.6 %collective-permute-start.10 = (bf16[4,512,128]{2,1,0:T(8,128)(2,1)S(1)}, bf16[4,512,128]{2,1,0:T(8,128)(2,1)S(1)}, u32[]{:S(2)}, u32[]{:S(2)}) collective-permute-start(bf16[4,512,128]{2,1,0:T(8,128)(2,1)S(1)} %shard_map.120.refs_5_), channel_id=1, source_target_pairs={{0,1},{1,0},{2,3},{3,2},{4,5},{5,4},{6,7},{7,6},{8,9},{9,8},{10,11... | collective-permute-start | bytes 1572872 | tf_op jit(solution)/shard_map/ppermute | solution.py:25
  34.0 5.5 %collective-permute-start.11 = (bf16[2,128,128]{2,1,0:T(8,128)(2,1)S(1)}, bf16[2,128,128]{2,1,0:T(8,128)(2,1)S(1)}, u32[]{:S(2)}, u32[]{:S(2)}) collective-permute-start(bf16[2,128,128]{2,1,0:T(8,128)(2,1)S(1)} %get-tuple-element.18.after_ref.refs_7_.refs_0_), channel_id=1, source_target_pairs={{0,4},{1,5},{2,6},{3,7},{4,0},{5,1},{6,2},{7,3},{8,12},{9,13},{10,... | collective-permute-start | bytes 196616 | tf_op jit(solution)/shard_map/ppermute | solution.py:25
  35.6 4.3 %collective-permute-start.12 = (bf16[2,128,128]{2,1,0:T(8,128)(2,1)S(1)}, bf16[2,128,128]{2,1,0:T(8,128)(2,1)S(1)}, u32[]{:S(2)}, u32[]{:S(2)}) collective-permute-start(bf16[2,128,128]{2,1,0:T(8,128)(2,1)S(1)} %get-tuple-element.18.after_ref.refs_7_.refs_0_), channel_id=1, source_target_pairs={{0,2},{1,3},{2,0},{3,1},{4,6},{5,7},{6,4},{7,5},{8,10},{9,11},{10,... | collective-permute-start | bytes 196616 | tf_op jit(solution)/shard_map/ppermute | solution.py:25
  37.1 5.2 %collective-permute-start.13 = (bf16[2,128,128]{2,1,0:T(8,128)(2,1)S(1)}, bf16[2,128,128]{2,1,0:T(8,128)(2,1)S(1)}, u32[]{:S(2)}, u32[]{:S(2)}) collective-permute-start(bf16[2,128,128]{2,1,0:T(8,128)(2,1)S(1)} %get-tuple-element.18.after_ref.refs_7_.refs_0_), channel_id=1, source_target_pairs={{0,6},{1,7},{2,4},{3,5},{4,2},{5,3},{6,0},{7,1},{8,14},{9,15},{10,... | collective-permute-start | bytes 196616 | tf_op jit(solution)/shard_map/ppermute | solution.py:25
  42.3 1.6 %collective-permute-start.14 = (bf16[8,128,128]{2,1,0:T(8,128)(2,1)S(1)}, bf16[8,128,128]{2,1,0:T(8,128)(2,1)S(1)}, u32[]{:S(2)}, u32[]{:S(2)}) collective-permute-start(bf16[8,128,128]{2,1,0:T(8,128)(2,1)S(1)} %shard_map.122.refs_3_), channel_id=1, source_target_pairs={{0,1},{1,0},{2,3},{3,2},{4,5},{5,4},{6,7},{7,6},{8,9},{9,8},{10,11... | collective-permute-start | bytes 786440 | tf_op jit(solution)/shard_map/ppermute | solution.py:25
  45.4 5.9 %collective-permute-start.15 = (bf16[128,128]{1,0:T(8,128)(2,1)S(1)}, bf16[128,128]{1,0:T(8,128)(2,1)S(1)}, u32[]{:S(2)}, u32[]{:S(2)}) collective-permute-start(bf16[128,128]{1,0:T(8,128)(2,1)S(1)} %get-tuple-element.22), channel_id=1, source_target_pairs={{0,24},{1,25},{2,26},{3,27},{4,28},{5,29},{6,30},{7,31},{8,16},{9,... | collective-permute-start | bytes 98312 | tf_op jit(solution)/shard_map/ppermute | solution.py:25
  46.7 5.3 %collective-permute-start.16 = (bf16[128,128]{1,0:T(8,128)(2,1)S(1)}, bf16[128,128]{1,0:T(8,128)(2,1)S(1)}, u32[]{:S(2)}, u32[]{:S(2)}) collective-permute-start(bf16[128,128]{1,0:T(8,128)(2,1)S(1)} %get-tuple-element.23), channel_id=1, source_target_pairs={{0,16},{1,17},{2,18},{3,19},{4,20},{5,21},{6,22},{7,23},{8,24},{9,... | collective-permute-start | bytes 98312 | tf_op jit(solution)/shard_map/ppermute | solution.py:25
  48.8 3.9 %collective-permute-start.17 = (bf16[128,128]{1,0:T(8,128)(2,1)S(1)}, bf16[128,128]{1,0:T(8,128)(2,1)S(1)}, u32[]{:S(2)}, u32[]{:S(2)}) collective-permute-start(bf16[128,128]{1,0:T(8,128)(2,1)S(1)} %get-tuple-element.24), channel_id=1, source_target_pairs={{0,8},{1,9},{2,10},{3,11},{4,12},{5,13},{6,14},{7,15},{8,0},{9,1},... | collective-permute-start | bytes 98312 | tf_op jit(solution)/shard_map/ppermute | solution.py:25
  (5 other events, 17.0 us)

commit v4 on v3

--- a/solution.py
+++ b/solution.py
@@ -48,8 +48,7 @@
         copy.wait()
 
 
-def pack_kernel(blk, readers_ref, couple_ref, q_ref, after_ref, out_ref):
-    del after_ref
+def pack_kernel(blk, readers_ref, couple_ref, q_ref, out_ref):
     pairs, nfun, npno = q_ref.shape
     count = (out_ref.shape[1] - nfun) // 2
     row = lax.broadcasted_iota(jnp.int32, (count, npno), 0)
@@ -65,10 +64,10 @@
         out_ref[p, nfun + count :, :] = (c - high.astype(F32)).astype(BF16)
 
 
-def beside_kernel(*refs):
+def beside_kernel(places, *refs):
     *in_refs, _, out_ref = refs
     count = in_refs[0].shape[0]
-    for i, ref in enumerate(in_refs):
+    for i, ref in zip(places, in_refs):
         out_ref[i * count : (i + 1) * count] = ref[...]
 
 
@@ -253,9 +252,10 @@
     pack = call(
         functools.partial(pack_kernel, blk),
         sds((pairs, nfun + 2 * count, npno), BF16),
-        [SMEM, SMEM, VMEM, ANY], 1,
-        readers, couple, trans, near_q[near - 2],
-    )
+        [SMEM] * 2 + [VMEM], 1,
+        readers, couple, trans,
+    )
+    pack = call(again_kernel, sds(pack.shape, BF16), [VMEM, ANY], 0.3, pack, near_q[near - 2])
     far_pack = swap(pack, partner, 0)
     for mask in range(2, near, 2):
         near_q[mask + 1] = swap(near_q[mask], 1, 0)
@@ -297,7 +297,7 @@
         scratch=scratch,
     )
     both_q = call(
-        beside_kernel, sds((2 * pairs, nfun, npno), BF16), [VMEM] * 2 + [ANY], 0.3, trans, near_q[1], near_tz[1]
+        functools.partial(beside_kernel, range(2)), sds((2 * pairs, nfun, npno), BF16), [VMEM] * 2 + [ANY], 0.3, trans, near_q[1], near_tz[1]
     )
     core_q = swap(both_q, 0, 1)
     mats = sds((pairs, npno, npno), F32)
@@ -320,10 +320,12 @@
         where, dom, integrals.reshape(nbas // blk, blk, cols), *[narrow_q[k] for k in range(narrow)], weights,
     )
     group = [(bit, mask) for mask in range(0, narrow, 2) for bit in range(2)]
-    arrived = {key: swap(weights, *key) if any(key) else weights for key in sorted(group, reverse=True)}
+    arrived = [swap(weights, *key) if any(key) else weights for key in reversed(group)]
     near_w = call(
-        beside_kernel, sds((len(group) * pairs, npno, npno), BF16), [VMEM] * len(group) + [ANY], 0.3,
-        *[arrived[key] for key in group], moved,
+        functools.partial(beside_kernel, range(len(group) - 1, -1, -1)),
+        sds((len(group) * pairs, npno, npno), BF16),
+        [VMEM] * len(group) + [ANY], 0.3,
+        *arrived, moved,
     )
     core_w = swap(near_w, 0, 1)
     others = list(range(wide - 2, 0, -2))

time: 53.6 us -> 52.6 us (0.981)
  waiting for transfers between devices: 16.1 us -> 14.7 us
    ppermute x18, waiting for transfers between devices: 16.1 us -> 14.7 us  [swap(): return lax.ppermute(value, ('wide', 'narrow'), pairs)]
    pallas_call x14 -> x15, Pallas kernels: 11.8 us -> 11.9 us  [call(): pl.pallas_call(kernel, out_shape=out_shape, in_specs=specs, out_specs=out...]
  transfers between devices with their start and end apart: 18 -> 18, of which waited for: 9 -> 9; matrix products, arithmetic and copies ran while one was open for 1% -> 1% of each run, Pallas kernels for 18% -> 19%
where the time goes in v4:
time: 52.6 us; the launch traced here: 52.3 us
  starting transfers between devices  23 us (44%)
  waiting for transfers between devices  14.7 us (28%)
  Pallas kernels  11.9 us (23%)
  local copies, waits for them, and re-layouts  1.93 us (4%)
  between operations  0.85 us (2%)
    ppermute x18, starting transfers between devices, swap(): return lax.ppermute(value, ('wide', 'narrow'), pairs)  23 us
    ppermute x18, waiting for transfers between devices, swap(): return lax.ppermute(value, ('wide', 'narrow'), pairs)  14.7 us
    pallas_call x15, Pallas kernels, call(): pl.pallas_call(kernel, out_shape=out_shape, in_specs=specs, out_specs=out...  11.9 us
    unnamed x23, local copies, waits for them, and re-layouts  1.82 us
  transfers between devices with their start and end apart: 18, of which 9 were waited for; matrix products, arithmetic and copies ran while one was open for 1% of the time, Pallas kernels for 19%

profile of v4, /device:TPU:0, one launch (start us, length us, event | category | flops | bytes accessed | tf_op | source)
XLA Modules:
  0.0 52.3 jit_solution(6164472904242413063)
XLA Ops:
  0.6 3.1 %collective-permute-start = (bf16[2,512,128]{2,1,0:T(8,128)(2,1)}, bf16[2,512,128]{2,1,0:T(8,128)(2,1)S(1)}, u32[]{:S(2)}, u32[]{:S(2)}) collective-permute-start(bf16[2,512,128]{2,1,0:T(8,128)(2,1)} %refs_0_.1), channel_id=1, source_target_pairs={{0,8},{1,9},{2,10},{3,11},{4,12},{5,13},{6,14},{7,15},{8,0},{9,1},... | collective-permute-start | bytes 786440 | tf_op jit(solution)/shard_map/ppermute | solution.py:25
  3.7 1.5 %collective-permute-start.4 = (bf16[2,512,128]{2,1,0:T(8,128)(2,1)}, bf16[2,512,128]{2,1,0:T(8,128)(2,1)S(1)}, u32[]{:S(2)}, u32[]{:S(2)}) collective-permute-start(bf16[2,512,128]{2,1,0:T(8,128)(2,1)} %refs_0_.1), channel_id=1, source_target_pairs={{0,4},{1,5},{2,6},{3,7},{4,0},{5,1},{6,2},{7,3},{8,12},{9,13},{10,... | collective-permute-start | bytes 786440 | tf_op jit(solution)/shard_map/ppermute | solution.py:25
  5.2 0.8 %copy-done.2 = bf16[2,128,128]{2,1,0:T(8,128)(2,1)S(1)} copy-done((bf16[2,128,128]{2,1,0:T(8,128)(2,1)S(1)}, bf16[2,128,128]{2,1,0:T(8,128)(2,1)}, u32[]{:S(2)}) %copy-start.2) | copy-done | bytes 65560
  8.3 2.7 %collective-permute-done.after_ref.refs_5_ = bf16[2,512,128]{2,1,0:T(8,128)(2,1)S(1)} collective-permute-done((bf16[2,512,128]{2,1,0:T(8,128)(2,1)}, bf16[2,512,128]{2,1,0:T(8,128)(2,1)S(1)}, u32[]{:S(2)}, u32[]{:S(2)}) %collective-permute-start) | collective-permute-done | bytes 262176 | tf_op jit(solution)/shard_map/ppermute | solution.py:25
  11.1 4.1 %collective-permute-start.6 = (bf16[2,544,128]{2,1,0:T(8,128)(2,1)S(1)}, bf16[2,544,128]{2,1,0:T(8,128)(2,1)S(1)}, u32[]{:S(2)}, u32[]{:S(2)}) collective-permute-start(bf16[2,544,128]{2,1,0:T(8,128)(2,1)S(1)} %shard_map.113.refs_2_), channel_id=1, source_target_pairs={{0,24},{1,25},{2,26},{3,27},{4,28},{5,29},{6,30},{7,31},{8,16},{9,... | collective-permute-start | bytes 835592 | tf_op jit(solution)/shard_map/ppermute | solution.py:25
  15.2 1.5 %collective-permute-start.1 = (bf16[2,512,128]{2,1,0:T(8,128)(2,1)S(1)}, bf16[2,512,128]{2,1,0:T(8,128)(2,1)S(1)}, u32[]{:S(2)}, u32[]{:S(2)}) collective-permute-start(bf16[2,512,128]{2,1,0:T(8,128)(2,1)S(1)} %collective-permute-done.after_ref.refs_5_), channel_id=1, source_target_pairs={{0,4},{1,5},{2,6},{3,7},{4,0},{5,1},{6,2},{7,3},{8,12},{9,13},{10,... | collective-permute-start | bytes 786440 | tf_op jit(solution)/shard_map/ppermute | solution.py:25
  17.8 1.6 %collective-permute-start.9 = (bf16[4,512,128]{2,1,0:T(8,128)(2,1)S(1)}, bf16[4,512,128]{2,1,0:T(8,128)(2,1)S(1)}, u32[]{:S(2)}, u32[]{:S(2)}) collective-permute-start(bf16[4,512,128]{2,1,0:T(8,128)(2,1)S(1)} %shard_map.119.refs_3_), channel_id=1, source_target_pairs={{0,2},{1,3},{2,0},{3,1},{4,6},{5,7},{6,4},{7,5},{8,10},{9,11},{10,... | collective-permute-start | bytes 1572872 | tf_op jit(solution)/shard_map/ppermute | solution.py:25
  19.3 1.9 %shard_map.115.refs_5_ = f32[2,256,128]{2,1,0:T(8,128)S(1)} custom-call(s32[2]{0:T(128)S(1)} %pad_add_fusion.refs_0_, s32[256]{0:T(256)S(1)} %reshape.12.refs_1_, bf16[2,544,128]{2,1,0:T(8,128)(2,1)S(1)} %shard_map.113.refs_2_, bf16[2,512,128]{2,1,0:T(8,128)(2,1)S(1)} %copy-done, bf16[2,512,128]{2,1,0:T(8,128)(2,1)S(1)} %collective-permute-done.4.refs_4_.refs_1_, ...), custom_call_target="tpu_custom_call" | custom-call | flops 2000000000 | tf_op jit(solution)/shard_map/pallas_call | solution.py:29
  21.3 1.1 %collective-permute-done.1.refs_3_.refs_6_ = bf16[2,512,128]{2,1,0:T(8,128)(2,1)S(1)} collective-permute-done((bf16[2,512,128]{2,1,0:T(8,128)(2,1)S(1)}, bf16[2,512,128]{2,1,0:T(8,128)(2,1)S(1)}, u32[]{:S(2)}, u32[]{:S(2)}) %collective-permute-start.1) | collective-permute-done | bytes 262176 | tf_op jit(solution)/shard_map/ppermute | solution.py:25
  22.4 2.1 %shard_map.117 = (f32[2,256,128]{2,1,0:T(8,128)S(1)}, bf16[2,256,128]{2,1,0:T(8,128)(2,1)S(1)}) custom-call(s32[2]{0:T(128)S(1)} %pad_add_fusion.refs_0_, s32[256]{0:T(256)S(1)} %reshape.12.refs_1_, bf16[2,544,128]{2,1,0:T(8,128)(2,1)S(1)} %collective-permute-done.6.refs_2_.refs_1_, bf16[2,512,128]{2,1,0:T(8,128)(2,1)S(1)} %copy-done, ...), custom_call_target="tpu_custom_call" | custom-call | flops 3000000000 | tf_op jit(solution)/shard_map/pallas_call | solution.py:29
  24.5 0.9 %shard_map.118 = bf16[2,256,128]{2,1,0:T(8,128)(2,1)S(1)} custom-call(s32[2]{0:T(128)S(1)} %pad_add_fusion.refs_0_, bf16[2,544,128]{2,1,0:T(8,128)(2,1)S(1)} %collective-permute-done.6.refs_2_.refs_1_, bf16[2,256,128]{2,1,0:T(8,128)(2,1)S(1)} %get-tuple-element.14.refs_2_, f32[2,256,128]{2,1,0:T(8,128)S(1)} %get-tuple-element.15.refs_3_, ...), custom_call_target="tpu_custom_call" | custom-call | flops 1000000000 | tf_op jit(solution)/shard_map/pallas_call | solution.py:29
  25.5 1.7 %collective-permute-start.7 = (bf16[2,256,128]{2,1,0:T(8,128)(2,1)S(1)}, bf16[2,256,128]{2,1,0:T(8,128)(2,1)S(1)}, u32[]{:S(2)}, u32[]{:S(2)}) collective-permute-start(bf16[2,256,128]{2,1,0:T(8,128)(2,1)S(1)} %shard_map.118), channel_id=1, source_target_pairs={{0,24},{1,25},{2,26},{3,27},{4,28},{5,29},{6,30},{7,31},{8,16},{9,... | collective-permute-start | bytes 393224 | tf_op jit(solution)/shard_map/ppermute | solution.py:25
  27.2 1.2 %shard_map.116.own_ref = f32[2,256,128]{2,1,0:T(8,128)S(1)} custom-call(s32[2]{0:T(128)S(1)} %pad_add_fusion.refs_0_, s32[256]{0:T(256)S(1)} %reshape.12.refs_1_, bf16[2,544,128]{2,1,0:T(8,128)(2,1)S(1)} %shard_map.113.refs_2_, bf16[2,512,128]{2,1,0:T(8,128)(2,1)S(1)} %collective-permute-done.1.refs_3_.refs_6_, ...), custom_call_target="tpu_custom_call" | custom-call | flops 2000000000 | tf_op jit(solution)/shard_map/pallas_call | solution.py:29
  28.4 4.0 %collective-permute-done.7.back_ref = bf16[2,256,128]{2,1,0:T(8,128)(2,1)S(1)} collective-permute-done((bf16[2,256,128]{2,1,0:T(8,128)(2,1)S(1)}, bf16[2,256,128]{2,1,0:T(8,128)(2,1)S(1)}, u32[]{:S(2)}, u32[]{:S(2)}) %collective-permute-start.7) | collective-permute-done | bytes 131104 | tf_op jit(solution)/shard_map/ppermute | solution.py:25
  32.4 0.8 %shard_map.120 = (f32[2,128,128]{2,1,0:T(8,128)}, f32[2,128,128]{2,1,0:T(8,128)}, bf16[2,128,128]{2,1,0:T(8,128)(2,1)S(1)}) custom-call(f32[2,256,128]{2,1,0:T(8,128)S(1)} %shard_map.116.own_ref, bf16[2,256,128]{2,1,0:T(8,128)(2,1)S(1)} %collective-permute-done.7.back_ref, bf16[2,128,128]{2,1,0:T(8,128)(2,1)S(1)} %copy-done.3, ...), custom_call_target="tpu_custom_call" | custom-call | flops 1000000000 | tf_op jit(solution)/shard_map/pallas_call | solution.py:29
  33.3 2.5 %collective-permute-start.11 = (bf16[2,128,128]{2,1,0:T(8,128)(2,1)S(1)}, bf16[2,128,128]{2,1,0:T(8,128)(2,1)S(1)}, u32[]{:S(2)}, u32[]{:S(2)}) collective-permute-start(bf16[2,128,128]{2,1,0:T(8,128)(2,1)S(1)} %get-tuple-element.18.after_ref.refs_7_.refs_3_), channel_id=1, source_target_pairs={{0,6},{1,7},{2,4},{3,5},{4,2},{5,3},{6,0},{7,1},{8,14},{9,15},{10,... | collective-permute-start | bytes 196616 | tf_op jit(solution)/shard_map/ppermute | solution.py:25
  36.9 2.0 %shard_map.122 = (bf16[5,128,2048]{2,1,0:T(8,128)(2,1)S(1)}, bf16[16,128,128]{2,1,0:T(8,128)(2,1)S(1)}) custom-call(s32[2]{0:T(128)S(1)} %pad_add_fusion.refs_0_, s32[256]{0:T(256)S(1)} %reshape.12.refs_1_, bf16[8,128,128]{2,1,0:T(8,128)(2,1)S(1)} %bitcast.3, bf16[4,512,128]{2,1,0:T(8,128)(2,1)S(1)} %shard_map.119.refs_3_, ...), custom_call_target="tpu_custom_call" | custom-call | flops 1000000000 | tf_op jit(solution)/shard_map/pallas_call | solution.py:29
  38.9 1.3 %collective-permute-done.12.refs_1_ = bf16[2,128,128]{2,1,0:T(8,128)(2,1)S(1)} collective-permute-done((bf16[2,128,128]{2,1,0:T(8,128)(2,1)S(1)}, bf16[2,128,128]{2,1,0:T(8,128)(2,1)S(1)}, u32[]{:S(2)}, u32[]{:S(2)}) %collective-permute-start.12) | collective-permute-done | bytes 65568 | tf_op jit(solution)/shard_map/ppermute | solution.py:25
  40.7 1.5 %collective-permute-done.14.refs_4_ = bf16[8,128,128]{2,1,0:T(8,128)(2,1)S(1)} collective-permute-done((bf16[8,128,128]{2,1,0:T(8,128)(2,1)S(1)}, bf16[8,128,128]{2,1,0:T(8,128)(2,1)S(1)}, u32[]{:S(2)}, u32[]{:S(2)}) %collective-permute-start.14) | collective-permute-done | bytes 262176 | tf_op jit(solution)/shard_map/ppermute | solution.py:25
  42.3 1.5 %shard_map.124 = (f32[128,128]{1,0:T(8,128)S(1)}, bf16[128,128]{1,0:T(8,128)(2,1)S(1)}, bf16[128,128]{1,0:T(8,128)(2,1)S(1)}, bf16[128,128]{1,0:T(8,128)(2,1)S(1)}) custom-call(s32[2]{0:T(128)S(1)} %pad_add_fusion.refs_0_, bf16[5,128,2048]{2,1,0:T(8,128)(2,1)S(1)} %get-tuple-element.19.refs_1_, bf16[16,128,128]{2,1,0:T(8,128)(2,1)S(1)} %get-tuple-element.20.refs_4_.refs_2_, ...), custom_call_target="tpu_custom_call" | custom-call | flops 1000000000 | tf_op jit(solution)/shard_map/pallas_call | solution.py:29
  43.7 1.7 %collective-permute-start.15 = (bf16[128,128]{1,0:T(8,128)(2,1)S(1)}, bf16[128,128]{1,0:T(8,128)(2,1)S(1)}, u32[]{:S(2)}, u32[]{:S(2)}) collective-permute-start(bf16[128,128]{1,0:T(8,128)(2,1)S(1)} %get-tuple-element.22), channel_id=1, source_target_pairs={{0,24},{1,25},{2,26},{3,27},{4,28},{5,29},{6,30},{7,31},{8,16},{9,... | collective-permute-start | bytes 98312 | tf_op jit(solution)/shard_map/ppermute | solution.py:25
  45.5 2.3 %collective-permute-start.16 = (bf16[128,128]{1,0:T(8,128)(2,1)S(1)}, bf16[128,128]{1,0:T(8,128)(2,1)S(1)}, u32[]{:S(2)}, u32[]{:S(2)}) collective-permute-start(bf16[128,128]{1,0:T(8,128)(2,1)S(1)} %get-tuple-element.23), channel_id=1, source_target_pairs={{0,16},{1,17},{2,18},{3,19},{4,20},{5,21},{6,22},{7,23},{8,24},{9,... | collective-permute-start | bytes 98312 | tf_op jit(solution)/shard_map/ppermute | solution.py:25
  48.2 1.5 %collective-permute-done.15.after_ref.refs_1_ = bf16[128,128]{1,0:T(8,128)(2,1)S(1)} collective-permute-done((bf16[128,128]{1,0:T(8,128)(2,1)S(1)}, bf16[128,128]{1,0:T(8,128)(2,1)S(1)}, u32[]{:S(2)}, u32[]{:S(2)}) %collective-permute-start.15) | collective-permute-done | bytes 32800 | tf_op jit(solution)/shard_map/ppermute | solution.py:25
  49.6 1.5 %collective-permute-done.16.refs_2_ = bf16[128,128]{1,0:T(8,128)(2,1)S(1)} collective-permute-done((bf16[128,128]{1,0:T(8,128)(2,1)S(1)}, bf16[128,128]{1,0:T(8,128)(2,1)S(1)}, u32[]{:S(2)}, u32[]{:S(2)}) %collective-permute-start.16) | collective-permute-done | bytes 32800 | tf_op jit(solution)/shard_map/ppermute | solution.py:25
  (52 shorter events, 6.6 us)
Async XLA Ops:
  0.6 7.0 %copy-start = (bf16[2,512,128]{2,1,0:T(8,128)(2,1)S(1)}, bf16[2,512,128]{2,1,0:T(8,128)(2,1)}, u32[]{:S(2)}) copy-start(bf16[2,512,128]{2,1,0:T(8,128)(2,1)} %refs_0_.1) | copy-start | bytes 786436
  0.6 10.4 %collective-permute-start = (bf16[2,512,128]{2,1,0:T(8,128)(2,1)}, bf16[2,512,128]{2,1,0:T(8,128)(2,1)S(1)}, u32[]{:S(2)}, u32[]{:S(2)}) collective-permute-start(bf16[2,512,128]{2,1,0:T(8,128)(2,1)} %refs_0_.1), channel_id=1, source_target_pairs={{0,8},{1,9},{2,10},{3,11},{4,12},{5,13},{6,14},{7,15},{8,0},{9,1},... | collective-permute-start | bytes 786440 | tf_op jit(solution)/shard_map/ppermute | solution.py:25
  3.7 13.9 %collective-permute-start.4 = (bf16[2,512,128]{2,1,0:T(8,128)(2,1)}, bf16[2,512,128]{2,1,0:T(8,128)(2,1)S(1)}, u32[]{:S(2)}, u32[]{:S(2)}) collective-permute-start(bf16[2,512,128]{2,1,0:T(8,128)(2,1)} %refs_0_.1), channel_id=1, source_target_pairs={{0,4},{1,5},{2,6},{3,7},{4,0},{5,1},{6,2},{7,3},{8,12},{9,13},{10,... | collective-permute-start | bytes 786440 | tf_op jit(solution)/shard_map/ppermute | solution.py:25
  7.0 9.9 %copy-start.10 = (s32[64,4]{0,1:T(4,128)S(1)}, s32[64,4]{0,1:T(4,128)}, u32[]{:S(2)}) copy-start(s32[64,4]{0,1:T(4,128)} %param.16) | copy-start | bytes 3076
  7.0 10.1 %collective-permute-start.2 = (bf16[2,128,256]{2,1,0:T(8,128)(2,1)S(1)}, bf16[2,128,256]{2,1,0:T(8,128)(2,1)S(1)}, u32[]{:S(2)}, u32[]{:S(2)}) collective-permute-start(bf16[2,128,256]{2,1,0:T(8,128)(2,1)S(1)} %shard_map.114.refs_6_.refs_7_), channel_id=1, source_target_pairs={{0,8},{1,9},{2,10},{3,11},{4,12},{5,13},{6,14},{7,15},{8,0},{9,1},... | collective-permute-start | bytes 393224 | tf_op jit(solution)/shard_map/ppermute | solution.py:25
  7.5 10.1 %collective-permute-start.5 = (bf16[2,128,256]{2,1,0:T(8,128)(2,1)S(1)}, bf16[2,128,256]{2,1,0:T(8,128)(2,1)S(1)}, u32[]{:S(2)}, u32[]{:S(2)}) collective-permute-start(bf16[2,128,256]{2,1,0:T(8,128)(2,1)S(1)} %shard_map.114.refs_6_.refs_7_), channel_id=1, source_target_pairs={{0,4},{1,5},{2,6},{3,7},{4,0},{5,1},{6,2},{7,3},{8,12},{9,13},{10,... | collective-permute-start | bytes 393224 | tf_op jit(solution)/shard_map/ppermute | solution.py:25
  11.1 11.3 %collective-permute-start.6 = (bf16[2,544,128]{2,1,0:T(8,128)(2,1)S(1)}, bf16[2,544,128]{2,1,0:T(8,128)(2,1)S(1)}, u32[]{:S(2)}, u32[]{:S(2)}) collective-permute-start(bf16[2,544,128]{2,1,0:T(8,128)(2,1)S(1)} %shard_map.113.refs_2_), channel_id=1, source_target_pairs={{0,24},{1,25},{2,26},{3,27},{4,28},{5,29},{6,30},{7,31},{8,16},{9,... | collective-permute-start | bytes 835592 | tf_op jit(solution)/shard_map/ppermute | solution.py:25
  15.2 7.2 %collective-permute-start.1 = (bf16[2,512,128]{2,1,0:T(8,128)(2,1)S(1)}, bf16[2,512,128]{2,1,0:T(8,128)(2,1)S(1)}, u32[]{:S(2)}, u32[]{:S(2)}) collective-permute-start(bf16[2,512,128]{2,1,0:T(8,128)(2,1)S(1)} %collective-permute-done.after_ref.refs_5_), channel_id=1, source_target_pairs={{0,4},{1,5},{2,6},{3,7},{4,0},{5,1},{6,2},{7,3},{8,12},{9,13},{10,... | collective-permute-start | bytes 786440 | tf_op jit(solution)/shard_map/ppermute | solution.py:25
  17.0 7.5 %collective-permute-start.3 = (bf16[2,128,256]{2,1,0:T(8,128)(2,1)S(1)}, bf16[2,128,256]{2,1,0:T(8,128)(2,1)S(1)}, u32[]{:S(2)}, u32[]{:S(2)}) collective-permute-start(bf16[2,128,256]{2,1,0:T(8,128)(2,1)S(1)} %collective-permute-done.2.refs_8_.refs_9_), channel_id=1, source_target_pairs={{0,4},{1,5},{2,6},{3,7},{4,0},{5,1},{6,2},{7,3},{8,12},{9,13},{10,... | collective-permute-start | bytes 393224 | tf_op jit(solution)/shard_map/ppermute | solution.py:25
  17.7 14.7 %collective-permute-start.8 = (bf16[4,512,128]{2,1,0:T(8,128)(2,1)S(1)}, bf16[4,512,128]{2,1,0:T(8,128)(2,1)S(1)}, u32[]{:S(2)}, u32[]{:S(2)}) collective-permute-start(bf16[4,512,128]{2,1,0:T(8,128)(2,1)S(1)} %shard_map.119.refs_3_), channel_id=1, source_target_pairs={{0,1},{1,0},{2,3},{3,2},{4,5},{5,4},{6,7},{7,6},{8,9},{9,8},{10,11... | collective-permute-start | bytes 1572872 | tf_op jit(solution)/shard_map/ppermute | solution.py:25
  17.8 15.5 %collective-permute-start.9 = (bf16[4,512,128]{2,1,0:T(8,128)(2,1)S(1)}, bf16[4,512,128]{2,1,0:T(8,128)(2,1)S(1)}, u32[]{:S(2)}, u32[]{:S(2)}) collective-permute-start(bf16[4,512,128]{2,1,0:T(8,128)(2,1)S(1)} %shard_map.119.refs_3_), channel_id=1, source_target_pairs={{0,2},{1,3},{2,0},{3,1},{4,6},{5,7},{6,4},{7,5},{8,10},{9,11},{10,... | collective-permute-start | bytes 1572872 | tf_op jit(solution)/shard_map/ppermute | solution.py:25
  25.4 6.9 %copy-start.3 = (bf16[2,128,128]{2,1,0:T(8,128)(2,1)S(1)}, bf16[2,128,128]{2,1,0:T(8,128)(2,1)}, u32[]{:S(2)}) copy-start(bf16[2,128,128]{2,1,0:T(8,128)(2,1)} %amps_ref.3) | copy-start | bytes 196612
  25.4 6.9 %copy-start.5 = (bf16[2,128,128]{2,1,0:T(8,128)(2,1)S(1)}, bf16[2,128,128]{2,1,0:T(8,128)(2,1)}, u32[]{:S(2)}) copy-start(bf16[2,128,128]{2,1,0:T(8,128)(2,1)} %resp_ref.3) | copy-start | bytes 196612
  25.4 6.9 %copy-start.6 = (bf16[2,128,128]{2,1,0:T(8,128)(2,1)S(1)}, bf16[2,128,128]{2,1,0:T(8,128)(2,1)}, u32[]{:S(2)}) copy-start(bf16[2,128,128]{2,1,0:T(8,128)(2,1)} %ints_ref.1) | copy-start | bytes 196612
  25.5 6.9 %collective-permute-start.7 = (bf16[2,256,128]{2,1,0:T(8,128)(2,1)S(1)}, bf16[2,256,128]{2,1,0:T(8,128)(2,1)S(1)}, u32[]{:S(2)}, u32[]{:S(2)}) collective-permute-start(bf16[2,256,128]{2,1,0:T(8,128)(2,1)S(1)} %shard_map.118), channel_id=1, source_target_pairs={{0,24},{1,25},{2,26},{3,27},{4,28},{5,29},{6,30},{7,31},{8,16},{9,... | collective-permute-start | bytes 393224 | tf_op jit(solution)/shard_map/ppermute | solution.py:25
  28.3 8.6 %copy-start.1 = (bf16[1024,128]{1,0:T(8,128)(2,1)S(1)}, bf16[1024,128]{1,0:T(8,128)(2,1)}, u32[]{:S(2)}) copy-start(bf16[1024,128]{1,0:T(8,128)(2,1)} %param.17) | copy-start | bytes 786436
  33.3 3.6 %collective-permute-start.10 = (bf16[4,512,128]{2,1,0:T(8,128)(2,1)S(1)}, bf16[4,512,128]{2,1,0:T(8,128)(2,1)S(1)}, u32[]{:S(2)}, u32[]{:S(2)}) collective-permute-start(bf16[4,512,128]{2,1,0:T(8,128)(2,1)S(1)} %shard_map.121.refs_5_), channel_id=1, source_target_pairs={{0,1},{1,0},{2,3},{3,2},{4,5},{5,4},{6,7},{7,6},{8,9},{9,8},{10,11... | collective-permute-start | bytes 1572872 | tf_op jit(solution)/shard_map/ppermute | solution.py:25
  33.3 5.5 %collective-permute-start.11 = (bf16[2,128,128]{2,1,0:T(8,128)(2,1)S(1)}, bf16[2,128,128]{2,1,0:T(8,128)(2,1)S(1)}, u32[]{:S(2)}, u32[]{:S(2)}) collective-permute-start(bf16[2,128,128]{2,1,0:T(8,128)(2,1)S(1)} %get-tuple-element.18.after_ref.refs_7_.refs_3_), channel_id=1, source_target_pairs={{0,6},{1,7},{2,4},{3,5},{4,2},{5,3},{6,0},{7,1},{8,14},{9,15},{10,... | collective-permute-start | bytes 196616 | tf_op jit(solution)/shard_map/ppermute | solution.py:25
  35.9 4.3 %collective-permute-start.12 = (bf16[2,128,128]{2,1,0:T(8,128)(2,1)S(1)}, bf16[2,128,128]{2,1,0:T(8,128)(2,1)S(1)}, u32[]{:S(2)}, u32[]{:S(2)}) collective-permute-start(bf16[2,128,128]{2,1,0:T(8,128)(2,1)S(1)} %get-tuple-element.18.after_ref.refs_7_.refs_3_), channel_id=1, source_target_pairs={{0,2},{1,3},{2,0},{3,1},{4,6},{5,7},{6,4},{7,5},{8,10},{9,11},{10,... | collective-permute-start | bytes 196616 | tf_op jit(solution)/shard_map/ppermute | solution.py:25
  36.4 4.3 %collective-permute-start.13 = (bf16[2,128,128]{2,1,0:T(8,128)(2,1)S(1)}, bf16[2,128,128]{2,1,0:T(8,128)(2,1)S(1)}, u32[]{:S(2)}, u32[]{:S(2)}) collective-permute-start(bf16[2,128,128]{2,1,0:T(8,128)(2,1)S(1)} %get-tuple-element.18.after_ref.refs_7_.refs_3_), channel_id=1, source_target_pairs={{0,4},{1,5},{2,6},{3,7},{4,0},{5,1},{6,2},{7,3},{8,12},{9,13},{10,... | collective-permute-start | bytes 196616 | tf_op jit(solution)/shard_map/ppermute | solution.py:25
  40.7 1.6 %collective-permute-start.14 = (bf16[8,128,128]{2,1,0:T(8,128)(2,1)S(1)}, bf16[8,128,128]{2,1,0:T(8,128)(2,1)S(1)}, u32[]{:S(2)}, u32[]{:S(2)}) collective-permute-start(bf16[8,128,128]{2,1,0:T(8,128)(2,1)S(1)} %shard_map.123.refs_3_), channel_id=1, source_target_pairs={{0,1},{1,0},{2,3},{3,2},{4,5},{5,4},{6,7},{7,6},{8,9},{9,8},{10,11... | collective-permute-start | bytes 786440 | tf_op jit(solution)/shard_map/ppermute | solution.py:25
  43.7 5.9 %collective-permute-start.15 = (bf16[128,128]{1,0:T(8,128)(2,1)S(1)}, bf16[128,128]{1,0:T(8,128)(2,1)S(1)}, u32[]{:S(2)}, u32[]{:S(2)}) collective-permute-start(bf16[128,128]{1,0:T(8,128)(2,1)S(1)} %get-tuple-element.22), channel_id=1, source_target_pairs={{0,24},{1,25},{2,26},{3,27},{4,28},{5,29},{6,30},{7,31},{8,16},{9,... | collective-permute-start | bytes 98312 | tf_op jit(solution)/shard_map/ppermute | solution.py:25
  45.5 5.7 %collective-permute-start.16 = (bf16[128,128]{1,0:T(8,128)(2,1)S(1)}, bf16[128,128]{1,0:T(8,128)(2,1)S(1)}, u32[]{:S(2)}, u32[]{:S(2)}) collective-permute-start(bf16[128,128]{1,0:T(8,128)(2,1)S(1)} %get-tuple-element.23), channel_id=1, source_target_pairs={{0,16},{1,17},{2,18},{3,19},{4,20},{5,21},{6,22},{7,23},{8,24},{9,... | collective-permute-start | bytes 98312 | tf_op jit(solution)/shard_map/ppermute | solution.py:25
  47.8 3.9 %collective-permute-start.17 = (bf16[128,128]{1,0:T(8,128)(2,1)S(1)}, bf16[128,128]{1,0:T(8,128)(2,1)S(1)}, u32[]{:S(2)}, u32[]{:S(2)}) collective-permute-start(bf16[128,128]{1,0:T(8,128)(2,1)S(1)} %get-tuple-element.24), channel_id=1, source_target_pairs={{0,8},{1,9},{2,10},{3,11},{4,12},{5,13},{6,14},{7,15},{8,0},{9,1},... | collective-permute-start | bytes 98312 | tf_op jit(solution)/shard_map/ppermute | solution.py:25
  (5 other events, 10.1 us)

commit v5 on v4

--- a/solution.py
+++ b/solution.py
@@ -71,9 +71,8 @@
         out_ref[i * count : (i + 1) * count] = ref[...]
 
 
-def mark_kernel(after_ref, out_ref):
-    del after_ref
-    out_ref[...] = jnp.zeros_like(out_ref)
+def mark_kernel(*refs):
+    refs[-1][...] = jnp.zeros_like(refs[-1])
 
 
 def again_kernel(value_ref, after_ref, out_ref):
@@ -109,10 +108,10 @@
         sums[g] = term if sums[g] is None else sums[g] + term
 
 
-def couple_kernel(masks, ahead, blk, narrow, flip, prior, *refs):
+def couple_kernel(masks, blk, narrow, flip, prior, *refs):
     where_ref, dom_ref, pack_ref = refs[:3]
     refs = refs[3:]
-    q_refs, refs = refs[: len(masks) + len(ahead)], refs[len(masks) + len(ahead) :]
+    q_refs, refs = refs[: len(masks)], refs[len(masks) :]
     tz_refs, refs = refs[: len(masks)], refs[len(masks) :]
     prior_ref, refs = (refs[0], refs[1:]) if prior else (None, refs)
     out_ref, spread_ref, c_ref = refs[0], refs[-2], refs[-1]
@@ -127,55 +126,46 @@
                 p, a * blk : (a + 1) * blk, :
             ]
     sums = [prior_ref[g] if prior else None for g in range(pairs)]
-    for k, mask in enumerate(masks + ahead):
+    for k, mask in enumerate(masks):
         dev = where_ref[0] ^ mask
         overlaps = []
         for p in range(pairs):
             pair = (dev * narrow + where_ref[1]) * pairs + p
             left = jnp.concatenate([spread_ref[dom_ref[pair * dom_blk + b]] for b in range(dom_blk)], axis=1)
             overlaps.append(jnp.dot(left, q_refs[k][p], preferred_element_type=F32).astype(BF16))
-        if k < len(masks):
-            add_terms(sums, overlaps, tz_refs[k], c_ref, dev)
-        else:
-            for p in range(pairs):
-                refs[1][(k - len(masks)) * pairs + p] = overlaps[p]
+        add_terms(sums, overlaps, tz_refs[k], c_ref, dev)
     for g in range(pairs):
         out_ref[g] = sums[g].astype(out_ref.dtype)
 
 
-def finish_kernel(masks, *refs):
-    where_ref, pack_ref, overlap_ref, prior_ref = refs[:4]
-    tz_refs, (out_ref, c_ref) = refs[4 : 4 + len(masks)], refs[4 + len(masks) :]
-    pairs = pack_ref.shape[0]
-    load_coefficients(pack_ref, c_ref)
-    sums = [prior_ref[g] for g in range(pairs)]
-    for k, mask in enumerate(masks):
-        overlaps = [overlap_ref[k * pairs + p] for p in range(pairs)]
-        add_terms(sums, overlaps, tz_refs[k], c_ref, where_ref[0] ^ mask)
-    for g in range(pairs):
-        out_ref[g] = sums[g].astype(out_ref.dtype)
-
-
-def update_kernel(
-    own_ref, back_ref, amps_ref, resp_ref, ints_ref, energy_ref, after_ref, new_amps_ref, new_resp_ref, w_ref
-):
-    del after_ref
+def updated(p, own_ref, back_ref, amps_ref, resp_ref, ints_ref, energy_ref):
     npno = amps_ref.shape[1]
-    for p in range(amps_ref.shape[0]):
-        across = jnp.broadcast_to(energy_ref[pl.ds(p, 1), :], (npno, npno))
-        denom = across + across.T
-        amps = amps_ref[p].astype(F32)
-        resp = resp_ref[p].astype(F32)
-        coupled_t = own_ref[p, :npno] + back_ref[p, :npno].astype(F32)
-        coupled_z = own_ref[p, npno:] + back_ref[p, npno:].astype(F32)
-        new_amps = amps - 0.5 * (ints_ref[p].astype(F32) + denom * amps + coupled_t) / denom
-        new_resp = resp - 0.5 * (amps + denom * resp + coupled_z) / denom
-        new_amps_ref[p] = new_amps
-        new_resp_ref[p] = new_resp
+    across = jnp.broadcast_to(energy_ref[pl.ds(p, 1), :], (npno, npno))
+    denom = across + across.T
+    amps = amps_ref[p].astype(F32)
+    resp = resp_ref[p].astype(F32)
+    coupled_t = own_ref[p, :npno] + back_ref[p, :npno].astype(F32)
+    coupled_z = own_ref[p, npno:] + back_ref[p, npno:].astype(F32)
+    new_amps = amps - 0.5 * (ints_ref[p].astype(F32) + denom * amps + coupled_t) / denom
+    new_resp = resp - 0.5 * (amps + denom * resp + coupled_z) / denom
+    return new_amps, new_resp
+
+
+def weights_kernel(*refs):
+    w_ref = refs[-1]
+    for p in range(w_ref.shape[0]):
+        new_amps, new_resp = updated(p, *refs[:6])
         prod = lax.dot_general(
             new_amps.astype(BF16), new_resp.astype(BF16), (((1,), (1,)), ((), ())), preferred_element_type=F32
         )
         w_ref[p] = (0.5 * (prod + prod.T)).astype(BF16)
+
+
+def update_kernel(*refs):
+    new_amps_ref, new_resp_ref, done_ref = refs[-3:]
+    for p in range(new_amps_ref.shape[0]):
+        new_amps_ref[p], new_resp_ref[p] = updated(p, *refs[:6])
+    done_ref[...] = jnp.zeros_like(done_ref)
 
 
 def place_kernel(blk, narrow, pairs, *refs):
@@ -268,29 +258,22 @@
     ]
     sums = sds((pairs, 2 * npno, npno), F32)
     own = call(
-        functools.partial(couple_kernel, early, [], blk, narrow, 0, False),
+        functools.partial(couple_kernel, early, blk, narrow, 0, False),
         sums,
         [SMEM] * 2 + [VMEM] * (1 + 2 * len(early)), 2,
         where, dom, pack, *[near_q[m] for m in early], *[near_tz[m] for m in early],
         scratch=scratch,
     )
-    far, overlap = call(
-        functools.partial(couple_kernel, early, late, blk, narrow, partner, False),
-        (sums, sds((len(late) * pairs, pairs * npno, npno), BF16)),
-        [SMEM] * 2 + [VMEM] * (1 + 2 * len(early) + len(late)), 3,
-        where, dom, far_pack, *[near_q[m] for m in early + late], *[near_tz[m] for m in early],
+    far = call(
+        functools.partial(couple_kernel, early + late, blk, narrow, partner, False),
+        sds(sums.shape, BF16),
+        [SMEM] * 2 + [VMEM] * (1 + 2 * near), 4,
+        where, dom, far_pack, *[near_q[m] for m in early + late], *[near_tz[m] for m in early + late],
         scratch=scratch,
-    )
-    far = call(
-        functools.partial(finish_kernel, late),
-        sds(sums.shape, BF16),
-        [SMEM] + [VMEM] * (3 + len(late)), 1,
-        where, far_pack, overlap, far, *[near_tz[m] for m in late],
-        scratch=scratch[1:],
     )
     back = swap(far, partner, 0)
     own_late = call(
-        functools.partial(couple_kernel, late, [], blk, narrow, 0, True),
+        functools.partial(couple_kernel, late, blk, narrow, 0, True),
         sums,
         [SMEM] * 2 + [VMEM] * (2 + 2 * len(late)), 2,
         where, dom, pack, *[near_q[m] for m in late], *[near_tz[m] for m in late], own,
@@ -301,12 +284,10 @@
     )
     core_q = swap(both_q, 0, 1)
     mats = sds((pairs, npno, npno), F32)
-    new_amps, new_resp, weights = call(
-        update_kernel,
-        (mats, mats, sds((pairs, npno, npno), BF16)),
-        [VMEM] * 6 + [ANY], 1,
-        own_late, back, amps, resp, ints, energies, core_q,
-    )
+    state = (own_late, back, amps, resp, ints, energies)
+    weights = call(weights_kernel, sds((pairs, npno, npno), BF16), [VMEM] * 6 + [ANY], 1, *state, core_q)
+    token = sds((8, 128), F32)
+    new_amps, new_resp, done = call(update_kernel, (mats, mats, token), [VMEM] * 6 + [ANY], 1, *state, weights)
     narrow_q = {0: both_q, 1: core_q}
     for mask in range(2, narrow, 2):
         arrived = swap(both_q, 0, mask)
@@ -338,7 +319,7 @@
         scratch=[pltpu.VMEM((near,) + block, F32)],
     )
     received = [swap(share, mask, 0) for mask, share in zip(others, shares[1:])]
-    mark = call(mark_kernel, sds((8, 128), F32), [ANY], 0.1, received[0])
+    mark = call(mark_kernel, token, [ANY] * 2, 0.1, received[0], done)
     response = call(
         sum_kernel, sds(block, F32), [VMEM] * (1 + len(others)) + [ANY], 0.1, shares[0], *received, mark
     )

time: 52.6 us -> 51.8 us (0.985)
  transfers between devices with their start and end apart: 18 -> 18, of which waited for: 9 -> 9; matrix products, arithmetic and copies ran while one was open for 1% -> 1% of each run, Pallas kernels for 19% -> 18%
where the time goes in v5:
time: 51.8 us; the launch traced here: 51.6 us
  starting transfers between devices  23 us (44%)
  waiting for transfers between devices  14.2 us (27%)
  Pallas kernels  11.6 us (22%)
  local copies, waits for them, and re-layouts  1.93 us (4%)
  between operations  0.86 us (2%)
    ppermute x18, starting transfers between devices, swap(): return lax.ppermute(value, ('wide', 'narrow'), pairs)  23 us
    ppermute x18, waiting for transfers between devices, swap(): return lax.ppermute(value, ('wide', 'narrow'), pairs)  14.2 us
    pallas_call x15, Pallas kernels, call(): pl.pallas_call(kernel, out_shape=out_shape, in_specs=specs, out_specs=out...  11.6 us
    unnamed x23, local copies, waits for them, and re-layouts  1.82 us
  transfers between devices with their start and end apart: 18, of which 9 were waited for; matrix products, arithmetic and copies ran while one was open for 1% of the time, Pallas kernels for 18%

profile of v5, /device:TPU:0, one launch (start us, length us, event | category | flops | bytes accessed | tf_op | source)
XLA Modules:
  0.0 51.6 jit_solution(8374983601446481221)
XLA Ops:
  0.6 3.1 %collective-permute-start = (bf16[2,512,128]{2,1,0:T(8,128)(2,1)}, bf16[2,512,128]{2,1,0:T(8,128)(2,1)S(1)}, u32[]{:S(2)}, u32[]{:S(2)}) collective-permute-start(bf16[2,512,128]{2,1,0:T(8,128)(2,1)} %refs_0_.1), channel_id=1, source_target_pairs={{0,8},{1,9},{2,10},{3,11},{4,12},{5,13},{6,14},{7,15},{8,0},{9,1},... | collective-permute-start | bytes 786440 | tf_op jit(solution)/shard_map/ppermute | solution.py:25
  3.7 1.5 %collective-permute-start.4 = (bf16[2,512,128]{2,1,0:T(8,128)(2,1)}, bf16[2,512,128]{2,1,0:T(8,128)(2,1)S(1)}, u32[]{:S(2)}, u32[]{:S(2)}) collective-permute-start(bf16[2,512,128]{2,1,0:T(8,128)(2,1)} %refs_0_.1), channel_id=1, source_target_pairs={{0,4},{1,5},{2,6},{3,7},{4,0},{5,1},{6,2},{7,3},{8,12},{9,13},{10,... | collective-permute-start | bytes 786440 | tf_op jit(solution)/shard_map/ppermute | solution.py:25
  5.2 0.8 %copy-done.2 = bf16[2,128,128]{2,1,0:T(8,128)(2,1)S(1)} copy-done((bf16[2,128,128]{2,1,0:T(8,128)(2,1)S(1)}, bf16[2,128,128]{2,1,0:T(8,128)(2,1)}, u32[]{:S(2)}) %copy-start.2) | copy-done | bytes 65560
  6.1 0.8 %copy-done.4 = bf16[2,128,128]{2,1,0:T(8,128)(2,1)S(1)} copy-done((bf16[2,128,128]{2,1,0:T(8,128)(2,1)S(1)}, bf16[2,128,128]{2,1,0:T(8,128)(2,1)}, u32[]{:S(2)}) %copy-start.4) | copy-done | bytes 65560
  8.3 2.7 %collective-permute-done.after_ref.refs_5_ = bf16[2,512,128]{2,1,0:T(8,128)(2,1)S(1)} collective-permute-done((bf16[2,512,128]{2,1,0:T(8,128)(2,1)}, bf16[2,512,128]{2,1,0:T(8,128)(2,1)S(1)}, u32[]{:S(2)}, u32[]{:S(2)}) %collective-permute-start) | collective-permute-done | bytes 262176 | tf_op jit(solution)/shard_map/ppermute | solution.py:25
  11.1 4.1 %collective-permute-start.6 = (bf16[2,544,128]{2,1,0:T(8,128)(2,1)S(1)}, bf16[2,544,128]{2,1,0:T(8,128)(2,1)S(1)}, u32[]{:S(2)}, u32[]{:S(2)}) collective-permute-start(bf16[2,544,128]{2,1,0:T(8,128)(2,1)S(1)} %shard_map.113.refs_2_), channel_id=1, source_target_pairs={{0,24},{1,25},{2,26},{3,27},{4,28},{5,29},{6,30},{7,31},{8,16},{9,... | collective-permute-start | bytes 835592 | tf_op jit(solution)/shard_map/ppermute | solution.py:25
  15.2 1.5 %collective-permute-start.1 = (bf16[2,512,128]{2,1,0:T(8,128)(2,1)S(1)}, bf16[2,512,128]{2,1,0:T(8,128)(2,1)S(1)}, u32[]{:S(2)}, u32[]{:S(2)}) collective-permute-start(bf16[2,512,128]{2,1,0:T(8,128)(2,1)S(1)} %collective-permute-done.after_ref.refs_5_), channel_id=1, source_target_pairs={{0,4},{1,5},{2,6},{3,7},{4,0},{5,1},{6,2},{7,3},{8,12},{9,13},{10,... | collective-permute-start | bytes 786440 | tf_op jit(solution)/shard_map/ppermute | solution.py:25
  17.8 1.6 %collective-permute-start.9 = (bf16[4,512,128]{2,1,0:T(8,128)(2,1)S(1)}, bf16[4,512,128]{2,1,0:T(8,128)(2,1)S(1)}, u32[]{:S(2)}, u32[]{:S(2)}) collective-permute-start(bf16[4,512,128]{2,1,0:T(8,128)(2,1)S(1)} %shard_map.118.refs_3_), channel_id=1, source_target_pairs={{0,2},{1,3},{2,0},{3,1},{4,6},{5,7},{6,4},{7,5},{8,10},{9,11},{10,... | collective-permute-start | bytes 1572872 | tf_op jit(solution)/shard_map/ppermute | solution.py:25
  19.3 1.9 %shard_map.115.refs_5_ = f32[2,256,128]{2,1,0:T(8,128)S(1)} custom-call(s32[2]{0:T(128)S(1)} %pad_add_fusion.refs_0_, s32[256]{0:T(256)S(1)} %reshape.12.refs_1_, bf16[2,544,128]{2,1,0:T(8,128)(2,1)S(1)} %shard_map.113.refs_2_, bf16[2,512,128]{2,1,0:T(8,128)(2,1)S(1)} %copy-done, bf16[2,512,128]{2,1,0:T(8,128)(2,1)S(1)} %collective-permute-done.4.refs_4_.refs_1_, ...), custom_call_target="tpu_custom_call" | custom-call | flops 2000000000 | tf_op jit(solution)/shard_map/pallas_call | solution.py:29
  21.3 2.5 %collective-permute-done.3.refs_4_.refs_10_ = bf16[2,128,256]{2,1,0:T(8,128)(2,1)S(1)} collective-permute-done((bf16[2,128,256]{2,1,0:T(8,128)(2,1)S(1)}, bf16[2,128,256]{2,1,0:T(8,128)(2,1)S(1)}, u32[]{:S(2)}, u32[]{:S(2)}) %collective-permute-start.3) | collective-permute-done | bytes 131104 | tf_op jit(solution)/shard_map/ppermute | solution.py:25
  23.8 2.4 %shard_map.117 = bf16[2,256,128]{2,1,0:T(8,128)(2,1)S(1)} custom-call(s32[2]{0:T(128)S(1)} %pad_add_fusion.refs_0_, s32[256]{0:T(256)S(1)} %reshape.12.refs_1_, bf16[2,544,128]{2,1,0:T(8,128)(2,1)S(1)} %collective-permute-done.6.refs_2_, bf16[2,512,128]{2,1,0:T(8,128)(2,1)S(1)} %copy-done, bf16[2,512,128]{2,1,0:T(8,128)(2,1)S(1)} %collective-permute-done.4.refs_4_.refs_1_, ...), custom_call_target="tpu_custom_call" | custom-call | flops 4000000000 | tf_op jit(solution)/shard_map/pallas_call | solution.py:29
  26.2 1.7 %collective-permute-start.7 = (bf16[2,256,128]{2,1,0:T(8,128)(2,1)S(1)}, bf16[2,256,128]{2,1,0:T(8,128)(2,1)S(1)}, u32[]{:S(2)}, u32[]{:S(2)}) collective-permute-start(bf16[2,256,128]{2,1,0:T(8,128)(2,1)S(1)} %shard_map.117), channel_id=1, source_target_pairs={{0,24},{1,25},{2,26},{3,27},{4,28},{5,29},{6,30},{7,31},{8,16},{9,... | collective-permute-start | bytes 393224 | tf_op jit(solution)/shard_map/ppermute | solution.py:25
  27.9 1.2 %shard_map.116.refs_0_ = f32[2,256,128]{2,1,0:T(8,128)S(1)} custom-call(s32[2]{0:T(128)S(1)} %pad_add_fusion.refs_0_, s32[256]{0:T(256)S(1)} %reshape.12.refs_1_, bf16[2,544,128]{2,1,0:T(8,128)(2,1)S(1)} %shard_map.113.refs_2_, bf16[2,512,128]{2,1,0:T(8,128)(2,1)S(1)} %collective-permute-done.1.refs_3_.refs_6_, ...), custom_call_target="tpu_custom_call" | custom-call | flops 2000000000 | tf_op jit(solution)/shard_map/pallas_call | solution.py:29
  29.1 4.1 %collective-permute-done.7.refs_1_ = bf16[2,256,128]{2,1,0:T(8,128)(2,1)S(1)} collective-permute-done((bf16[2,256,128]{2,1,0:T(8,128)(2,1)S(1)}, bf16[2,256,128]{2,1,0:T(8,128)(2,1)S(1)}, u32[]{:S(2)}, u32[]{:S(2)}) %collective-permute-start.7) | collective-permute-done | bytes 131104 | tf_op jit(solution)/shard_map/ppermute | solution.py:25
  33.7 2.5 %collective-permute-start.11 = (bf16[2,128,128]{2,1,0:T(8,128)(2,1)S(1)}, bf16[2,128,128]{2,1,0:T(8,128)(2,1)S(1)}, u32[]{:S(2)}, u32[]{:S(2)}) collective-permute-start(bf16[2,128,128]{2,1,0:T(8,128)(2,1)S(1)} %shard_map.119.refs_6_.after_ref.refs_7_.refs_3_), channel_id=1, source_target_pairs={{0,6},{1,7},{2,4},{3,5},{4,2},{5,3},{6,0},{7,1},{8,14},{9,15},{10,... | collective-permute-start | bytes 196616 | tf_op jit(solution)/shard_map/ppermute | solution.py:25
  37.3 2.0 %shard_map.122 = (bf16[5,128,2048]{2,1,0:T(8,128)(2,1)S(1)}, bf16[16,128,128]{2,1,0:T(8,128)(2,1)S(1)}) custom-call(s32[2]{0:T(128)S(1)} %pad_add_fusion.refs_0_, s32[256]{0:T(256)S(1)} %reshape.12.refs_1_, bf16[8,128,128]{2,1,0:T(8,128)(2,1)S(1)} %bitcast.3, bf16[4,512,128]{2,1,0:T(8,128)(2,1)S(1)} %shard_map.118.refs_3_, ...), custom_call_target="tpu_custom_call" | custom-call | flops 1000000000 | tf_op jit(solution)/shard_map/pallas_call | solution.py:29
  39.2 1.3 %collective-permute-done.12.refs_1_ = bf16[2,128,128]{2,1,0:T(8,128)(2,1)S(1)} collective-permute-done((bf16[2,128,128]{2,1,0:T(8,128)(2,1)S(1)}, bf16[2,128,128]{2,1,0:T(8,128)(2,1)S(1)}, u32[]{:S(2)}, u32[]{:S(2)}) %collective-permute-start.12) | collective-permute-done | bytes 65568 | tf_op jit(solution)/shard_map/ppermute | solution.py:25
  41.1 1.5 %collective-permute-done.14.refs_4_ = bf16[8,128,128]{2,1,0:T(8,128)(2,1)S(1)} collective-permute-done((bf16[8,128,128]{2,1,0:T(8,128)(2,1)S(1)}, bf16[8,128,128]{2,1,0:T(8,128)(2,1)S(1)}, u32[]{:S(2)}, u32[]{:S(2)}) %collective-permute-start.14) | collective-permute-done | bytes 262176 | tf_op jit(solution)/shard_map/ppermute | solution.py:25
  42.6 1.5 %shard_map.124 = (f32[128,128]{1,0:T(8,128)S(1)}, bf16[128,128]{1,0:T(8,128)(2,1)S(1)}, bf16[128,128]{1,0:T(8,128)(2,1)S(1)}, bf16[128,128]{1,0:T(8,128)(2,1)S(1)}) custom-call(s32[2]{0:T(128)S(1)} %pad_add_fusion.refs_0_, bf16[5,128,2048]{2,1,0:T(8,128)(2,1)S(1)} %get-tuple-element.14.refs_1_, bf16[16,128,128]{2,1,0:T(8,128)(2,1)S(1)} %get-tuple-element.15.refs_4_.refs_2_, ...), custom_call_target="tpu_custom_call" | custom-call | flops 1000000000 | tf_op jit(solution)/shard_map/pallas_call | solution.py:29
  44.1 1.7 %collective-permute-start.15 = (bf16[128,128]{1,0:T(8,128)(2,1)S(1)}, bf16[128,128]{1,0:T(8,128)(2,1)S(1)}, u32[]{:S(2)}, u32[]{:S(2)}) collective-permute-start(bf16[128,128]{1,0:T(8,128)(2,1)S(1)} %get-tuple-element.17), channel_id=1, source_target_pairs={{0,24},{1,25},{2,26},{3,27},{4,28},{5,29},{6,30},{7,31},{8,16},{9,... | collective-permute-start | bytes 98312 | tf_op jit(solution)/shard_map/ppermute | solution.py:25
  45.8 1.1 %collective-permute-start.16 = (bf16[128,128]{1,0:T(8,128)(2,1)S(1)}, bf16[128,128]{1,0:T(8,128)(2,1)S(1)}, u32[]{:S(2)}, u32[]{:S(2)}) collective-permute-start(bf16[128,128]{1,0:T(8,128)(2,1)S(1)} %get-tuple-element.18), channel_id=1, source_target_pairs={{0,16},{1,17},{2,18},{3,19},{4,20},{5,21},{6,22},{7,23},{8,24},{9,... | collective-permute-start | bytes 98312 | tf_op jit(solution)/shard_map/ppermute | solution.py:25
  46.9 1.7 %collective-permute-start.17 = (bf16[128,128]{1,0:T(8,128)(2,1)S(1)}, bf16[128,128]{1,0:T(8,128)(2,1)S(1)}, u32[]{:S(2)}, u32[]{:S(2)}) collective-permute-start(bf16[128,128]{1,0:T(8,128)(2,1)S(1)} %get-tuple-element.19), channel_id=1, source_target_pairs={{0,8},{1,9},{2,10},{3,11},{4,12},{5,13},{6,14},{7,15},{8,0},{9,1},... | collective-permute-start | bytes 98312 | tf_op jit(solution)/shard_map/ppermute | solution.py:25
  48.6 0.8 %shard_map.120 = (f32[2,128,128]{2,1,0:T(8,128)}, f32[2,128,128]{2,1,0:T(8,128)}, f32[8,128]{1,0:T(8,128)S(1)}) custom-call(f32[2,256,128]{2,1,0:T(8,128)S(1)} %shard_map.116.refs_0_, bf16[2,256,128]{2,1,0:T(8,128)(2,1)S(1)} %collective-permute-done.7.refs_1_, bf16[2,128,128]{2,1,0:T(8,128)(2,1)S(1)} %copy-done.3, bf16[2,128,128]{2,1,0:T(8,128)(2,1)S(1)} %copy-done.5, ...), custom_call_target="tpu_custom_call" | custom-call | flops 1000000000 | tf_op jit(solution)/shard_map/pallas_call | solution.py:29
  49.4 0.8 %collective-permute-done.15.refs_0_.refs_1_ = bf16[128,128]{1,0:T(8,128)(2,1)S(1)} collective-permute-done((bf16[128,128]{1,0:T(8,128)(2,1)S(1)}, bf16[128,128]{1,0:T(8,128)(2,1)S(1)}, u32[]{:S(2)}, u32[]{:S(2)}) %collective-permute-start.15) | collective-permute-done | bytes 32800 | tf_op jit(solution)/shard_map/ppermute | solution.py:25
  (52 shorter events, 5.9 us)
Async XLA Ops:
  0.6 7.0 %copy-start = (bf16[2,512,128]{2,1,0:T(8,128)(2,1)S(1)}, bf16[2,512,128]{2,1,0:T(8,128)(2,1)}, u32[]{:S(2)}) copy-start(bf16[2,512,128]{2,1,0:T(8,128)(2,1)} %refs_0_.1) | copy-start | bytes 786436
  0.6 10.4 %collective-permute-start = (bf16[2,512,128]{2,1,0:T(8,128)(2,1)}, bf16[2,512,128]{2,1,0:T(8,128)(2,1)S(1)}, u32[]{:S(2)}, u32[]{:S(2)}) collective-permute-start(bf16[2,512,128]{2,1,0:T(8,128)(2,1)} %refs_0_.1), channel_id=1, source_target_pairs={{0,8},{1,9},{2,10},{3,11},{4,12},{5,13},{6,14},{7,15},{8,0},{9,1},... | collective-permute-start | bytes 786440 | tf_op jit(solution)/shard_map/ppermute | solution.py:25
  3.7 13.9 %collective-permute-start.4 = (bf16[2,512,128]{2,1,0:T(8,128)(2,1)}, bf16[2,512,128]{2,1,0:T(8,128)(2,1)S(1)}, u32[]{:S(2)}, u32[]{:S(2)}) collective-permute-start(bf16[2,512,128]{2,1,0:T(8,128)(2,1)} %refs_0_.1), channel_id=1, source_target_pairs={{0,4},{1,5},{2,6},{3,7},{4,0},{5,1},{6,2},{7,3},{8,12},{9,13},{10,... | collective-permute-start | bytes 786440 | tf_op jit(solution)/shard_map/ppermute | solution.py:25
  7.0 9.9 %copy-start.10 = (s32[64,4]{0,1:T(4,128)S(1)}, s32[64,4]{0,1:T(4,128)}, u32[]{:S(2)}) copy-start(s32[64,4]{0,1:T(4,128)} %param.16) | copy-start | bytes 3076
  7.0 10.1 %collective-permute-start.2 = (bf16[2,128,256]{2,1,0:T(8,128)(2,1)S(1)}, bf16[2,128,256]{2,1,0:T(8,128)(2,1)S(1)}, u32[]{:S(2)}, u32[]{:S(2)}) collective-permute-start(bf16[2,128,256]{2,1,0:T(8,128)(2,1)S(1)} %shard_map.114.refs_6_.refs_7_), channel_id=1, source_target_pairs={{0,8},{1,9},{2,10},{3,11},{4,12},{5,13},{6,14},{7,15},{8,0},{9,1},... | collective-permute-start | bytes 393224 | tf_op jit(solution)/shard_map/ppermute | solution.py:25
  7.5 10.1 %collective-permute-start.5 = (bf16[2,128,256]{2,1,0:T(8,128)(2,1)S(1)}, bf16[2,128,256]{2,1,0:T(8,128)(2,1)S(1)}, u32[]{:S(2)}, u32[]{:S(2)}) collective-permute-start(bf16[2,128,256]{2,1,0:T(8,128)(2,1)S(1)} %shard_map.114.refs_6_.refs_7_), channel_id=1, source_target_pairs={{0,4},{1,5},{2,6},{3,7},{4,0},{5,1},{6,2},{7,3},{8,12},{9,13},{10,... | collective-permute-start | bytes 393224 | tf_op jit(solution)/shard_map/ppermute | solution.py:25
  11.1 12.7 %collective-permute-start.6 = (bf16[2,544,128]{2,1,0:T(8,128)(2,1)S(1)}, bf16[2,544,128]{2,1,0:T(8,128)(2,1)S(1)}, u32[]{:S(2)}, u32[]{:S(2)}) collective-permute-start(bf16[2,544,128]{2,1,0:T(8,128)(2,1)S(1)} %shard_map.113.refs_2_), channel_id=1, source_target_pairs={{0,24},{1,25},{2,26},{3,27},{4,28},{5,29},{6,30},{7,31},{8,16},{9,... | collective-permute-start | bytes 835592 | tf_op jit(solution)/shard_map/ppermute | solution.py:25
  15.2 8.6 %collective-permute-start.1 = (bf16[2,512,128]{2,1,0:T(8,128)(2,1)S(1)}, bf16[2,512,128]{2,1,0:T(8,128)(2,1)S(1)}, u32[]{:S(2)}, u32[]{:S(2)}) collective-permute-start(bf16[2,512,128]{2,1,0:T(8,128)(2,1)S(1)} %collective-permute-done.after_ref.refs_5_), channel_id=1, source_target_pairs={{0,4},{1,5},{2,6},{3,7},{4,0},{5,1},{6,2},{7,3},{8,12},{9,13},{10,... | collective-permute-start | bytes 786440 | tf_op jit(solution)/shard_map/ppermute | solution.py:25
  17.0 6.8 %collective-permute-start.3 = (bf16[2,128,256]{2,1,0:T(8,128)(2,1)S(1)}, bf16[2,128,256]{2,1,0:T(8,128)(2,1)S(1)}, u32[]{:S(2)}, u32[]{:S(2)}) collective-permute-start(bf16[2,128,256]{2,1,0:T(8,128)(2,1)S(1)} %collective-permute-done.2.refs_8_.refs_9_), channel_id=1, source_target_pairs={{0,4},{1,5},{2,6},{3,7},{4,0},{5,1},{6,2},{7,3},{8,12},{9,13},{10,... | collective-permute-start | bytes 393224 | tf_op jit(solution)/shard_map/ppermute | solution.py:25
  17.7 15.5 %collective-permute-start.8 = (bf16[4,512,128]{2,1,0:T(8,128)(2,1)S(1)}, bf16[4,512,128]{2,1,0:T(8,128)(2,1)S(1)}, u32[]{:S(2)}, u32[]{:S(2)}) collective-permute-start(bf16[4,512,128]{2,1,0:T(8,128)(2,1)S(1)} %shard_map.118.refs_3_), channel_id=1, source_target_pairs={{0,1},{1,0},{2,3},{3,2},{4,5},{5,4},{6,7},{7,6},{8,9},{9,8},{10,11... | collective-permute-start | bytes 1572872 | tf_op jit(solution)/shard_map/ppermute | solution.py:25
  17.8 15.8 %collective-permute-start.9 = (bf16[4,512,128]{2,1,0:T(8,128)(2,1)S(1)}, bf16[4,512,128]{2,1,0:T(8,128)(2,1)S(1)}, u32[]{:S(2)}, u32[]{:S(2)}) collective-permute-start(bf16[4,512,128]{2,1,0:T(8,128)(2,1)S(1)} %shard_map.118.refs_3_), channel_id=1, source_target_pairs={{0,2},{1,3},{2,0},{3,1},{4,6},{5,7},{6,4},{7,5},{8,10},{9,11},{10,... | collective-permute-start | bytes 1572872 | tf_op jit(solution)/shard_map/ppermute | solution.py:25
  26.2 7.0 %copy-start.3 = (bf16[2,128,128]{2,1,0:T(8,128)(2,1)S(1)}, bf16[2,128,128]{2,1,0:T(8,128)(2,1)}, u32[]{:S(2)}) copy-start(bf16[2,128,128]{2,1,0:T(8,128)(2,1)} %refs_2_.3) | copy-start | bytes 196612
  26.2 7.0 %copy-start.5 = (bf16[2,128,128]{2,1,0:T(8,128)(2,1)S(1)}, bf16[2,128,128]{2,1,0:T(8,128)(2,1)}, u32[]{:S(2)}) copy-start(bf16[2,128,128]{2,1,0:T(8,128)(2,1)} %refs_3_.7) | copy-start | bytes 196612
  26.2 7.0 %copy-start.6 = (bf16[2,128,128]{2,1,0:T(8,128)(2,1)S(1)}, bf16[2,128,128]{2,1,0:T(8,128)(2,1)}, u32[]{:S(2)}) copy-start(bf16[2,128,128]{2,1,0:T(8,128)(2,1)} %refs_4_.3) | copy-start | bytes 196612
  26.2 6.9 %collective-permute-start.7 = (bf16[2,256,128]{2,1,0:T(8,128)(2,1)S(1)}, bf16[2,256,128]{2,1,0:T(8,128)(2,1)S(1)}, u32[]{:S(2)}, u32[]{:S(2)}) collective-permute-start(bf16[2,256,128]{2,1,0:T(8,128)(2,1)S(1)} %shard_map.117), channel_id=1, source_target_pairs={{0,24},{1,25},{2,26},{3,27},{4,28},{5,29},{6,30},{7,31},{8,16},{9,... | collective-permute-start | bytes 393224 | tf_op jit(solution)/shard_map/ppermute | solution.py:25
  29.1 8.2 %copy-start.1 = (bf16[1024,128]{1,0:T(8,128)(2,1)S(1)}, bf16[1024,128]{1,0:T(8,128)(2,1)}, u32[]{:S(2)}) copy-start(bf16[1024,128]{1,0:T(8,128)(2,1)} %param.17) | copy-start | bytes 786436
  33.6 3.6 %collective-permute-start.10 = (bf16[4,512,128]{2,1,0:T(8,128)(2,1)S(1)}, bf16[4,512,128]{2,1,0:T(8,128)(2,1)S(1)}, u32[]{:S(2)}, u32[]{:S(2)}) collective-permute-start(bf16[4,512,128]{2,1,0:T(8,128)(2,1)S(1)} %shard_map.121.refs_5_), channel_id=1, source_target_pairs={{0,1},{1,0},{2,3},{3,2},{4,5},{5,4},{6,7},{7,6},{8,9},{9,8},{10,11... | collective-permute-start | bytes 1572872 | tf_op jit(solution)/shard_map/ppermute | solution.py:25
  33.7 5.5 %collective-permute-start.11 = (bf16[2,128,128]{2,1,0:T(8,128)(2,1)S(1)}, bf16[2,128,128]{2,1,0:T(8,128)(2,1)S(1)}, u32[]{:S(2)}, u32[]{:S(2)}) collective-permute-start(bf16[2,128,128]{2,1,0:T(8,128)(2,1)S(1)} %shard_map.119.refs_6_.after_ref.refs_7_.refs_3_), channel_id=1, source_target_pairs={{0,6},{1,7},{2,4},{3,5},{4,2},{5,3},{6,0},{7,1},{8,14},{9,15},{10,... | collective-permute-start | bytes 196616 | tf_op jit(solution)/shard_map/ppermute | solution.py:25
  36.2 4.3 %collective-permute-start.12 = (bf16[2,128,128]{2,1,0:T(8,128)(2,1)S(1)}, bf16[2,128,128]{2,1,0:T(8,128)(2,1)S(1)}, u32[]{:S(2)}, u32[]{:S(2)}) collective-permute-start(bf16[2,128,128]{2,1,0:T(8,128)(2,1)S(1)} %shard_map.119.refs_6_.after_ref.refs_7_.refs_3_), channel_id=1, source_target_pairs={{0,2},{1,3},{2,0},{3,1},{4,6},{5,7},{6,4},{7,5},{8,10},{9,11},{10,... | collective-permute-start | bytes 196616 | tf_op jit(solution)/shard_map/ppermute | solution.py:25
  36.7 4.3 %collective-permute-start.13 = (bf16[2,128,128]{2,1,0:T(8,128)(2,1)S(1)}, bf16[2,128,128]{2,1,0:T(8,128)(2,1)S(1)}, u32[]{:S(2)}, u32[]{:S(2)}) collective-permute-start(bf16[2,128,128]{2,1,0:T(8,128)(2,1)S(1)} %shard_map.119.refs_6_.after_ref.refs_7_.refs_3_), channel_id=1, source_target_pairs={{0,4},{1,5},{2,6},{3,7},{4,0},{5,1},{6,2},{7,3},{8,12},{9,13},{10,... | collective-permute-start | bytes 196616 | tf_op jit(solution)/shard_map/ppermute | solution.py:25
  41.0 1.6 %collective-permute-start.14 = (bf16[8,128,128]{2,1,0:T(8,128)(2,1)S(1)}, bf16[8,128,128]{2,1,0:T(8,128)(2,1)S(1)}, u32[]{:S(2)}, u32[]{:S(2)}) collective-permute-start(bf16[8,128,128]{2,1,0:T(8,128)(2,1)S(1)} %shard_map.123.refs_3_), channel_id=1, source_target_pairs={{0,1},{1,0},{2,3},{3,2},{4,5},{5,4},{6,7},{7,6},{8,9},{9,8},{10,11... | collective-permute-start | bytes 786440 | tf_op jit(solution)/shard_map/ppermute | solution.py:25
  44.1 6.1 %collective-permute-start.15 = (bf16[128,128]{1,0:T(8,128)(2,1)S(1)}, bf16[128,128]{1,0:T(8,128)(2,1)S(1)}, u32[]{:S(2)}, u32[]{:S(2)}) collective-permute-start(bf16[128,128]{1,0:T(8,128)(2,1)S(1)} %get-tuple-element.17), channel_id=1, source_target_pairs={{0,24},{1,25},{2,26},{3,27},{4,28},{5,29},{6,30},{7,31},{8,16},{9,... | collective-permute-start | bytes 98312 | tf_op jit(solution)/shard_map/ppermute | solution.py:25
  45.8 4.8 %collective-permute-start.16 = (bf16[128,128]{1,0:T(8,128)(2,1)S(1)}, bf16[128,128]{1,0:T(8,128)(2,1)S(1)}, u32[]{:S(2)}, u32[]{:S(2)}) collective-permute-start(bf16[128,128]{1,0:T(8,128)(2,1)S(1)} %get-tuple-element.18), channel_id=1, source_target_pairs={{0,16},{1,17},{2,18},{3,19},{4,20},{5,21},{6,22},{7,23},{8,24},{9,... | collective-permute-start | bytes 98312 | tf_op jit(solution)/shard_map/ppermute | solution.py:25
  46.9 4.1 %collective-permute-start.17 = (bf16[128,128]{1,0:T(8,128)(2,1)S(1)}, bf16[128,128]{1,0:T(8,128)(2,1)S(1)}, u32[]{:S(2)}, u32[]{:S(2)}) collective-permute-start(bf16[128,128]{1,0:T(8,128)(2,1)S(1)} %get-tuple-element.19), channel_id=1, source_target_pairs={{0,8},{1,9},{2,10},{3,11},{4,12},{5,13},{6,14},{7,15},{8,0},{9,1},... | collective-permute-start | bytes 98312 | tf_op jit(solution)/shard_map/ppermute | solution.py:25
  (5 other events, 10.2 us)

commit v6 on v5

--- a/solution.py
+++ b/solution.py
@@ -153,12 +153,20 @@
 
 def weights_kernel(*refs):
     w_ref = refs[-1]
-    for p in range(w_ref.shape[0]):
-        new_amps, new_resp = updated(p, *refs[:6])
-        prod = lax.dot_general(
-            new_amps.astype(BF16), new_resp.astype(BF16), (((1,), (1,)), ((), ())), preferred_element_type=F32
-        )
-        w_ref[p] = (0.5 * (prod + prod.T)).astype(BF16)
+    npno = w_ref.shape[2]
+    row = lax.broadcasted_iota(jnp.int32, (npno, npno), 0)
+    col = lax.broadcasted_iota(jnp.int32, (npno, npno), 1)
+    for at in range(w_ref.shape[0]):
+        both = []
+        for p in (2 * at, 2 * at + 1):
+            new_amps, new_resp = updated(p, *refs[:6])
+            prod = lax.dot_general(
+                new_amps.astype(BF16), new_resp.astype(BF16), (((1,), (1,)), ((), ())), preferred_element_type=F32
+            )
+            both.append(0.5 * (prod + prod.T))
+        w_ref[at, :npno, :] = jnp.where(row <= col, both[0], both[1]).astype(BF16)
+        diagonal = jnp.sum(jnp.where(row == col, both[1], 0.0), axis=0, keepdims=True)
+        w_ref[at, npno:, :] = jnp.broadcast_to(diagonal, (w_ref.shape[1] - npno, npno)).astype(BF16)
 
 
 def update_kernel(*refs):
@@ -184,7 +192,8 @@
                 f = dom_ref[pair * dom_blk + a]
                 for j in range(blk // rows):
                     dev = f * (blk // rows) + j
-                    at = jnp.where((dev ^ where_ref[0]) & 1, trash, dev // 2)
+                    apart = dev ^ where_ref[0]
+                    at = jnp.where(apart & 1, trash, apart // 2)
                     start = a * blk + j * rows
                     full_ref[at, :, slot * npno : (slot + 1) * npno] = q_refs[k][i, start : start + rows, :]
                 blocks.append(ints_ref[f])
@@ -193,22 +202,43 @@
             ).astype(BF16)
 
 
+def unpacked(ref, at):
+    npno = ref.shape[2]
+    row = lax.broadcasted_iota(jnp.int32, (npno, npno), 0)
+    col = lax.broadcasted_iota(jnp.int32, (npno, npno), 1)
+    mixed = ref[at, :npno, :]
+    upper, lower = mixed.astype(F32), mixed.T.astype(F32)
+    diagonal = jnp.broadcast_to(ref[at, npno:, :].astype(F32)[:1], (npno, npno))
+    first = jnp.where(row <= col, upper, lower)
+    second = jnp.where(row == col, diagonal, jnp.where(row > col, upper, lower))
+    return first.astype(BF16), second.astype(BF16)
+
+
+def half_response(narrow, odd, full_ref, moved_ref, w_ref, total):
+    both, npno = moved_ref.shape[0] // narrow, moved_ref.shape[1]
+    devs, rows = full_ref.shape[0] - 1, full_ref.shape[1]
+    for k in range(odd, narrow, 2):
+        parts = []
+        for at in range(k // 2 * both // 2, (k // 2 + 1) * both // 2):
+            for w in unpacked(w_ref, at):
+                moved = moved_ref[k * both + len(parts)]
+                parts.append(jnp.dot(w, moved, preferred_element_type=F32).astype(BF16))
+        left = full_ref[:devs, :, k * both * npno : (k + 1) * both * npno].reshape(devs * rows, both * npno)
+        term = jnp.dot(left, jnp.concatenate(parts, axis=0), preferred_element_type=F32)
+        total = term if total is None else total + term
+    return total
+
+
+def near_kernel(narrow, full_ref, moved_ref, w_ref, out_ref):
+    out_ref[...] = half_response(narrow, 0, full_ref, moved_ref, w_ref, None).reshape(out_ref.shape)
+
+
 def response_kernel(others, narrow, *refs):
-    where_ref, full_ref, moved_ref, near_w_ref, core_w_ref = refs[:5]
-    out_refs, sum_ref = refs[5:-1], refs[-1]
-    slots = moved_ref.shape[0]
-    both = slots // narrow
-    parts = []
-    for slot in range(slots):
-        k, i = slot // both, slot % both
-        w = (core_w_ref if k % 2 else near_w_ref)[k // 2 * both + i]
-        parts.append(jnp.dot(w, moved_ref[slot], preferred_element_type=F32).astype(BF16))
-    right = jnp.concatenate(parts, axis=0)
-    devs, rows, depth = sum_ref.shape[0], full_ref.shape[1], full_ref.shape[2]
-    total = jnp.dot(full_ref[:devs].reshape(devs * rows, depth), right, preferred_element_type=F32)
-    sum_ref[...] = total.reshape(sum_ref.shape)
-    for mask, out_ref in zip([0] + others, out_refs):
-        out_ref[...] = sum_ref[(where_ref[0] ^ mask) // 2].astype(out_ref.dtype)
+    full_ref, moved_ref, near_ref, w_ref = refs[:4]
+    devs, rows, cols = near_ref.shape
+    total = half_response(narrow, 1, full_ref, moved_ref, w_ref, near_ref[...].reshape(devs * rows, cols))
+    for mask, out_ref in zip([0] + others, refs[4:]):
+        out_ref[...] = total[mask // 2 * rows : (mask // 2 + 1) * rows].astype(out_ref.dtype)
 
 
 def sum_kernel(*refs):
@@ -285,7 +315,7 @@
     core_q = swap(both_q, 0, 1)
     mats = sds((pairs, npno, npno), F32)
     state = (own_late, back, amps, resp, ints, energies)
-    weights = call(weights_kernel, sds((pairs, npno, npno), BF16), [VMEM] * 6 + [ANY], 1, *state, core_q)
+    weights = call(weights_kernel, sds((pairs // 2, npno + 16, npno), BF16), [VMEM] * 6 + [ANY], 1, *state, core_q)
     token = sds((8, 128), F32)
     new_amps, new_resp, done = call(update_kernel, (mats, mats, token), [VMEM] * 6 + [ANY], 1, *state, weights)
     narrow_q = {0: both_q, 1: core_q}
@@ -304,19 +334,22 @@
     arrived = [swap(weights, *key) if any(key) else weights for key in reversed(group)]
     near_w = call(
         functools.partial(beside_kernel, range(len(group) - 1, -1, -1)),
-        sds((len(group) * pairs, npno, npno), BF16),
+        sds((len(group) * pairs // 2, npno + 16, npno), BF16),
         [VMEM] * len(group) + [ANY], 0.3,
         *arrived, moved,
     )
     core_w = swap(near_w, 0, 1)
+    near_part = call(
+        functools.partial(near_kernel, narrow), sds((near, nbas // wide, cols), F32), [VMEM] * 3, 0.5,
+        full, moved, near_w,
+    )
     others = list(range(wide - 2, 0, -2))
     block = (nbas // wide, cols)
     shares = call(
         functools.partial(response_kernel, others, narrow),
         (sds(block, F32),) + (sds(block, BF16),) * len(others),
-        [SMEM] + [VMEM] * 4, 1,
-        where, full, moved, near_w, core_w,
-        scratch=[pltpu.VMEM((near,) + block, F32)],
+        [VMEM] * 4, 1,
+        full, moved, near_part, core_w,
     )
     received = [swap(share, mask, 0) for mask, share in zip(others, shares[1:])]
     mark = call(mark_kernel, token, [ANY] * 2, 0.1, received[0], done)

time: 51.8 us -> 50.9 us (0.983)
  waiting for transfers between devices: 14.2 us -> 13 us
    ppermute x18, waiting for transfers between devices: 14.2 us -> 13 us  [swap(): return lax.ppermute(value, ('wide', 'narrow'), pairs)]
    pallas_call x15 -> x16, Pallas kernels: 11.6 us -> 11.8 us  [call(): pl.pallas_call(kernel, out_shape=out_shape, in_specs=specs, out_specs=out...]
  transfers between devices with their start and end apart: 18 -> 18, of which waited for: 9 -> 9; matrix products, arithmetic and copies ran while one was open for 1% -> 1% of each run, Pallas kernels for 18% -> 20%
where the time goes in v6:
time: 50.9 us; the launch traced here: 50.7 us
  starting transfers between devices  23 us (45%)
  waiting for transfers between devices  13 us (26%)
  Pallas kernels  11.8 us (23%)
  local copies, waits for them, and re-layouts  1.93 us (4%)
  between operations  0.86 us (2%)
    ppermute x18, starting transfers between devices, swap(): return lax.ppermute(value, ('wide', 'narrow'), pairs)  23 us
    ppermute x18, waiting for transfers between devices, swap(): return lax.ppermute(value, ('wide', 'narrow'), pairs)  13 us
    pallas_call x16, Pallas kernels, call(): pl.pallas_call(kernel, out_shape=out_shape, in_specs=specs, out_specs=out...  11.8 us
    unnamed x23, local copies, waits for them, and re-layouts  1.82 us
  transfers between devices with their start and end apart: 18, of which 9 were waited for; matrix products, arithmetic and copies ran while one was open for 1% of the time, Pallas kernels for 20%

profile of v6, /device:TPU:0, one launch (start us, length us, event | category | flops | bytes accessed | tf_op | source)
XLA Modules:
  0.0 50.7 jit_solution(16119837334224484638)
XLA Ops:
  0.6 3.1 %collective-permute-start = (bf16[2,512,128]{2,1,0:T(8,128)(2,1)}, bf16[2,512,128]{2,1,0:T(8,128)(2,1)S(1)}, u32[]{:S(2)}, u32[]{:S(2)}) collective-permute-start(bf16[2,512,128]{2,1,0:T(8,128)(2,1)} %refs_0_.1), channel_id=1, source_target_pairs={{0,8},{1,9},{2,10},{3,11},{4,12},{5,13},{6,14},{7,15},{8,0},{9,1},... | collective-permute-start | bytes 786440 | tf_op jit(solution)/shard_map/ppermute | solution.py:25
  3.7 1.5 %collective-permute-start.4 = (bf16[2,512,128]{2,1,0:T(8,128)(2,1)}, bf16[2,512,128]{2,1,0:T(8,128)(2,1)S(1)}, u32[]{:S(2)}, u32[]{:S(2)}) collective-permute-start(bf16[2,512,128]{2,1,0:T(8,128)(2,1)} %refs_0_.1), channel_id=1, source_target_pairs={{0,4},{1,5},{2,6},{3,7},{4,0},{5,1},{6,2},{7,3},{8,12},{9,13},{10,... | collective-permute-start | bytes 786440 | tf_op jit(solution)/shard_map/ppermute | solution.py:25
  5.2 0.8 %copy-done.2 = bf16[2,128,128]{2,1,0:T(8,128)(2,1)S(1)} copy-done((bf16[2,128,128]{2,1,0:T(8,128)(2,1)S(1)}, bf16[2,128,128]{2,1,0:T(8,128)(2,1)}, u32[]{:S(2)}) %copy-start.2) | copy-done | bytes 65560
  6.1 0.8 %copy-done.4 = bf16[2,128,128]{2,1,0:T(8,128)(2,1)S(1)} copy-done((bf16[2,128,128]{2,1,0:T(8,128)(2,1)S(1)}, bf16[2,128,128]{2,1,0:T(8,128)(2,1)}, u32[]{:S(2)}) %copy-start.4) | copy-done | bytes 65560
  8.3 2.7 %collective-permute-done.after_ref.refs_5_ = bf16[2,512,128]{2,1,0:T(8,128)(2,1)S(1)} collective-permute-done((bf16[2,512,128]{2,1,0:T(8,128)(2,1)}, bf16[2,512,128]{2,1,0:T(8,128)(2,1)S(1)}, u32[]{:S(2)}, u32[]{:S(2)}) %collective-permute-start) | collective-permute-done | bytes 262176 | tf_op jit(solution)/shard_map/ppermute | solution.py:25
  11.1 4.1 %collective-permute-start.6 = (bf16[2,544,128]{2,1,0:T(8,128)(2,1)S(1)}, bf16[2,544,128]{2,1,0:T(8,128)(2,1)S(1)}, u32[]{:S(2)}, u32[]{:S(2)}) collective-permute-start(bf16[2,544,128]{2,1,0:T(8,128)(2,1)S(1)} %shard_map.113.refs_2_), channel_id=1, source_target_pairs={{0,24},{1,25},{2,26},{3,27},{4,28},{5,29},{6,30},{7,31},{8,16},{9,... | collective-permute-start | bytes 835592 | tf_op jit(solution)/shard_map/ppermute | solution.py:25
  15.2 1.5 %collective-permute-start.1 = (bf16[2,512,128]{2,1,0:T(8,128)(2,1)S(1)}, bf16[2,512,128]{2,1,0:T(8,128)(2,1)S(1)}, u32[]{:S(2)}, u32[]{:S(2)}) collective-permute-start(bf16[2,512,128]{2,1,0:T(8,128)(2,1)S(1)} %collective-permute-done.after_ref.refs_5_), channel_id=1, source_target_pairs={{0,4},{1,5},{2,6},{3,7},{4,0},{5,1},{6,2},{7,3},{8,12},{9,13},{10,... | collective-permute-start | bytes 786440 | tf_op jit(solution)/shard_map/ppermute | solution.py:25
  17.8 1.6 %collective-permute-start.9 = (bf16[4,512,128]{2,1,0:T(8,128)(2,1)S(1)}, bf16[4,512,128]{2,1,0:T(8,128)(2,1)S(1)}, u32[]{:S(2)}, u32[]{:S(2)}) collective-permute-start(bf16[4,512,128]{2,1,0:T(8,128)(2,1)S(1)} %shard_map.118.refs_3_), channel_id=1, source_target_pairs={{0,2},{1,3},{2,0},{3,1},{4,6},{5,7},{6,4},{7,5},{8,10},{9,11},{10,... | collective-permute-start | bytes 1572872 | tf_op jit(solution)/shard_map/ppermute | solution.py:25
  19.3 1.9 %shard_map.115.refs_5_ = f32[2,256,128]{2,1,0:T(8,128)S(1)} custom-call(s32[2]{0:T(128)S(1)} %pad_add_fusion.refs_0_, s32[256]{0:T(256)S(1)} %reshape.12.refs_1_, bf16[2,544,128]{2,1,0:T(8,128)(2,1)S(1)} %shard_map.113.refs_2_, bf16[2,512,128]{2,1,0:T(8,128)(2,1)S(1)} %copy-done, bf16[2,512,128]{2,1,0:T(8,128)(2,1)S(1)} %collective-permute-done.4.refs_4_.refs_1_, ...), custom_call_target="tpu_custom_call" | custom-call | flops 2000000000 | tf_op jit(solution)/shard_map/pallas_call | solution.py:29
  21.3 2.5 %collective-permute-done.3.refs_4_.refs_10_ = bf16[2,128,256]{2,1,0:T(8,128)(2,1)S(1)} collective-permute-done((bf16[2,128,256]{2,1,0:T(8,128)(2,1)S(1)}, bf16[2,128,256]{2,1,0:T(8,128)(2,1)S(1)}, u32[]{:S(2)}, u32[]{:S(2)}) %collective-permute-start.3) | collective-permute-done | bytes 131104 | tf_op jit(solution)/shard_map/ppermute | solution.py:25
  23.8 2.4 %shard_map.117 = bf16[2,256,128]{2,1,0:T(8,128)(2,1)S(1)} custom-call(s32[2]{0:T(128)S(1)} %pad_add_fusion.refs_0_, s32[256]{0:T(256)S(1)} %reshape.12.refs_1_, bf16[2,544,128]{2,1,0:T(8,128)(2,1)S(1)} %collective-permute-done.6.refs_2_, bf16[2,512,128]{2,1,0:T(8,128)(2,1)S(1)} %copy-done, bf16[2,512,128]{2,1,0:T(8,128)(2,1)S(1)} %collective-permute-done.4.refs_4_.refs_1_, ...), custom_call_target="tpu_custom_call" | custom-call | flops 4000000000 | tf_op jit(solution)/shard_map/pallas_call | solution.py:29
  26.2 1.7 %collective-permute-start.7 = (bf16[2,256,128]{2,1,0:T(8,128)(2,1)S(1)}, bf16[2,256,128]{2,1,0:T(8,128)(2,1)S(1)}, u32[]{:S(2)}, u32[]{:S(2)}) collective-permute-start(bf16[2,256,128]{2,1,0:T(8,128)(2,1)S(1)} %shard_map.117), channel_id=1, source_target_pairs={{0,24},{1,25},{2,26},{3,27},{4,28},{5,29},{6,30},{7,31},{8,16},{9,... | collective-permute-start | bytes 393224 | tf_op jit(solution)/shard_map/ppermute | solution.py:25
  27.9 1.2 %shard_map.116.refs_0_ = f32[2,256,128]{2,1,0:T(8,128)S(1)} custom-call(s32[2]{0:T(128)S(1)} %pad_add_fusion.refs_0_, s32[256]{0:T(256)S(1)} %reshape.12.refs_1_, bf16[2,544,128]{2,1,0:T(8,128)(2,1)S(1)} %shard_map.113.refs_2_, bf16[2,512,128]{2,1,0:T(8,128)(2,1)S(1)} %collective-permute-done.1.refs_3_.refs_6_, ...), custom_call_target="tpu_custom_call" | custom-call | flops 2000000000 | tf_op jit(solution)/shard_map/pallas_call | solution.py:29
  29.1 4.1 %collective-permute-done.7.refs_1_ = bf16[2,256,128]{2,1,0:T(8,128)(2,1)S(1)} collective-permute-done((bf16[2,256,128]{2,1,0:T(8,128)(2,1)S(1)}, bf16[2,256,128]{2,1,0:T(8,128)(2,1)S(1)}, u32[]{:S(2)}, u32[]{:S(2)}) %collective-permute-start.7) | collective-permute-done | bytes 131104 | tf_op jit(solution)/shard_map/ppermute | solution.py:25
  33.7 2.5 %collective-permute-start.11 = (bf16[1,144,128]{2,1,0:T(8,128)(2,1)S(1)}, bf16[1,144,128]{2,1,0:T(8,128)(2,1)S(1)}, u32[]{:S(2)}, u32[]{:S(2)}) collective-permute-start(bf16[1,144,128]{2,1,0:T(8,128)(2,1)S(1)} %shard_map.119.refs_6_.after_ref.refs_7_.refs_3_), channel_id=1, source_target_pairs={{0,6},{1,7},{2,4},{3,5},{4,2},{5,3},{6,0},{7,1},{8,14},{9,15},{10,... | collective-permute-start | bytes 110600 | tf_op jit(solution)/shard_map/ppermute | solution.py:25
  37.3 1.9 %shard_map.122 = (bf16[5,128,2048]{2,1,0:T(8,128)(2,1)S(1)}, bf16[16,128,128]{2,1,0:T(8,128)(2,1)S(1)}) custom-call(s32[2]{0:T(128)S(1)} %pad_add_fusion.refs_0_, s32[256]{0:T(256)S(1)} %reshape.12.refs_1_, bf16[8,128,128]{2,1,0:T(8,128)(2,1)S(1)} %bitcast.3, bf16[4,512,128]{2,1,0:T(8,128)(2,1)S(1)} %shard_map.118.refs_3_, ...), custom_call_target="tpu_custom_call" | custom-call | flops 1000000000 | tf_op jit(solution)/shard_map/pallas_call | solution.py:29
  39.2 0.9 %collective-permute-done.12.refs_1_ = bf16[1,144,128]{2,1,0:T(8,128)(2,1)S(1)} collective-permute-done((bf16[1,144,128]{2,1,0:T(8,128)(2,1)S(1)}, bf16[1,144,128]{2,1,0:T(8,128)(2,1)S(1)}, u32[]{:S(2)}, u32[]{:S(2)}) %collective-permute-start.12) | collective-permute-done | bytes 36896 | tf_op jit(solution)/shard_map/ppermute | solution.py:25
  40.8 0.7 %shard_map.124.refs_2_ = f32[4,128,128]{2,1,0:T(8,128)S(1)} custom-call(bf16[5,128,2048]{2,1,0:T(8,128)(2,1)S(1)} %get-tuple-element.14.full_ref.refs_0_, bf16[16,128,128]{2,1,0:T(8,128)(2,1)S(1)} %get-tuple-element.15.refs_4_.moved_ref.refs_1_, bf16[4,144,128]{2,1,0:T(8,128)(2,1)S(1)} %shard_map.123.w_ref), custom_call_target="tpu_custom_call" | custom-call | flops 500000000 | tf_op jit(solution)/shard_map/pallas_call | solution.py:29
  42.2 1.0 %shard_map.125 = (f32[128,128]{1,0:T(8,128)S(1)}, bf16[128,128]{1,0:T(8,128)(2,1)S(1)}, bf16[128,128]{1,0:T(8,128)(2,1)S(1)}, bf16[128,128]{1,0:T(8,128)(2,1)S(1)}) custom-call(bf16[5,128,2048]{2,1,0:T(8,128)(2,1)S(1)} %get-tuple-element.14.full_ref.refs_0_, bf16[16,128,128]{2,1,0:T(8,128)(2,1)S(1)} %get-tuple-element.15.refs_4_.moved_ref.refs_1_, ...), custom_call_target="tpu_custom_call" | custom-call | flops 1000000000 | tf_op jit(solution)/shard_map/pallas_call | solution.py:29
  43.2 1.7 %collective-permute-start.15 = (bf16[128,128]{1,0:T(8,128)(2,1)S(1)}, bf16[128,128]{1,0:T(8,128)(2,1)S(1)}, u32[]{:S(2)}, u32[]{:S(2)}) collective-permute-start(bf16[128,128]{1,0:T(8,128)(2,1)S(1)} %get-tuple-element.17), channel_id=1, source_target_pairs={{0,24},{1,25},{2,26},{3,27},{4,28},{5,29},{6,30},{7,31},{8,16},{9,... | collective-permute-start | bytes 98312 | tf_op jit(solution)/shard_map/ppermute | solution.py:25
  44.8 1.1 %collective-permute-start.16 = (bf16[128,128]{1,0:T(8,128)(2,1)S(1)}, bf16[128,128]{1,0:T(8,128)(2,1)S(1)}, u32[]{:S(2)}, u32[]{:S(2)}) collective-permute-start(bf16[128,128]{1,0:T(8,128)(2,1)S(1)} %get-tuple-element.18), channel_id=1, source_target_pairs={{0,16},{1,17},{2,18},{3,19},{4,20},{5,21},{6,22},{7,23},{8,24},{9,... | collective-permute-start | bytes 98312 | tf_op jit(solution)/shard_map/ppermute | solution.py:25
  46.0 1.7 %collective-permute-start.17 = (bf16[128,128]{1,0:T(8,128)(2,1)S(1)}, bf16[128,128]{1,0:T(8,128)(2,1)S(1)}, u32[]{:S(2)}, u32[]{:S(2)}) collective-permute-start(bf16[128,128]{1,0:T(8,128)(2,1)S(1)} %get-tuple-element.19), channel_id=1, source_target_pairs={{0,8},{1,9},{2,10},{3,11},{4,12},{5,13},{6,14},{7,15},{8,0},{9,1},... | collective-permute-start | bytes 98312 | tf_op jit(solution)/shard_map/ppermute | solution.py:25
  47.6 0.9 %shard_map.120 = (f32[2,128,128]{2,1,0:T(8,128)}, f32[2,128,128]{2,1,0:T(8,128)}, f32[8,128]{1,0:T(8,128)S(1)}) custom-call(f32[2,256,128]{2,1,0:T(8,128)S(1)} %shard_map.116.refs_0_, bf16[2,256,128]{2,1,0:T(8,128)(2,1)S(1)} %collective-permute-done.7.refs_1_, bf16[2,128,128]{2,1,0:T(8,128)(2,1)S(1)} %copy-done.3, bf16[2,128,128]{2,1,0:T(8,128)(2,1)S(1)} %copy-done.5, ...), custom_call_target="tpu_custom_call" | custom-call | flops 1000000000 | tf_op jit(solution)/shard_map/pallas_call | solution.py:29
  48.5 0.8 %collective-permute-done.15.refs_0_.refs_1_ = bf16[128,128]{1,0:T(8,128)(2,1)S(1)} collective-permute-done((bf16[128,128]{1,0:T(8,128)(2,1)S(1)}, bf16[128,128]{1,0:T(8,128)(2,1)S(1)}, u32[]{:S(2)}, u32[]{:S(2)}) %collective-permute-start.15) | collective-permute-done | bytes 32800 | tf_op jit(solution)/shard_map/ppermute | solution.py:25
  (53 shorter events, 6.6 us)
Async XLA Ops:
  0.6 7.0 %copy-start = (bf16[2,512,128]{2,1,0:T(8,128)(2,1)S(1)}, bf16[2,512,128]{2,1,0:T(8,128)(2,1)}, u32[]{:S(2)}) copy-start(bf16[2,512,128]{2,1,0:T(8,128)(2,1)} %refs_0_.1) | copy-start | bytes 786436
  0.6 10.4 %collective-permute-start = (bf16[2,512,128]{2,1,0:T(8,128)(2,1)}, bf16[2,512,128]{2,1,0:T(8,128)(2,1)S(1)}, u32[]{:S(2)}, u32[]{:S(2)}) collective-permute-start(bf16[2,512,128]{2,1,0:T(8,128)(2,1)} %refs_0_.1), channel_id=1, source_target_pairs={{0,8},{1,9},{2,10},{3,11},{4,12},{5,13},{6,14},{7,15},{8,0},{9,1},... | collective-permute-start | bytes 786440 | tf_op jit(solution)/shard_map/ppermute | solution.py:25
  3.7 13.9 %collective-permute-start.4 = (bf16[2,512,128]{2,1,0:T(8,128)(2,1)}, bf16[2,512,128]{2,1,0:T(8,128)(2,1)S(1)}, u32[]{:S(2)}, u32[]{:S(2)}) collective-permute-start(bf16[2,512,128]{2,1,0:T(8,128)(2,1)} %refs_0_.1), channel_id=1, source_target_pairs={{0,4},{1,5},{2,6},{3,7},{4,0},{5,1},{6,2},{7,3},{8,12},{9,13},{10,... | collective-permute-start | bytes 786440 | tf_op jit(solution)/shard_map/ppermute | solution.py:25
  7.0 9.9 %copy-start.10 = (s32[64,4]{0,1:T(4,128)S(1)}, s32[64,4]{0,1:T(4,128)}, u32[]{:S(2)}) copy-start(s32[64,4]{0,1:T(4,128)} %param.16) | copy-start | bytes 3076
  7.0 10.1 %collective-permute-start.2 = (bf16[2,128,256]{2,1,0:T(8,128)(2,1)S(1)}, bf16[2,128,256]{2,1,0:T(8,128)(2,1)S(1)}, u32[]{:S(2)}, u32[]{:S(2)}) collective-permute-start(bf16[2,128,256]{2,1,0:T(8,128)(2,1)S(1)} %shard_map.114.refs_6_.refs_7_), channel_id=1, source_target_pairs={{0,8},{1,9},{2,10},{3,11},{4,12},{5,13},{6,14},{7,15},{8,0},{9,1},... | collective-permute-start | bytes 393224 | tf_op jit(solution)/shard_map/ppermute | solution.py:25
  7.5 10.1 %collective-permute-start.5 = (bf16[2,128,256]{2,1,0:T(8,128)(2,1)S(1)}, bf16[2,128,256]{2,1,0:T(8,128)(2,1)S(1)}, u32[]{:S(2)}, u32[]{:S(2)}) collective-permute-start(bf16[2,128,256]{2,1,0:T(8,128)(2,1)S(1)} %shard_map.114.refs_6_.refs_7_), channel_id=1, source_target_pairs={{0,4},{1,5},{2,6},{3,7},{4,0},{5,1},{6,2},{7,3},{8,12},{9,13},{10,... | collective-permute-start | bytes 393224 | tf_op jit(solution)/shard_map/ppermute | solution.py:25
  11.1 12.7 %collective-permute-start.6 = (bf16[2,544,128]{2,1,0:T(8,128)(2,1)S(1)}, bf16[2,544,128]{2,1,0:T(8,128)(2,1)S(1)}, u32[]{:S(2)}, u32[]{:S(2)}) collective-permute-start(bf16[2,544,128]{2,1,0:T(8,128)(2,1)S(1)} %shard_map.113.refs_2_), channel_id=1, source_target_pairs={{0,24},{1,25},{2,26},{3,27},{4,28},{5,29},{6,30},{7,31},{8,16},{9,... | collective-permute-start | bytes 835592 | tf_op jit(solution)/shard_map/ppermute | solution.py:25
  15.2 8.6 %collective-permute-start.1 = (bf16[2,512,128]{2,1,0:T(8,128)(2,1)S(1)}, bf16[2,512,128]{2,1,0:T(8,128)(2,1)S(1)}, u32[]{:S(2)}, u32[]{:S(2)}) collective-permute-start(bf16[2,512,128]{2,1,0:T(8,128)(2,1)S(1)} %collective-permute-done.after_ref.refs_5_), channel_id=1, source_target_pairs={{0,4},{1,5},{2,6},{3,7},{4,0},{5,1},{6,2},{7,3},{8,12},{9,13},{10,... | collective-permute-start | bytes 786440 | tf_op jit(solution)/shard_map/ppermute | solution.py:25
  17.0 6.8 %collective-permute-start.3 = (bf16[2,128,256]{2,1,0:T(8,128)(2,1)S(1)}, bf16[2,128,256]{2,1,0:T(8,128)(2,1)S(1)}, u32[]{:S(2)}, u32[]{:S(2)}) collective-permute-start(bf16[2,128,256]{2,1,0:T(8,128)(2,1)S(1)} %collective-permute-done.2.refs_8_.refs_9_), channel_id=1, source_target_pairs={{0,4},{1,5},{2,6},{3,7},{4,0},{5,1},{6,2},{7,3},{8,12},{9,13},{10,... | collective-permute-start | bytes 393224 | tf_op jit(solution)/shard_map/ppermute | solution.py:25
  17.7 15.5 %collective-permute-start.8 = (bf16[4,512,128]{2,1,0:T(8,128)(2,1)S(1)}, bf16[4,512,128]{2,1,0:T(8,128)(2,1)S(1)}, u32[]{:S(2)}, u32[]{:S(2)}) collective-permute-start(bf16[4,512,128]{2,1,0:T(8,128)(2,1)S(1)} %shard_map.118.refs_3_), channel_id=1, source_target_pairs={{0,1},{1,0},{2,3},{3,2},{4,5},{5,4},{6,7},{7,6},{8,9},{9,8},{10,11... | collective-permute-start | bytes 1572872 | tf_op jit(solution)/shard_map/ppermute | solution.py:25
  17.8 15.8 %collective-permute-start.9 = (bf16[4,512,128]{2,1,0:T(8,128)(2,1)S(1)}, bf16[4,512,128]{2,1,0:T(8,128)(2,1)S(1)}, u32[]{:S(2)}, u32[]{:S(2)}) collective-permute-start(bf16[4,512,128]{2,1,0:T(8,128)(2,1)S(1)} %shard_map.118.refs_3_), channel_id=1, source_target_pairs={{0,2},{1,3},{2,0},{3,1},{4,6},{5,7},{6,4},{7,5},{8,10},{9,11},{10,... | collective-permute-start | bytes 1572872 | tf_op jit(solution)/shard_map/ppermute | solution.py:25
  26.2 7.0 %copy-start.3 = (bf16[2,128,128]{2,1,0:T(8,128)(2,1)S(1)}, bf16[2,128,128]{2,1,0:T(8,128)(2,1)}, u32[]{:S(2)}) copy-start(bf16[2,128,128]{2,1,0:T(8,128)(2,1)} %refs_2_.3) | copy-start | bytes 196612
  26.2 7.0 %copy-start.5 = (bf16[2,128,128]{2,1,0:T(8,128)(2,1)S(1)}, bf16[2,128,128]{2,1,0:T(8,128)(2,1)}, u32[]{:S(2)}) copy-start(bf16[2,128,128]{2,1,0:T(8,128)(2,1)} %refs_3_.7) | copy-start | bytes 196612
  26.2 7.0 %copy-start.6 = (bf16[2,128,128]{2,1,0:T(8,128)(2,1)S(1)}, bf16[2,128,128]{2,1,0:T(8,128)(2,1)}, u32[]{:S(2)}) copy-start(bf16[2,128,128]{2,1,0:T(8,128)(2,1)} %refs_4_.3) | copy-start | bytes 196612
  26.2 6.9 %collective-permute-start.7 = (bf16[2,256,128]{2,1,0:T(8,128)(2,1)S(1)}, bf16[2,256,128]{2,1,0:T(8,128)(2,1)S(1)}, u32[]{:S(2)}, u32[]{:S(2)}) collective-permute-start(bf16[2,256,128]{2,1,0:T(8,128)(2,1)S(1)} %shard_map.117), channel_id=1, source_target_pairs={{0,24},{1,25},{2,26},{3,27},{4,28},{5,29},{6,30},{7,31},{8,16},{9,... | collective-permute-start | bytes 393224 | tf_op jit(solution)/shard_map/ppermute | solution.py:25
  29.1 8.2 %copy-start.1 = (bf16[1024,128]{1,0:T(8,128)(2,1)S(1)}, bf16[1024,128]{1,0:T(8,128)(2,1)}, u32[]{:S(2)}) copy-start(bf16[1024,128]{1,0:T(8,128)(2,1)} %param.17) | copy-start | bytes 786436
  33.6 3.6 %collective-permute-start.10 = (bf16[4,512,128]{2,1,0:T(8,128)(2,1)S(1)}, bf16[4,512,128]{2,1,0:T(8,128)(2,1)S(1)}, u32[]{:S(2)}, u32[]{:S(2)}) collective-permute-start(bf16[4,512,128]{2,1,0:T(8,128)(2,1)S(1)} %shard_map.121.refs_5_), channel_id=1, source_target_pairs={{0,1},{1,0},{2,3},{3,2},{4,5},{5,4},{6,7},{7,6},{8,9},{9,8},{10,11... | collective-permute-start | bytes 1572872 | tf_op jit(solution)/shard_map/ppermute | solution.py:25
  33.7 5.5 %collective-permute-start.11 = (bf16[1,144,128]{2,1,0:T(8,128)(2,1)S(1)}, bf16[1,144,128]{2,1,0:T(8,128)(2,1)S(1)}, u32[]{:S(2)}, u32[]{:S(2)}) collective-permute-start(bf16[1,144,128]{2,1,0:T(8,128)(2,1)S(1)} %shard_map.119.refs_6_.after_ref.refs_7_.refs_3_), channel_id=1, source_target_pairs={{0,6},{1,7},{2,4},{3,5},{4,2},{5,3},{6,0},{7,1},{8,14},{9,15},{10,... | collective-permute-start | bytes 110600 | tf_op jit(solution)/shard_map/ppermute | solution.py:25
  36.2 4.0 %collective-permute-start.12 = (bf16[1,144,128]{2,1,0:T(8,128)(2,1)S(1)}, bf16[1,144,128]{2,1,0:T(8,128)(2,1)S(1)}, u32[]{:S(2)}, u32[]{:S(2)}) collective-permute-start(bf16[1,144,128]{2,1,0:T(8,128)(2,1)S(1)} %shard_map.119.refs_6_.after_ref.refs_7_.refs_3_), channel_id=1, source_target_pairs={{0,2},{1,3},{2,0},{3,1},{4,6},{5,7},{6,4},{7,5},{8,10},{9,11},{10,... | collective-permute-start | bytes 110600 | tf_op jit(solution)/shard_map/ppermute | solution.py:25
  36.7 4.0 %collective-permute-start.13 = (bf16[1,144,128]{2,1,0:T(8,128)(2,1)S(1)}, bf16[1,144,128]{2,1,0:T(8,128)(2,1)S(1)}, u32[]{:S(2)}, u32[]{:S(2)}) collective-permute-start(bf16[1,144,128]{2,1,0:T(8,128)(2,1)S(1)} %shard_map.119.refs_6_.after_ref.refs_7_.refs_3_), channel_id=1, source_target_pairs={{0,4},{1,5},{2,6},{3,7},{4,0},{5,1},{6,2},{7,3},{8,12},{9,13},{10,... | collective-permute-start | bytes 110600 | tf_op jit(solution)/shard_map/ppermute | solution.py:25
  40.7 1.4 %collective-permute-start.14 = (bf16[4,144,128]{2,1,0:T(8,128)(2,1)S(1)}, bf16[4,144,128]{2,1,0:T(8,128)(2,1)S(1)}, u32[]{:S(2)}, u32[]{:S(2)}) collective-permute-start(bf16[4,144,128]{2,1,0:T(8,128)(2,1)S(1)} %shard_map.123.w_ref), channel_id=1, source_target_pairs={{0,1},{1,0},{2,3},{3,2},{4,5},{5,4},{6,7},{7,6},{8,9},{9,8},{10,11... | collective-permute-start | bytes 442376 | tf_op jit(solution)/shard_map/ppermute | solution.py:25
  43.2 6.1 %collective-permute-start.15 = (bf16[128,128]{1,0:T(8,128)(2,1)S(1)}, bf16[128,128]{1,0:T(8,128)(2,1)S(1)}, u32[]{:S(2)}, u32[]{:S(2)}) collective-permute-start(bf16[128,128]{1,0:T(8,128)(2,1)S(1)} %get-tuple-element.17), channel_id=1, source_target_pairs={{0,24},{1,25},{2,26},{3,27},{4,28},{5,29},{6,30},{7,31},{8,16},{9,... | collective-permute-start | bytes 98312 | tf_op jit(solution)/shard_map/ppermute | solution.py:25
  44.8 4.8 %collective-permute-start.16 = (bf16[128,128]{1,0:T(8,128)(2,1)S(1)}, bf16[128,128]{1,0:T(8,128)(2,1)S(1)}, u32[]{:S(2)}, u32[]{:S(2)}) collective-permute-start(bf16[128,128]{1,0:T(8,128)(2,1)S(1)} %get-tuple-element.18), channel_id=1, source_target_pairs={{0,16},{1,17},{2,18},{3,19},{4,20},{5,21},{6,22},{7,23},{8,24},{9,... | collective-permute-start | bytes 98312 | tf_op jit(solution)/shard_map/ppermute | solution.py:25
  46.0 4.1 %collective-permute-start.17 = (bf16[128,128]{1,0:T(8,128)(2,1)S(1)}, bf16[128,128]{1,0:T(8,128)(2,1)S(1)}, u32[]{:S(2)}, u32[]{:S(2)}) collective-permute-start(bf16[128,128]{1,0:T(8,128)(2,1)S(1)} %get-tuple-element.19), channel_id=1, source_target_pairs={{0,8},{1,9},{2,10},{3,11},{4,12},{5,13},{6,14},{7,15},{8,0},{9,1},... | collective-permute-start | bytes 98312 | tf_op jit(solution)/shard_map/ppermute | solution.py:25
  (5 other events, 10.2 us)

commit v7 on v6

--- a/solution.py
+++ b/solution.py
@@ -104,7 +104,7 @@
         left = jnp.concatenate(
             [jnp.concatenate([h[g][:, i * npno : (i + 1) * npno] for h in half], axis=1) for i in range(2)], axis=0
         )
-        term = lax.dot_general(left, right, (((1,), (1,)), ((), ())), preferred_element_type=F32)
+        term = lax.dot_general(right, left, (((1,), (1,)), ((), ())), preferred_element_type=F32)
         sums[g] = term if sums[g] is None else sums[g] + term
 
 
@@ -125,7 +125,7 @@
             spread_ref[dom_ref[pair * dom_blk + a], p * npno : (p + 1) * npno, :] = pack_ref[
                 p, a * blk : (a + 1) * blk, :
             ]
-    sums = [prior_ref[g] if prior else None for g in range(pairs)]
+    sums = [None] * pairs
     for k, mask in enumerate(masks):
         dev = where_ref[0] ^ mask
         overlaps = []
@@ -135,7 +135,9 @@
             overlaps.append(jnp.dot(left, q_refs[k][p], preferred_element_type=F32).astype(BF16))
         add_terms(sums, overlaps, tz_refs[k], c_ref, dev)
     for g in range(pairs):
-        out_ref[g] = sums[g].astype(out_ref.dtype)
+        for rows in (slice(0, npno), slice(npno, 2 * npno)):
+            total = sums[g][:, rows].T
+            out_ref[g, rows, :] = (total + prior_ref[g, rows, :] if prior else total).astype(out_ref.dtype)
 
 
 def updated(p, own_ref, back_ref, amps_ref, resp_ref, ints_ref, energy_ref):
@@ -264,7 +266,7 @@
     for mask in range(2, near, 2):
         near_q[mask] = swap(trans, mask, 0)
     near_tz[0] = call(
-        join_kernel, sds((pairs, npno, 2 * npno), BF16), [ANY, ANY], 1, amps, resp, scratch=[pltpu.SemaphoreType.DMA((2,))]
+        join_kernel, sds((pairs, npno, 2 * npno), BF16), [ANY, ANY], 1, amps, resp, scratch=[pltpu.SemaphoreType.DMA((2,))], limit=60,
     )
     near_tz[1] = swap(near_tz[0], 1, 0)
     for mask in range(2, near, 2):

time: 50.9 us -> 51 us (level)
  Pallas kernels: 11.8 us -> 13.6 us
  local copies, waits for them, and re-layouts: 1.93 us -> 0.25 us
    pallas_call x16, Pallas kernels: 11.8 us -> 13.6 us  [call(): pl.pallas_call(kernel, out_shape=out_shape, in_specs=specs, out_specs=out...]
    unnamed x23 -> x21, local copies, waits for them, and re-layouts: 1.82 us -> 0.15 us
  transfers between devices with their start and end apart: 18 -> 18, of which waited for: 9 -> 9; matrix products, arithmetic and copies ran while one was open for 1% -> 1% of each run, Pallas kernels for 20% -> 23%
where the time goes in v7:
time: 51 us; the launch traced here: 50.8 us
  starting transfers between devices  23 us (45%)
  Pallas kernels  13.6 us (27%)
  waiting for transfers between devices  13 us (25%)
  between operations  0.88 us (2%)
    ppermute x18, starting transfers between devices, swap(): return lax.ppermute(value, ('wide', 'narrow'), pairs)  23 us
    pallas_call x16, Pallas kernels, call(): pl.pallas_call(kernel, out_shape=out_shape, in_specs=specs, out_specs=out...  13.6 us
    ppermute x18, waiting for transfers between devices, swap(): return lax.ppermute(value, ('wide', 'narrow'), pairs)  13 us
  transfers between devices with their start and end apart: 18, of which 9 were waited for; matrix products, arithmetic and copies ran while one was open for 1% of the time, Pallas kernels for 23%

profile of v7, /device:TPU:0, one launch (start us, length us, event | category | flops | bytes accessed | tf_op | source)
XLA Modules:
  0.0 50.8 jit_solution(2270785275032750481)
XLA Ops:
  0.7 3.1 %collective-permute-start = (bf16[2,512,128]{2,1,0:T(8,128)(2,1)}, bf16[2,512,128]{2,1,0:T(8,128)(2,1)S(1)}, u32[]{:S(2)}, u32[]{:S(2)}) collective-permute-start(bf16[2,512,128]{2,1,0:T(8,128)(2,1)} %refs_0_.1), channel_id=1, source_target_pairs={{0,8},{1,9},{2,10},{3,11},{4,12},{5,13},{6,14},{7,15},{8,0},{9,1},... | collective-permute-start | bytes 786440 | tf_op jit(solution)/shard_map/ppermute | solution.py:25
  3.8 1.5 %collective-permute-start.4 = (bf16[2,512,128]{2,1,0:T(8,128)(2,1)}, bf16[2,512,128]{2,1,0:T(8,128)(2,1)S(1)}, u32[]{:S(2)}, u32[]{:S(2)}) collective-permute-start(bf16[2,512,128]{2,1,0:T(8,128)(2,1)} %refs_0_.1), channel_id=1, source_target_pairs={{0,4},{1,5},{2,6},{3,7},{4,0},{5,1},{6,2},{7,3},{8,12},{9,13},{10,... | collective-permute-start | bytes 786440 | tf_op jit(solution)/shard_map/ppermute | solution.py:25
  5.2 1.5 %shard_map.114.refs_6_.refs_7_ = bf16[2,128,256]{2,1,0:T(8,128)(2,1)} custom-call(bf16[2,128,128]{2,1,0:T(8,128)(2,1)} %refs_2_.3, bf16[2,128,128]{2,1,0:T(8,128)(2,1)} %refs_3_.7), custom_call_target="tpu_custom_call" | custom-call | flops 1000000000 | tf_op jit(solution)/shard_map/pallas_call | solution.py:29
  7.5 0.7 %shard_map.112.value_ref = bf16[2,544,128]{2,1,0:T(8,128)(2,1)S(1)} custom-call(s32[2,12]{1,0:T(2,128)S(1)} %copy-done.6, f32[2,12]{1,0:T(2,128)S(1)} %copy-done.7, bf16[2,512,128]{2,1,0:T(8,128)(2,1)S(1)} %copy-done), custom_call_target="tpu_custom_call" | custom-call | flops 1000000000 | tf_op jit(solution)/shard_map/pallas_call | solution.py:29
  8.2 2.9 %collective-permute-done.after_ref.refs_5_ = bf16[2,512,128]{2,1,0:T(8,128)(2,1)S(1)} collective-permute-done((bf16[2,512,128]{2,1,0:T(8,128)(2,1)}, bf16[2,512,128]{2,1,0:T(8,128)(2,1)S(1)}, u32[]{:S(2)}, u32[]{:S(2)}) %collective-permute-start) | collective-permute-done | bytes 262176 | tf_op jit(solution)/shard_map/ppermute | solution.py:25
  11.1 4.1 %collective-permute-start.6 = (bf16[2,544,128]{2,1,0:T(8,128)(2,1)S(1)}, bf16[2,544,128]{2,1,0:T(8,128)(2,1)S(1)}, u32[]{:S(2)}, u32[]{:S(2)}) collective-permute-start(bf16[2,544,128]{2,1,0:T(8,128)(2,1)S(1)} %shard_map.113.refs_2_), channel_id=1, source_target_pairs={{0,24},{1,25},{2,26},{3,27},{4,28},{5,29},{6,30},{7,31},{8,16},{9,... | collective-permute-start | bytes 835592 | tf_op jit(solution)/shard_map/ppermute | solution.py:25
  15.3 1.5 %collective-permute-start.1 = (bf16[2,512,128]{2,1,0:T(8,128)(2,1)S(1)}, bf16[2,512,128]{2,1,0:T(8,128)(2,1)S(1)}, u32[]{:S(2)}, u32[]{:S(2)}) collective-permute-start(bf16[2,512,128]{2,1,0:T(8,128)(2,1)S(1)} %collective-permute-done.after_ref.refs_5_), channel_id=1, source_target_pairs={{0,4},{1,5},{2,6},{3,7},{4,0},{5,1},{6,2},{7,3},{8,12},{9,13},{10,... | collective-permute-start | bytes 786440 | tf_op jit(solution)/shard_map/ppermute | solution.py:25
  17.8 1.6 %collective-permute-start.9 = (bf16[4,512,128]{2,1,0:T(8,128)(2,1)S(1)}, bf16[4,512,128]{2,1,0:T(8,128)(2,1)S(1)}, u32[]{:S(2)}, u32[]{:S(2)}) collective-permute-start(bf16[4,512,128]{2,1,0:T(8,128)(2,1)S(1)} %shard_map.118.refs_3_), channel_id=1, source_target_pairs={{0,2},{1,3},{2,0},{3,1},{4,6},{5,7},{6,4},{7,5},{8,10},{9,11},{10,... | collective-permute-start | bytes 1572872 | tf_op jit(solution)/shard_map/ppermute | solution.py:25
  19.4 2.0 %shard_map.115.refs_5_ = f32[2,256,128]{2,1,0:T(8,128)S(1)} custom-call(s32[2]{0:T(128)S(1)} %pad_add_fusion.refs_0_, s32[256]{0:T(256)S(1)} %reshape.12.refs_1_, bf16[2,544,128]{2,1,0:T(8,128)(2,1)S(1)} %shard_map.113.refs_2_, bf16[2,512,128]{2,1,0:T(8,128)(2,1)S(1)} %copy-done, bf16[2,512,128]{2,1,0:T(8,128)(2,1)S(1)} %collective-permute-done.4.refs_4_.refs_1_, ...), custom_call_target="tpu_custom_call" | custom-call | flops 2000000000 | tf_op jit(solution)/shard_map/pallas_call | solution.py:29
  21.4 2.4 %collective-permute-done.3.refs_4_.refs_10_ = bf16[2,128,256]{2,1,0:T(8,128)(2,1)S(1)} collective-permute-done((bf16[2,128,256]{2,1,0:T(8,128)(2,1)S(1)}, bf16[2,128,256]{2,1,0:T(8,128)(2,1)S(1)}, u32[]{:S(2)}, u32[]{:S(2)}) %collective-permute-start.3) | collective-permute-done | bytes 131104 | tf_op jit(solution)/shard_map/ppermute | solution.py:25
  23.8 2.5 %shard_map.117 = bf16[2,256,128]{2,1,0:T(8,128)(2,1)S(1)} custom-call(s32[2]{0:T(128)S(1)} %pad_add_fusion.refs_0_, s32[256]{0:T(256)S(1)} %reshape.12.refs_1_, bf16[2,544,128]{2,1,0:T(8,128)(2,1)S(1)} %collective-permute-done.6.refs_2_, bf16[2,512,128]{2,1,0:T(8,128)(2,1)S(1)} %copy-done, bf16[2,512,128]{2,1,0:T(8,128)(2,1)S(1)} %collective-permute-done.4.refs_4_.refs_1_, ...), custom_call_target="tpu_custom_call" | custom-call | flops 4000000000 | tf_op jit(solution)/shard_map/pallas_call | solution.py:29
  26.4 1.7 %collective-permute-start.7 = (bf16[2,256,128]{2,1,0:T(8,128)(2,1)S(1)}, bf16[2,256,128]{2,1,0:T(8,128)(2,1)S(1)}, u32[]{:S(2)}, u32[]{:S(2)}) collective-permute-start(bf16[2,256,128]{2,1,0:T(8,128)(2,1)S(1)} %shard_map.117), channel_id=1, source_target_pairs={{0,24},{1,25},{2,26},{3,27},{4,28},{5,29},{6,30},{7,31},{8,16},{9,... | collective-permute-start | bytes 393224 | tf_op jit(solution)/shard_map/ppermute | solution.py:25
  28.1 1.3 %shard_map.116.refs_0_ = f32[2,256,128]{2,1,0:T(8,128)S(1)} custom-call(s32[2]{0:T(128)S(1)} %pad_add_fusion.refs_0_, s32[256]{0:T(256)S(1)} %reshape.12.refs_1_, bf16[2,544,128]{2,1,0:T(8,128)(2,1)S(1)} %shard_map.113.refs_2_, bf16[2,512,128]{2,1,0:T(8,128)(2,1)S(1)} %collective-permute-done.1.refs_3_.refs_6_, ...), custom_call_target="tpu_custom_call" | custom-call | flops 2000000000 | tf_op jit(solution)/shard_map/pallas_call | solution.py:29
  29.4 4.0 %collective-permute-done.7.refs_1_ = bf16[2,256,128]{2,1,0:T(8,128)(2,1)S(1)} collective-permute-done((bf16[2,256,128]{2,1,0:T(8,128)(2,1)S(1)}, bf16[2,256,128]{2,1,0:T(8,128)(2,1)S(1)}, u32[]{:S(2)}, u32[]{:S(2)}) %collective-permute-start.7) | collective-permute-done | bytes 131104 | tf_op jit(solution)/shard_map/ppermute | solution.py:25
  33.9 2.5 %collective-permute-start.11 = (bf16[1,144,128]{2,1,0:T(8,128)(2,1)S(1)}, bf16[1,144,128]{2,1,0:T(8,128)(2,1)S(1)}, u32[]{:S(2)}, u32[]{:S(2)}) collective-permute-start(bf16[1,144,128]{2,1,0:T(8,128)(2,1)S(1)} %shard_map.119.refs_6_.after_ref.refs_7_.refs_3_), channel_id=1, source_target_pairs={{0,6},{1,7},{2,4},{3,5},{4,2},{5,3},{6,0},{7,1},{8,14},{9,15},{10,... | collective-permute-start | bytes 110600 | tf_op jit(solution)/shard_map/ppermute | solution.py:25
  37.4 1.9 %shard_map.122 = (bf16[5,128,2048]{2,1,0:T(8,128)(2,1)S(1)}, bf16[16,128,128]{2,1,0:T(8,128)(2,1)S(1)}) custom-call(s32[2]{0:T(128)S(1)} %pad_add_fusion.refs_0_, s32[256]{0:T(256)S(1)} %reshape.12.refs_1_, bf16[8,128,128]{2,1,0:T(8,128)(2,1)S(1)} %bitcast.3, bf16[4,512,128]{2,1,0:T(8,128)(2,1)S(1)} %shard_map.118.refs_3_, ...), custom_call_target="tpu_custom_call" | custom-call | flops 1000000000 | tf_op jit(solution)/shard_map/pallas_call | solution.py:29
  39.4 1.0 %collective-permute-done.12.refs_1_ = bf16[1,144,128]{2,1,0:T(8,128)(2,1)S(1)} collective-permute-done((bf16[1,144,128]{2,1,0:T(8,128)(2,1)S(1)}, bf16[1,144,128]{2,1,0:T(8,128)(2,1)S(1)}, u32[]{:S(2)}, u32[]{:S(2)}) %collective-permute-start.12) | collective-permute-done | bytes 36896 | tf_op jit(solution)/shard_map/ppermute | solution.py:25
  40.9 0.7 %shard_map.124.refs_2_ = f32[4,128,128]{2,1,0:T(8,128)S(1)} custom-call(bf16[5,128,2048]{2,1,0:T(8,128)(2,1)S(1)} %get-tuple-element.14.full_ref.refs_0_, bf16[16,128,128]{2,1,0:T(8,128)(2,1)S(1)} %get-tuple-element.15.refs_4_.moved_ref.refs_1_, bf16[4,144,128]{2,1,0:T(8,128)(2,1)S(1)} %shard_map.123.w_ref), custom_call_target="tpu_custom_call" | custom-call | flops 500000000 | tf_op jit(solution)/shard_map/pallas_call | solution.py:29
  42.3 1.0 %shard_map.125 = (f32[128,128]{1,0:T(8,128)S(1)}, bf16[128,128]{1,0:T(8,128)(2,1)S(1)}, bf16[128,128]{1,0:T(8,128)(2,1)S(1)}, bf16[128,128]{1,0:T(8,128)(2,1)S(1)}) custom-call(bf16[5,128,2048]{2,1,0:T(8,128)(2,1)S(1)} %get-tuple-element.14.full_ref.refs_0_, bf16[16,128,128]{2,1,0:T(8,128)(2,1)S(1)} %get-tuple-element.15.refs_4_.moved_ref.refs_1_, ...), custom_call_target="tpu_custom_call" | custom-call | flops 1000000000 | tf_op jit(solution)/shard_map/pallas_call | solution.py:29
  43.3 1.7 %collective-permute-start.15 = (bf16[128,128]{1,0:T(8,128)(2,1)S(1)}, bf16[128,128]{1,0:T(8,128)(2,1)S(1)}, u32[]{:S(2)}, u32[]{:S(2)}) collective-permute-start(bf16[128,128]{1,0:T(8,128)(2,1)S(1)} %get-tuple-element.17), channel_id=1, source_target_pairs={{0,24},{1,25},{2,26},{3,27},{4,28},{5,29},{6,30},{7,31},{8,16},{9,... | collective-permute-start | bytes 98312 | tf_op jit(solution)/shard_map/ppermute | solution.py:25
  45.0 1.1 %collective-permute-start.16 = (bf16[128,128]{1,0:T(8,128)(2,1)S(1)}, bf16[128,128]{1,0:T(8,128)(2,1)S(1)}, u32[]{:S(2)}, u32[]{:S(2)}) collective-permute-start(bf16[128,128]{1,0:T(8,128)(2,1)S(1)} %get-tuple-element.18), channel_id=1, source_target_pairs={{0,16},{1,17},{2,18},{3,19},{4,20},{5,21},{6,22},{7,23},{8,24},{9,... | collective-permute-start | bytes 98312 | tf_op jit(solution)/shard_map/ppermute | solution.py:25
  46.1 1.7 %collective-permute-start.17 = (bf16[128,128]{1,0:T(8,128)(2,1)S(1)}, bf16[128,128]{1,0:T(8,128)(2,1)S(1)}, u32[]{:S(2)}, u32[]{:S(2)}) collective-permute-start(bf16[128,128]{1,0:T(8,128)(2,1)S(1)} %get-tuple-element.19), channel_id=1, source_target_pairs={{0,8},{1,9},{2,10},{3,11},{4,12},{5,13},{6,14},{7,15},{8,0},{9,1},... | collective-permute-start | bytes 98312 | tf_op jit(solution)/shard_map/ppermute | solution.py:25
  47.8 0.9 %shard_map.120 = (f32[2,128,128]{2,1,0:T(8,128)}, f32[2,128,128]{2,1,0:T(8,128)}, f32[8,128]{1,0:T(8,128)S(1)}) custom-call(f32[2,256,128]{2,1,0:T(8,128)S(1)} %shard_map.116.refs_0_, bf16[2,256,128]{2,1,0:T(8,128)(2,1)S(1)} %collective-permute-done.7.refs_1_, bf16[2,128,128]{2,1,0:T(8,128)(2,1)S(1)} %copy-done.3, bf16[2,128,128]{2,1,0:T(8,128)(2,1)S(1)} %copy-done.4, ...), custom_call_target="tpu_custom_call" | custom-call | flops 1000000000 | tf_op jit(solution)/shard_map/pallas_call | solution.py:29
  48.6 0.8 %collective-permute-done.15.refs_0_.refs_1_ = bf16[128,128]{1,0:T(8,128)(2,1)S(1)} collective-permute-done((bf16[128,128]{1,0:T(8,128)(2,1)S(1)}, bf16[128,128]{1,0:T(8,128)(2,1)S(1)}, u32[]{:S(2)}, u32[]{:S(2)}) %collective-permute-start.15) | collective-permute-done | bytes 32800 | tf_op jit(solution)/shard_map/ppermute | solution.py:25
  (51 shorter events, 5.9 us)
Async XLA Ops:
  0.7 10.4 %collective-permute-start = (bf16[2,512,128]{2,1,0:T(8,128)(2,1)}, bf16[2,512,128]{2,1,0:T(8,128)(2,1)S(1)}, u32[]{:S(2)}, u32[]{:S(2)}) collective-permute-start(bf16[2,512,128]{2,1,0:T(8,128)(2,1)} %refs_0_.1), channel_id=1, source_target_pairs={{0,8},{1,9},{2,10},{3,11},{4,12},{5,13},{6,14},{7,15},{8,0},{9,1},... | collective-permute-start | bytes 786440 | tf_op jit(solution)/shard_map/ppermute | solution.py:25
  3.8 13.9 %collective-permute-start.4 = (bf16[2,512,128]{2,1,0:T(8,128)(2,1)}, bf16[2,512,128]{2,1,0:T(8,128)(2,1)S(1)}, u32[]{:S(2)}, u32[]{:S(2)}) collective-permute-start(bf16[2,512,128]{2,1,0:T(8,128)(2,1)} %refs_0_.1), channel_id=1, source_target_pairs={{0,4},{1,5},{2,6},{3,7},{4,0},{5,1},{6,2},{7,3},{8,12},{9,13},{10,... | collective-permute-start | bytes 786440 | tf_op jit(solution)/shard_map/ppermute | solution.py:25
  6.8 10.0 %copy-start.9 = (s32[64,4]{0,1:T(4,128)S(1)}, s32[64,4]{0,1:T(4,128)}, u32[]{:S(2)}) copy-start(s32[64,4]{0,1:T(4,128)} %param.16) | copy-start | bytes 3076
  6.8 10.2 %collective-permute-start.2 = (bf16[2,128,256]{2,1,0:T(8,128)(2,1)}, bf16[2,128,256]{2,1,0:T(8,128)(2,1)S(1)}, u32[]{:S(2)}, u32[]{:S(2)}) collective-permute-start(bf16[2,128,256]{2,1,0:T(8,128)(2,1)} %shard_map.114.refs_6_.refs_7_), channel_id=1, source_target_pairs={{0,8},{1,9},{2,10},{3,11},{4,12},{5,13},{6,14},{7,15},{8,0},{9,1},... | collective-permute-start | bytes 393224 | tf_op jit(solution)/shard_map/ppermute | solution.py:25
  7.3 10.3 %collective-permute-start.5 = (bf16[2,128,256]{2,1,0:T(8,128)(2,1)}, bf16[2,128,256]{2,1,0:T(8,128)(2,1)S(1)}, u32[]{:S(2)}, u32[]{:S(2)}) collective-permute-start(bf16[2,128,256]{2,1,0:T(8,128)(2,1)} %shard_map.114.refs_6_.refs_7_), channel_id=1, source_target_pairs={{0,4},{1,5},{2,6},{3,7},{4,0},{5,1},{6,2},{7,3},{8,12},{9,13},{10,... | collective-permute-start | bytes 393224 | tf_op jit(solution)/shard_map/ppermute | solution.py:25
  7.5 11.9 %copy-start.2 = (bf16[2,128,256]{2,1,0:T(8,128)(2,1)S(1)}, bf16[2,128,256]{2,1,0:T(8,128)(2,1)}, u32[]{:S(2)}) copy-start(bf16[2,128,256]{2,1,0:T(8,128)(2,1)} %shard_map.114.refs_6_.refs_7_) | copy-start | bytes 393220
  11.1 12.7 %collective-permute-start.6 = (bf16[2,544,128]{2,1,0:T(8,128)(2,1)S(1)}, bf16[2,544,128]{2,1,0:T(8,128)(2,1)S(1)}, u32[]{:S(2)}, u32[]{:S(2)}) collective-permute-start(bf16[2,544,128]{2,1,0:T(8,128)(2,1)S(1)} %shard_map.113.refs_2_), channel_id=1, source_target_pairs={{0,24},{1,25},{2,26},{3,27},{4,28},{5,29},{6,30},{7,31},{8,16},{9,... | collective-permute-start | bytes 835592 | tf_op jit(solution)/shard_map/ppermute | solution.py:25
  15.3 8.6 %collective-permute-start.1 = (bf16[2,512,128]{2,1,0:T(8,128)(2,1)S(1)}, bf16[2,512,128]{2,1,0:T(8,128)(2,1)S(1)}, u32[]{:S(2)}, u32[]{:S(2)}) collective-permute-start(bf16[2,512,128]{2,1,0:T(8,128)(2,1)S(1)} %collective-permute-done.after_ref.refs_5_), channel_id=1, source_target_pairs={{0,4},{1,5},{2,6},{3,7},{4,0},{5,1},{6,2},{7,3},{8,12},{9,13},{10,... | collective-permute-start | bytes 786440 | tf_op jit(solution)/shard_map/ppermute | solution.py:25
  17.0 6.8 %collective-permute-start.3 = (bf16[2,128,256]{2,1,0:T(8,128)(2,1)S(1)}, bf16[2,128,256]{2,1,0:T(8,128)(2,1)S(1)}, u32[]{:S(2)}, u32[]{:S(2)}) collective-permute-start(bf16[2,128,256]{2,1,0:T(8,128)(2,1)S(1)} %collective-permute-done.2.refs_8_.refs_9_), channel_id=1, source_target_pairs={{0,4},{1,5},{2,6},{3,7},{4,0},{5,1},{6,2},{7,3},{8,12},{9,13},{10,... | collective-permute-start | bytes 393224 | tf_op jit(solution)/shard_map/ppermute | solution.py:25
  17.7 15.6 %collective-permute-start.8 = (bf16[4,512,128]{2,1,0:T(8,128)(2,1)S(1)}, bf16[4,512,128]{2,1,0:T(8,128)(2,1)S(1)}, u32[]{:S(2)}, u32[]{:S(2)}) collective-permute-start(bf16[4,512,128]{2,1,0:T(8,128)(2,1)S(1)} %shard_map.118.refs_3_), channel_id=1, source_target_pairs={{0,1},{1,0},{2,3},{3,2},{4,5},{5,4},{6,7},{7,6},{8,9},{9,8},{10,11... | collective-permute-start | bytes 1572872 | tf_op jit(solution)/shard_map/ppermute | solution.py:25
  17.8 16.0 %collective-permute-start.9 = (bf16[4,512,128]{2,1,0:T(8,128)(2,1)S(1)}, bf16[4,512,128]{2,1,0:T(8,128)(2,1)S(1)}, u32[]{:S(2)}, u32[]{:S(2)}) collective-permute-start(bf16[4,512,128]{2,1,0:T(8,128)(2,1)S(1)} %shard_map.118.refs_3_), channel_id=1, source_target_pairs={{0,2},{1,3},{2,0},{3,1},{4,6},{5,7},{6,4},{7,5},{8,10},{9,11},{10,... | collective-permute-start | bytes 1572872 | tf_op jit(solution)/shard_map/ppermute | solution.py:25
  26.3 7.0 %copy-start.3 = (bf16[2,128,128]{2,1,0:T(8,128)(2,1)S(1)}, bf16[2,128,128]{2,1,0:T(8,128)(2,1)}, u32[]{:S(2)}) copy-start(bf16[2,128,128]{2,1,0:T(8,128)(2,1)} %refs_2_.3) | copy-start | bytes 196612
  26.4 7.0 %copy-start.4 = (bf16[2,128,128]{2,1,0:T(8,128)(2,1)S(1)}, bf16[2,128,128]{2,1,0:T(8,128)(2,1)}, u32[]{:S(2)}) copy-start(bf16[2,128,128]{2,1,0:T(8,128)(2,1)} %refs_3_.7) | copy-start | bytes 196612
  26.4 7.0 %copy-start.5 = (bf16[2,128,128]{2,1,0:T(8,128)(2,1)S(1)}, bf16[2,128,128]{2,1,0:T(8,128)(2,1)}, u32[]{:S(2)}) copy-start(bf16[2,128,128]{2,1,0:T(8,128)(2,1)} %refs_4_.3) | copy-start | bytes 196612
  26.4 6.9 %collective-permute-start.7 = (bf16[2,256,128]{2,1,0:T(8,128)(2,1)S(1)}, bf16[2,256,128]{2,1,0:T(8,128)(2,1)S(1)}, u32[]{:S(2)}, u32[]{:S(2)}) collective-permute-start(bf16[2,256,128]{2,1,0:T(8,128)(2,1)S(1)} %shard_map.117), channel_id=1, source_target_pairs={{0,24},{1,25},{2,26},{3,27},{4,28},{5,29},{6,30},{7,31},{8,16},{9,... | collective-permute-start | bytes 393224 | tf_op jit(solution)/shard_map/ppermute | solution.py:25
  29.3 8.1 %copy-start.1 = (bf16[1024,128]{1,0:T(8,128)(2,1)S(1)}, bf16[1024,128]{1,0:T(8,128)(2,1)}, u32[]{:S(2)}) copy-start(bf16[1024,128]{1,0:T(8,128)(2,1)} %param.17) | copy-start | bytes 786436
  33.8 3.6 %collective-permute-start.10 = (bf16[4,512,128]{2,1,0:T(8,128)(2,1)S(1)}, bf16[4,512,128]{2,1,0:T(8,128)(2,1)S(1)}, u32[]{:S(2)}, u32[]{:S(2)}) collective-permute-start(bf16[4,512,128]{2,1,0:T(8,128)(2,1)S(1)} %shard_map.121.refs_5_), channel_id=1, source_target_pairs={{0,1},{1,0},{2,3},{3,2},{4,5},{5,4},{6,7},{7,6},{8,9},{9,8},{10,11... | collective-permute-start | bytes 1572872 | tf_op jit(solution)/shard_map/ppermute | solution.py:25
  33.9 5.5 %collective-permute-start.11 = (bf16[1,144,128]{2,1,0:T(8,128)(2,1)S(1)}, bf16[1,144,128]{2,1,0:T(8,128)(2,1)S(1)}, u32[]{:S(2)}, u32[]{:S(2)}) collective-permute-start(bf16[1,144,128]{2,1,0:T(8,128)(2,1)S(1)} %shard_map.119.refs_6_.after_ref.refs_7_.refs_3_), channel_id=1, source_target_pairs={{0,6},{1,7},{2,4},{3,5},{4,2},{5,3},{6,0},{7,1},{8,14},{9,15},{10,... | collective-permute-start | bytes 110600 | tf_op jit(solution)/shard_map/ppermute | solution.py:25
  36.4 4.0 %collective-permute-start.12 = (bf16[1,144,128]{2,1,0:T(8,128)(2,1)S(1)}, bf16[1,144,128]{2,1,0:T(8,128)(2,1)S(1)}, u32[]{:S(2)}, u32[]{:S(2)}) collective-permute-start(bf16[1,144,128]{2,1,0:T(8,128)(2,1)S(1)} %shard_map.119.refs_6_.after_ref.refs_7_.refs_3_), channel_id=1, source_target_pairs={{0,2},{1,3},{2,0},{3,1},{4,6},{5,7},{6,4},{7,5},{8,10},{9,11},{10,... | collective-permute-start | bytes 110600 | tf_op jit(solution)/shard_map/ppermute | solution.py:25
  36.9 4.0 %collective-permute-start.13 = (bf16[1,144,128]{2,1,0:T(8,128)(2,1)S(1)}, bf16[1,144,128]{2,1,0:T(8,128)(2,1)S(1)}, u32[]{:S(2)}, u32[]{:S(2)}) collective-permute-start(bf16[1,144,128]{2,1,0:T(8,128)(2,1)S(1)} %shard_map.119.refs_6_.after_ref.refs_7_.refs_3_), channel_id=1, source_target_pairs={{0,4},{1,5},{2,6},{3,7},{4,0},{5,1},{6,2},{7,3},{8,12},{9,13},{10,... | collective-permute-start | bytes 110600 | tf_op jit(solution)/shard_map/ppermute | solution.py:25
  40.9 1.4 %collective-permute-start.14 = (bf16[4,144,128]{2,1,0:T(8,128)(2,1)S(1)}, bf16[4,144,128]{2,1,0:T(8,128)(2,1)S(1)}, u32[]{:S(2)}, u32[]{:S(2)}) collective-permute-start(bf16[4,144,128]{2,1,0:T(8,128)(2,1)S(1)} %shard_map.123.w_ref), channel_id=1, source_target_pairs={{0,1},{1,0},{2,3},{3,2},{4,5},{5,4},{6,7},{7,6},{8,9},{9,8},{10,11... | collective-permute-start | bytes 442376 | tf_op jit(solution)/shard_map/ppermute | solution.py:25
  43.3 6.1 %collective-permute-start.15 = (bf16[128,128]{1,0:T(8,128)(2,1)S(1)}, bf16[128,128]{1,0:T(8,128)(2,1)S(1)}, u32[]{:S(2)}, u32[]{:S(2)}) collective-permute-start(bf16[128,128]{1,0:T(8,128)(2,1)S(1)} %get-tuple-element.17), channel_id=1, source_target_pairs={{0,24},{1,25},{2,26},{3,27},{4,28},{5,29},{6,30},{7,31},{8,16},{9,... | collective-permute-start | bytes 98312 | tf_op jit(solution)/shard_map/ppermute | solution.py:25
  45.0 4.8 %collective-permute-start.16 = (bf16[128,128]{1,0:T(8,128)(2,1)S(1)}, bf16[128,128]{1,0:T(8,128)(2,1)S(1)}, u32[]{:S(2)}, u32[]{:S(2)}) collective-permute-start(bf16[128,128]{1,0:T(8,128)(2,1)S(1)} %get-tuple-element.18), channel_id=1, source_target_pairs={{0,16},{1,17},{2,18},{3,19},{4,20},{5,21},{6,22},{7,23},{8,24},{9,... | collective-permute-start | bytes 98312 | tf_op jit(solution)/shard_map/ppermute | solution.py:25
  46.1 4.1 %collective-permute-start.17 = (bf16[128,128]{1,0:T(8,128)(2,1)S(1)}, bf16[128,128]{1,0:T(8,128)(2,1)S(1)}, u32[]{:S(2)}, u32[]{:S(2)}) collective-permute-start(bf16[128,128]{1,0:T(8,128)(2,1)S(1)} %get-tuple-element.19), channel_id=1, source_target_pairs={{0,8},{1,9},{2,10},{3,11},{4,12},{5,13},{6,14},{7,15},{8,0},{9,1},... | collective-permute-start | bytes 98312 | tf_op jit(solution)/shard_map/ppermute | solution.py:25
  (4 other events, 27.5 us)
